TPU v7x, 32 devices: a whole 2x2x4 slice. The times are simulated.
32 devices in a mesh: section: 4 (over z), expert: 8 (over y, x, core).
Axes of the slice: x: 2, y: 2, z: 4, core: 2. Of those that a mesh axis runs over, the one named last changes fastest.
Arguments:
- grad_out: bfloat16 [1024, 4096], P('expert', 'section'), may hold values from -6 to 6
- probs: float32 [1024, 8], P('expert'), may hold values from 0.05 to 0.4
- expert_ids: int32 [1024, 8], P('expert'), may hold values from 0 to 15, all different within a row; in each aligned block of 128 rows (0 to 127, 128 to 255, ...) at most 96 rows name the same one
- w_gate: bfloat16 [16, 1536, 4096], P('expert', 'section'), may hold values from -0.09375 to 0.09375
- w_up: bfloat16 [16, 1536, 4096], P('expert', 'section'), may hold values from -0.09375 to 0.09375
- w_down: bfloat16 [16, 1536, 4096], P('expert', 'section'), may hold values from -0.15625 to 0.15625
- saved_gate: bfloat16 [16, 1536, 768], P('expert', 'section'), may hold values from -3 to 3
- saved_up: bfloat16 [16, 1536, 768], P('expert', 'section'), may hold values from -3 to 3
Outputs:
- grad_in: bfloat16 [1024, 4096], P('expert', 'section')
- grad_probs: bfloat16 [1024, 8], P('expert')
Inputs may be any that keep to these rules, and one draw needn't show every extreme that they name: `expert_ids`: each token names 8 different experts. Within the tokens of one index of expert (aligned blocks of 128 tokens) no expert is named more than 96 times, a bound that some block reaches.
All inputs are finite; a program needn't handle non-finite values.
Results may differ from a plain program's by a relative error of at most 0.015.
Values may be sent and summed in bfloat16 or wider, within the bound.
No kernel may reach another device: no remote copies, remote signals or barrier semaphores. Data moves between devices by JAX's collectives and lax.ppermute only.
A program may use at most 128 MiB of HBM per device.

v0:
```python
import jax
import jax.numpy as jnp
from jax import lax
from jax.sharding import PartitionSpec as P

TOPK = 8


def local(grad_out, probs, expert_ids, w_gate, w_up, w_down, saved_gate, saved_up):
    groups = lax.axis_size("expert")
    local_experts = w_gate.shape[0]
    expert_count = local_experts * groups
    slot_count = saved_gate.shape[2]
    capacity = slot_count // groups
    token_count = grad_out.shape[0]
    feature_share = grad_out.shape[1]
    picked = expert_ids.reshape(-1)
    onehot = (picked[:, None] == jnp.arange(expert_count, dtype=jnp.int32)[None, :]).astype(
        jnp.int32
    )
    before = jnp.cumsum(onehot, axis=0) - onehot
    position = jnp.sum(before * onehot, axis=1)
    slot = picked * capacity + position
    owner = jnp.arange(picked.shape[0], dtype=jnp.int32) // TOPK
    table = jnp.full((expert_count * capacity,), token_count, jnp.int32).at[slot].set(owner)
    full_rows = lax.all_gather(grad_out, "section", axis=1, tiled=True)
    padded = jnp.concatenate([full_rows, jnp.zeros((1, full_rows.shape[1]), jnp.bfloat16)], axis=0)
    outgoing = padded[table].reshape(expert_count, capacity, full_rows.shape[1])
    arrived = lax.all_to_all(outgoing, "expert", split_axis=0, concat_axis=1, tiled=True)
    hidden_grad = jnp.einsum("esd,efd->efs", arrived, w_down, preferred_element_type=jnp.float32)
    gate_act = saved_gate.astype(jnp.float32)
    up_act = saved_up.astype(jnp.float32)
    sigmoid_gate = jax.nn.sigmoid(gate_act)
    silu_gate = gate_act * sigmoid_gate
    router_part = jnp.sum(silu_gate * up_act * hidden_grad, axis=1)
    router_grad = lax.psum(router_part, "section").astype(jnp.bfloat16)
    gate_grad = (
        hidden_grad * up_act * sigmoid_gate * (1.0 + gate_act * (1.0 - sigmoid_gate))
    ).astype(jnp.bfloat16)
    up_grad = (hidden_grad * silu_gate).astype(jnp.bfloat16)
    term = jnp.einsum("efc,efs->esc", w_gate, gate_grad, preferred_element_type=jnp.float32)
    term = term + jnp.einsum("efc,efs->esc", w_up, up_grad, preferred_element_type=jnp.float32)
    shares = lax.psum_scatter(term.astype(jnp.bfloat16), "section", scatter_dimension=2, tiled=True)
    back_grad, back_router = (
        lax.all_to_all(shares, "expert", split_axis=1, concat_axis=0, tiled=True),
        lax.all_to_all(router_grad, "expert", split_axis=1, concat_axis=0, tiled=True),
    )
    rows = back_grad.reshape(expert_count * capacity, feature_share)[slot]
    weighted = (
        rows.astype(jnp.float32).reshape(token_count, TOPK, feature_share) * probs[:, :, None]
    )
    grad_in = jnp.sum(weighted, axis=1).astype(jnp.bfloat16)
    grad_probs = back_router.reshape(-1)[slot].reshape(token_count, TOPK)
    return (grad_in, grad_probs)


def solution(mesh):
    placed = (
        P("expert", "section"),
        P("expert", None),
        P("expert", None),
        P("expert", "section", None),
        P("expert", "section", None),
        P("expert", "section", None),
        P("expert", "section", None),
        P("expert", "section", None),
    )
    return jax.shard_map(
        local,
        mesh=mesh,
        in_specs=placed,
        out_specs=(P("expert", "section"), P("expert", None)),
        check_vma=False,
    )
```

profile of v0, /device:TPU:0, one launch (start us, length us, event | category | flops | bytes accessed | tf_op | source)
XLA Modules:
  0.0 513.8 jit_solution(11798525857975127705)
XLA Ops:
  7.2 0.7 all-gather.2.cloned.1.call-update
  7.9 0.8 copy.40
  8.9 4.5 reduce-window.6
  13.8 0.7 broadcast_multiply_fusion
  14.8 4.3 scatter_custom_fusion
  19.2 21.1 %all-gather.2.cloned.1.call-done = bf16[128,4096]{1,0:T(8,128)(2,1)} async-done(((bf16[128,1024]{1,0:T(8,128)(2,1)}), bf16[128,4096]{1,0:T(8,128)(2,1)}) %all-gather.2.cloned.1.call-update) | async-done | bytes 1048592 | tf_op jit(solution)/shard_map/all_gather | solution.py:26
  40.2 1.3 concatenate.3
  41.6 9.5 %gather_fusion = bf16[1536,4096]{1,0:T(8,128)(2,1)} fusion(bf16[129,4096]{1,0:T(8,128)(2,1)S(1)} %concatenate.3, s32[2048]{0:T(1024)S(1)} %pad_clamp_fusion), kind=kCustom, calls=%fused_computation | custom fusion | bytes 25171968 | tf_op jit(solution)/shard_map/gather | solution.py:28
  51.1 142.9 %all_to_all.49 = bf16[16,96,4096]{2,1,0:T(8,128)(2,1)S(1)} all-to-all(bf16[16,96,4096]{2,1,0:T(8,128)(2,1)} %bitcast.46), channel_id=1, replica_groups=mesh['section'=4,'expert'=8] {'expert'}, dimensions={0} | all-to-all | bytes 25165824 | tf_op jit(solution)/shard_map/all_to_all | solution.py:29
  194.0 1.9 copy.44
  196.0 7.9 %fusion.5 = (f32[2,768]{1,0:T(2,128)S(1)}, f32[2,768,384]{1,2,0:T(8,128)S(1)}) fusion(bf16[2,384,768]{2,1,0:T(8,128)(2,1)S(1)} %copy-done.2, bf16[2,384,768]{2,1,0:T(8,128)(2,1)S(1)} %copy-done.1, bf16[2,768,4096]{2,1,0:T(8,128)(2,1)S(1)} %bitcast.48, bf16[2,384,4096]{2,1,0:T(8,128)(2,1)} %param.13), kind=kOutput, calls=%fused_computation.16 | convolution fusion | flops 4837145088 | bytes 23599104 | tf_op jit(solution)/shard_map/esd,efd->efs/dot_general | solution.py:30
  203.9 14.8 %fusion.12 = f32[2,768,4096]{2,1,0:T(8,128)} fusion(bf16[2,384,4096]{2,1,0:T(8,128)(2,1)} %param.11, bf16[2,384,768]{2,1,0:T(8,128)(2,1)S(1)} %copy-done.2, bf16[2,384,768]{2,1,0:T(8,128)(2,1)S(1)} %copy-done.1, f32[2,768,384]{1,2,0:T(8,128)S(1)} %get-tuple-element.9), kind=kOutput, calls=%fused_computation.23 | convolution fusion | flops 4838916096 | bytes 36175872 | tf_op jit(solution)/shard_map/efc,efs->esc/dot_general | solution.py:41
  218.7 16.3 %add_convert_fusion = bf16[2,768,4096]{2,1,0:T(8,128)(2,1)} fusion(f32[2,768,4096]{2,1,0:T(8,128)} %fusion.12, bf16[2,384,4096]{2,1,0:T(8,128)(2,1)} %param.12, f32[2,768,384]{1,2,0:T(8,128)S(1)} %get-tuple-element.9, bf16[2,384,768]{2,1,0:T(8,128)(2,1)S(1)} %copy-done.1), kind=kOutput, calls=%fused_computation.4 | convolution fusion | flops 4848549888 | bytes 47579136 | tf_op jit(solution)/shard_map/efc,efs->esc/dot_general | solution.py:42
  235.0 10.8 %psum.7 = bf16[2,768]{1,0:T(2,128)(2,1)S(1)} all-reduce(f32[2,768]{1,0:T(2,128)S(1)} %get-tuple-element.8), channel_id=1, replica_groups=mesh['section'=4,'expert'=8] {'section'}, use_global_device_ids=true, to_apply=%region_7.8 | all-reduce | flops 1536 | bytes 9216 | tf_op jit(solution)/shard_map/psum | solution.py:36
  246.5 3.5 all-to-all-start.2
  250.0 194.9 %reduce-scatter.2.cloned.1.call-done = bf16[2,768,1024]{2,1,0:T(8,128)(2,1)} async-done(((bf16[2,768,4096]{2,1,0:T(8,128)(2,1)}), bf16[2,768,1024]{2,1,0:T(8,128)(2,1)}) %reduce-scatter.2.cloned.1.call-update) | async-done | bytes 3145744 | tf_op jit(solution)/shard_map/reduce_scatter | solution.py:43
  445.0 6.8 %copy.47 = bf16[2,768,1024]{2,0,1:T(2,128)(2,1)} copy(bf16[2,768,1024]{2,1,0:T(8,128)(2,1)} %reduce-scatter.2.cloned.1.call-done) | data formatting | bytes 6291456 | tf_op jit(solution)/shard_map/reduce_scatter | solution.py:43
  451.8 3.8 all-to-all-start.1
  455.8 6.8 %gather_fusion.2 = bf16[1024]{0:T(1024)(128)(2,1)S(1)} fusion(bf16[1536]{0:T(1024)(128)(2,1)S(1)} %reshape.75, s32[1024]{0:T(1024)S(1)} %broadcast_clamp_fusion), kind=kCustom, calls=%fused_computation.2 | custom fusion | bytes 8192 | tf_op jit(solution)/shard_map/gather | solution.py:53
  463.4 30.0 %all-to-all-done.1 = bf16[2,768,1024]{2,0,1:T(2,128)(2,1)S(1)} async-done(((bf16[2,768,1024]{2,0,1:T(2,128)(2,1)}), bf16[2,768,1024]{2,0,1:T(2,128)(2,1)S(1)}, u32[]{:S(2)}, u32[]{:S(2)}) %all-to-all-start.1) | async-done | bytes 3145760 | tf_op jit(solution)/shard_map/all_to_all | solution.py:45
  493.4 1.7 copy-done
  495.1 2.9 copy.48
  498.0 5.4 %gather_fusion.1 = bf16[1024,1024]{1,0:T(8,128)(2,1)} fusion(bf16[1536,1024]{1,0:T(8,128)(2,1)S(1)} %bitcast.45, s32[1024]{0:T(1024)S(1)} %broadcast_clamp_fusion), kind=kCustom, calls=%fused_computation.1 | custom fusion | bytes 4198400 | tf_op jit(solution)/shard_map/gather | solution.py:48
  503.3 3.7 fusion
  (34 shorter events, 2.6 us)
Async XLA Ops:
  7.2 33.1 %all-gather.2.cloned.1.call-start = ((), (), s32[]{:S(2)}) async-start(), calls=%async_computation.4 | async-start | bytes 1310720 | tf_op jit(solution)/shard_map/all_gather | solution.py:26
  7.9 437.1 %reduce-scatter.2.cloned.1.call-start = ((), (), s32[]{:S(2)}) async-start(), calls=%async_computation.5 | async-start | bytes 15728640 | tf_op jit(solution)/shard_map/reduce_scatter | solution.py:43
  194.0 2.0 copy-start.1
  194.0 2.0 copy-start.2
  246.5 205.3 %all-to-all-start.2 = ((bf16[2,8,96]{2,0,1:T(2,128)(2,1)}), bf16[2,8,96]{2,0,1:T(2,128)(2,1)S(1)}, u32[]{:S(2)}, u32[]{:S(2)}) async-start(bf16[2,8,96]{2,0,1:T(2,128)(2,1)} %copy.50), calls=%async_computation.3 | async-start | bytes 8192 | tf_op jit(solution)/shard_map/all_to_all | solution.py:46
  451.8 3.8 copy-start.3
  451.8 41.6 %all-to-all-start.1 = ((bf16[2,768,1024]{2,0,1:T(2,128)(2,1)}), bf16[2,768,1024]{2,0,1:T(2,128)(2,1)S(1)}, u32[]{:S(2)}, u32[]{:S(2)}) async-start(bf16[2,768,1024]{2,0,1:T(2,128)(2,1)} %copy.47), calls=%async_computation.2 | async-start | bytes 6291456 | tf_op jit(solution)/shard_map/all_to_all | solution.py:45
  493.4 1.7 copy-start
Sparse Core Ops, SparseCore 0:
  9.6 30.6 all-gather.1
  235.1 209.7 reduce-scatter.1
where the time goes:
time: 514 us
  waiting for transfers between devices  247 us (48%)
  blocking collectives  154 us (30%)
  local copies, waits for them, and re-layouts  43.7 us (9%)
  matrix products  39 us (8%)
  between operations  14.2 us (3%)
  other arithmetic  9.03 us (2%)
  starting transfers between devices  7.39 us (1%)
    reduce_scatter x1, waiting for transfers between devices, local(): lax.psum_scatter(term.astype(jnp.bfloat16), 'section', scatter_dimension=...  195 us
    all_to_all x1, blocking collectives, local(): lax.all_to_all(outgoing, 'expert', split_axis=0, concat_axis=1, tiled=True)  143 us
    all_to_all x1, waiting for transfers between devices, local(): lax.all_to_all(shares, 'expert', split_axis=1, concat_axis=0, tiled=True)  30 us
    all_gather x1, waiting for transfers between devices, local(): full_rows = lax.all_gather(grad_out, 'section', axis=1, tiled=True)  21.1 us
    dot_general x1, matrix products, local(): jnp.einsum('efc,efs->esc', w_up, up_grad, preferred_element_type=jnp.floa...  16.3 us
    dot_general x1, matrix products, local(): jnp.einsum('efc,efs->esc', w_gate, gate_grad, preferred_element_type=jnp....  14.8 us
    psum x1, blocking collectives, local(): router_grad = lax.psum(router_part, 'section').astype(jnp.bfloat16)  10.8 us
  transfers between devices with their start and end apart: 4, of which 3 were waited for; matrix products, arithmetic and copies ran while one was open for 5% of the time, Pallas kernels for 0%

commit v1 on v0

v1 whole, which is shorter than its diff:
```python
import functools

import jax
import jax.numpy as jnp
from jax import lax
from jax.experimental import pallas as pl
from jax.experimental.pallas import tpu as pltpu
from jax.sharding import PartitionSpec as P

CHUNKS = 2
F32, BF16 = jnp.float32, jnp.bfloat16
ROWS_BY_ROWS = (((1,), (1,)), ((), ()))
VMEM = 40 << 20


def coefficient_kernel(slot_ref, prob_ref, gate_ref, up_ref, cg_ref, cu_ref, cr_ref):
    rows, slots = slot_ref.shape[0], gate_ref.shape[2]
    width = gate_ref.shape[1]
    column = lax.broadcasted_iota(jnp.int32, (rows, slots), 1)
    for e in range(gate_ref.shape[0]):
        pick = jnp.where(slot_ref[:, e : e + 1] == column, 1.0, 0.0).astype(BF16)
        g = lax.dot_general(pick, gate_ref[e], ROWS_BY_ROWS, preferred_element_type=F32)
        u = lax.dot_general(pick, up_ref[e], ROWS_BY_ROWS, preferred_element_type=F32)
        p = prob_ref[:, e : e + 1]
        sg = 1.0 / (1.0 + jnp.exp(-g))
        silu = g * sg
        span = slice(e * width, (e + 1) * width)
        cg_ref[:, span] = u * sg * (1.0 + g * (1.0 - sg)) * p
        cu_ref[:, span] = silu * p
        cr_ref[:, span] = silu * u


def coefficients(slot, prob, saved_gate, saved_up, tile):
    total, experts = slot.shape
    width = saved_gate.shape[1]
    row = lambda n: pl.BlockSpec((tile, n), lambda i: (i, 0))
    whole = pl.BlockSpec(saved_gate.shape, lambda i: (0, 0, 0))
    return pl.pallas_call(
        coefficient_kernel,
        grid=(total // tile,),
        in_specs=[row(experts), row(experts), whole, whole],
        out_specs=[row(experts * width)] * 3,
        out_shape=[jax.ShapeDtypeStruct((total, experts * width), F32)] * 3,
        compiler_params=pltpu.CompilerParams(vmem_limit_bytes=VMEM),
        name="coefficients",
    )(slot, prob, saved_gate, saved_up)


def hidden_kernel(order, experts, z_ref, *refs):
    blocks = refs[: len(refs) - 8]
    wd_ref, cg_ref, cu_ref, cr_ref, ag_ref, au_ref, r_ref, acc_ref = refs[len(refs) - 8 :]
    step, last = pl.program_id(0), pl.num_programs(0) - 1
    x = jnp.concatenate([blocks[i][j, 0] for i, j in order], axis=0)
    part = lax.dot_general(x, wd_ref[...], ROWS_BY_ROWS, preferred_element_type=F32)

    @pl.when(step == 0)
    def _():
        acc_ref[...] = part

    @pl.when(step > 0)
    def _():
        acc_ref[...] += part

    @pl.when(step == last)
    def _():
        h = acc_ref[...]
        ag_ref[...] = (h * cg_ref[...]).astype(BF16)
        au_ref[...] = (h * cu_ref[...]).astype(BF16)
        terms = h * cr_ref[...]
        width = terms.shape[1] // experts
        for e in range(experts):
            r_ref[:, e : e + 1] = jnp.sum(
                terms[:, e * width : (e + 1) * width], axis=1, keepdims=True
            )


def hidden(z, blocks, order, w_down, coefs, chunk, experts):
    steps, rows, span = blocks[0].shape[1:]
    total = rows * len(order)
    units = w_down.shape[0]
    block = lambda n: pl.BlockSpec((n, 1, rows, span), lambda s, z: (0, s, 0, 0))
    coef = pl.BlockSpec((total, units), lambda s, z: (chunk, 0))
    full = lambda n: pl.BlockSpec((total, n), lambda s, z: (0, 0))
    return pl.pallas_call(
        functools.partial(hidden_kernel, order, experts),
        grid_spec=pltpu.PrefetchScalarGridSpec(
            num_scalar_prefetch=1,
            grid=(steps,),
            in_specs=[block(b.shape[0]) for b in blocks]
            + [pl.BlockSpec((units, span), lambda s, z: (0, lax.rem(z[0] + s, steps)))]
            + [coef] * 3,
            out_specs=[full(units), full(units), full(experts)],
            scratch_shapes=[pltpu.VMEM((total, units), F32)],
        ),
        out_shape=[jax.ShapeDtypeStruct((total, units), BF16)] * 2
        + [jax.ShapeDtypeStruct((total, experts), F32)],
        compiler_params=pltpu.CompilerParams(vmem_limit_bytes=VMEM),
        name="hidden",
    )(z, *blocks, w_down, *coefs)


def out_kernel(z_ref, ag_ref, au_ref, wg_ref, wu_ref, *outs):
    y = jnp.dot(ag_ref[...], wg_ref[...], preferred_element_type=F32)
    y = y + jnp.dot(au_ref[...], wu_ref[...], preferred_element_type=F32)
    y = y.astype(BF16)
    at = 0
    for out in outs:
        count, _, rows, _ = out.shape
        for j in range(count):
            out[j, 0] = y[at : at + rows]
            at += rows


def expand(z, ag, au, w_gate, w_up, steps, rows, counts):
    total, units = ag.shape
    span = w_gate.shape[1] // steps
    whole = pl.BlockSpec((total, units), lambda s, z: (0, 0))
    weight = pl.BlockSpec((units, span), lambda s, z: (0, lax.rem(z[0] + s, steps)))
    return pl.pallas_call(
        out_kernel,
        grid_spec=pltpu.PrefetchScalarGridSpec(
            num_scalar_prefetch=1,
            grid=(steps,),
            in_specs=[whole, whole, weight, weight],
            out_specs=[
                pl.BlockSpec((n, 1, rows, span), lambda s, z: (0, s, 0, 0)) for n in counts
            ],
        ),
        out_shape=[jax.ShapeDtypeStruct((n, steps, rows, span), BF16) for n in counts],
        compiler_params=pltpu.CompilerParams(vmem_limit_bytes=VMEM),
        name="expand",
    )(z, ag, au, w_gate, w_up)


def add(*terms):
    return functools.reduce(lambda a, b: a + b, [t.astype(F32) for t in terms])


def local(grad_out, probs, expert_ids, w_gate, w_up, w_down, saved_gate, saved_up):
    groups, sections = lax.axis_size("expert"), lax.axis_size("section")
    me, z = lax.axis_index("expert"), lax.axis_index("section")
    experts, units, features = w_gate.shape
    slots = saved_gate.shape[2]
    capacity = slots // groups
    tokens, topk = expert_ids.shape
    span = grad_out.shape[1]
    rows = tokens // CHUNKS
    square = groups == 8

    core = me % 2
    near = jnp.where(core == 0, 2, 4)
    far = 6 - near

    def swap(x, even, odd):
        return lax.ppermute(x, "expert", [(i, i ^ (even, odd)[i % 2]) for i in range(groups)])

    def shift(x, by):
        return lax.ppermute(x, "section", [(i, (i + by) % sections) for i in range(sections)])

    if square:
        owners = jnp.stack([me, me ^ near, me ^ near ^ 1, me ^ 6, me ^ 1, me ^ 1 ^ far, me ^ far, me ^ 7])
        order = ((0, 0), (1, 0), (1, 1), (3, 0), (0, 1), (2, 0), (2, 1), (4, 0))
        counts = (groups // 2, groups // 2)
    else:
        owners = jnp.arange(groups)
        order = tuple((0, i) for i in range(groups))
        counts = (groups,)

    routing = jnp.concatenate([expert_ids.T.astype(F32), probs.T], axis=0)[None]
    if square:
        for bit in (2, 4, 1):
            routing = jnp.concatenate([routing, swap(routing, bit, bit)], axis=0)
        even = routing[jnp.array([0, 1, 5, 3, 4, 6, 2, 7])]
        odd = routing[jnp.array([0, 2, 6, 3, 4, 5, 1, 7])]
        routing = jnp.where(core == 0, even, odd)
    else:
        routing = lax.all_gather(routing, "expert", axis=0, tiled=True)
    mine = (me * experts + jnp.arange(experts)).astype(F32)
    chosen = routing[:, None, :topk] == mine[None, :, None, None]
    weight = jnp.sum(jnp.where(chosen, routing[:, None, topk:], 0.0), axis=2)
    named = jnp.any(chosen, axis=2)
    earlier = jnp.arange(tokens)[:, None] < jnp.arange(tokens)[None, :]
    position = lax.dot_general(
        named.astype(BF16), earlier.astype(BF16), (((2,), (0,)), ((), ())), preferred_element_type=F32
    ).astype(jnp.int32)
    slot = jnp.where(named, owners[:, None, None] * capacity + position, -1)

    def by_chunk(x):
        x = x.reshape(groups, experts, CHUNKS, rows)
        return x.transpose(2, 0, 3, 1).reshape(CHUNKS * groups * rows, experts)

    coefs = coefficients(by_chunk(slot), by_chunk(weight), saved_gate, saved_up, min(512, groups * rows))

    flat = lambda w: w.reshape(experts * units, features)
    start = z.astype(jnp.int32).reshape(1)
    results, routers = [], []
    for c in range(CHUNKS):
        piece = grad_out[c * rows : (c + 1) * rows]
        own = jnp.stack([piece] + [shift(piece, -i) for i in range(1, sections)])
        if square:
            pair = jnp.stack([own, swap(own, 1, 1)])
            first = swap(pair, 2, 4)
            second = swap(first[:1], 4, 2)
            blocks = [pair, first, swap(first, 1, 1), second, swap(second, 1, 1)]
        else:
            blocks = [lax.all_gather(own, "expert")]
        ag, au, router = hidden(start, blocks, order, flat(w_down), coefs, c, experts)
        routers.append(router.reshape(groups, rows, experts))
        outs = expand(start, ag, au, flat(w_gate), flat(w_up), sections, rows, counts)
        if square:
            kept = add(outs[0], swap(outs[1], 1, 1)).astype(BF16)
            diagonal = swap(kept[3], 4, 2)
            sent = jnp.stack([add(kept[1], diagonal).astype(BF16), kept[2]])
            received = swap(sent, 2, 4)
            total = add(kept[0], received[0], swap(received[1], 1, 1))
        else:
            total = lax.psum_scatter(outs[0], "expert", scatter_dimension=0, tiled=True)[0].astype(F32)
        sums = total.astype(BF16)
        results.append(add(total[0], *[shift(sums[i], i) for i in range(1, sections)]).astype(BF16))
    grad_in = jnp.concatenate(results, axis=0)

    router = jnp.concatenate(routers, axis=1)
    if square:
        for bit in range(sections.bit_length() - 1):
            by = 1 << bit
            router = router + lax.ppermute(router, "section", [(i, i ^ by) for i in range(sections)])
        even = router[jnp.array([0, 4, 1, 2, 6, 5, 3, 7])]
        odd = router[jnp.array([0, 4, 6, 5, 1, 2, 3, 7])]
        router = jnp.where(core == 0, even, odd)
        router = router.transpose(0, 2, 1)
        gathered = router[None]
        for bit in (1, 2, 4):
            gathered = jnp.concatenate([gathered, swap(gathered, bit, bit)], axis=0)
        back = jnp.stack([gathered[q, q] for q in range(groups)])
        source = me ^ jnp.arange(groups)
    else:
        router = lax.psum(router, "section").transpose(0, 2, 1)
        back = lax.all_to_all(router, "expert", split_axis=0, concat_axis=0)
        source = jnp.arange(groups)
    number = (source[:, None] * experts + jnp.arange(experts)).reshape(-1)
    back = back.reshape(groups * experts, tokens)
    match = expert_ids[None] == number[:, None, None]
    grad_probs = jnp.sum(jnp.where(match, back[:, :, None], 0.0), axis=0).astype(BF16)
    return (grad_in, grad_probs)


def solution(mesh):
    placed = (
        P("expert", "section"),
        P("expert", None),
        P("expert", None),
        P("expert", "section", None),
        P("expert", "section", None),
        P("expert", "section", None),
        P("expert", "section", None),
        P("expert", "section", None),
    )
    return jax.shard_map(
        local,
        mesh=mesh,
        in_specs=placed,
        out_specs=(P("expert", "section"), P("expert", None)),
        check_vma=False,
    )
```

time: 514 us -> 219 us (0.43)
  blocking collectives: 154 us -> 0 us
  waiting for transfers between devices: 247 us -> 96.2 us
  starting transfers between devices: 7.39 us -> 51.6 us
  Pallas kernels: 0 us -> 40.2 us
  matrix products: 39 us -> 0.09 us
  local copies, waits for them, and re-layouts: 43.7 us -> 21.1 us
  between operations: 14.2 us -> 1.09 us
    reduce_scatter x1 -> x0, waiting for transfers between devices: 195 us -> none  [local(): lax.psum_scatter(term.astype(jnp.bfloat16), 'section', scatter_dimension=...]
    all_to_all x1 -> x0, blocking collectives: 143 us -> none  [local(): lax.all_to_all(outgoing, 'expert', split_axis=0, concat_axis=1, tiled=True)]
    ppermute x0 -> x38, waiting for transfers between devices: none -> 96.2 us  [the longest x24 63.3 us: swap(): lax.ppermute(x, 'expert', [(i, i ^ (even, odd)[i % 2]) for i in range(gro...]
    ppermute x0 -> x38, starting transfers between devices: none -> 51.6 us  [the longest x12 26.6 us: shift(): lax.ppermute(x, 'section', [(i, (i + by) % sections) for i in range(secti...]
    pallas_call x0 -> x5, Pallas kernels: none -> 40.2 us  [the longest x2 20.1 us: expand(): pl.pallas_call(out_kernel, grid_spec=pltpu.PrefetchScalarGridSpec(num_sca...]
    dot_general x3 -> x1, matrix products: 39 us -> 0.09 us  [local(): lax.dot_general(named.astype(BF16), earlier.astype(BF16), (((2,), (0,)),...]
    all_to_all x2 -> x0, waiting for transfers between devices: 30.1 us -> none  [the longest x1 30 us: local(): lax.all_to_all(shares, 'expert', split_axis=1, concat_axis=0, tiled=True)]
    all_gather x1 -> x0, waiting for transfers between devices: 21.1 us -> none  [local(): full_rows = lax.all_gather(grad_out, 'section', axis=1, tiled=True)]
  transfers between devices with their start and end apart: 4 -> 38, of which waited for: 3 -> 20; matrix products, arithmetic and copies ran while one was open for 5% -> 7% of each run, Pallas kernels for 0% -> 18%
where the time goes in v1:
time: 219 us
  waiting for transfers between devices  96.2 us (44%)
  starting transfers between devices  51.6 us (24%)
  Pallas kernels  40.2 us (18%)
  local copies, waits for them, and re-layouts  21.1 us (10%)
  other arithmetic  8.61 us (4%)
    ppermute x24, waiting for transfers between devices, swap(): lax.ppermute(x, 'expert', [(i, i ^ (even, odd)[i % 2]) for i in range(gro...  63.3 us
    ppermute x12, waiting for transfers between devices, shift(): lax.ppermute(x, 'section', [(i, (i + by) % sections) for i in range(secti...  28.2 us
    ppermute x12, starting transfers between devices, shift(): lax.ppermute(x, 'section', [(i, (i + by) % sections) for i in range(secti...  26.6 us
    ppermute x24, starting transfers between devices, swap(): lax.ppermute(x, 'expert', [(i, i ^ (even, odd)[i % 2]) for i in range(gro...  20.4 us
    pallas_call x2, Pallas kernels, expand(): pl.pallas_call(out_kernel, grid_spec=pltpu.PrefetchScalarGridSpec(num_sca...  20.1 us
    pallas_call x2, Pallas kernels, hidden(): pl.pallas_call(functools.partial(hidden_kernel, order, experts), grid_spe...  16 us
    unnamed x57, local copies, waits for them, and re-layouts  11.8 us
    convert_element_type x2, other arithmetic, local(): kept = add(outs[0], swap(outs[1], 1, 1)).astype(BF16)  5.11 us
  transfers between devices with their start and end apart: 38, of which 20 were waited for; matrix products, arithmetic and copies ran while one was open for 7% of the time, Pallas kernels for 18%

profile of v1, /device:TPU:0, one launch (start us, length us, event | category | flops | bytes accessed | tf_op | source)
XLA Modules:
  0.0 218.9 jit_solution(8419918383582790987)
XLA Ops:
  1.7 3.1 %collective-permute-start.20 = (bf16[64,1024]{1,0:T(8,128)(2,1)S(1)}, bf16[64,1024]{1,0:T(8,128)(2,1)S(1)}, u32[]{:S(2)}, u32[]{:S(2)}) collective-permute-start(bf16[64,1024]{1,0:T(8,128)(2,1)S(1)} %get-tuple-element.48), channel_id=1, source_target_pairs={{0,8},{8,16},{16,24},{24,0},{1,9},{9,17},{17,25},{25,1},{2,10},{10... | collective-permute-start | bytes 393224 | tf_op jit(solution)/shard_map/ppermute | solution.py:158
  4.7 2.6 %collective-permute-start.19 = (bf16[64,1024]{1,0:T(8,128)(2,1)S(1)}, bf16[64,1024]{1,0:T(8,128)(2,1)S(1)}, u32[]{:S(2)}, u32[]{:S(2)}) collective-permute-start(bf16[64,1024]{1,0:T(8,128)(2,1)S(1)} %get-tuple-element.48), channel_id=1, source_target_pairs={{0,16},{8,24},{16,0},{24,8},{1,17},{9,25},{17,1},{25,9},{2,18},{10... | collective-permute-start | bytes 393224 | tf_op jit(solution)/shard_map/ppermute | solution.py:158
  11.2 4.8 %collective-permute-done.19 = bf16[64,1024]{1,0:T(8,128)(2,1)S(1)} collective-permute-done((bf16[64,1024]{1,0:T(8,128)(2,1)S(1)}, bf16[64,1024]{1,0:T(8,128)(2,1)S(1)}, u32[]{:S(2)}, u32[]{:S(2)}) %collective-permute-start.19) | collective-permute-done | bytes 131104 | tf_op jit(solution)/shard_map/ppermute | solution.py:158
  16.1 3.3 %collective-permute-start.2 = (bf16[64,1024]{1,0:T(8,128)(2,1)S(1)}, bf16[64,1024]{1,0:T(8,128)(2,1)S(1)}, u32[]{:S(2)}, u32[]{:S(2)}) collective-permute-start(bf16[64,1024]{1,0:T(8,128)(2,1)S(1)} %get-tuple-element.49), channel_id=1, source_target_pairs={{0,8},{8,16},{16,24},{24,0},{1,9},{9,17},{17,25},{25,1},{2,10},{10... | collective-permute-start | bytes 393224 | tf_op jit(solution)/shard_map/ppermute | solution.py:158
  21.9 3.1 %collective-permute-done.2 = bf16[64,1024]{1,0:T(8,128)(2,1)S(1)} collective-permute-done((bf16[64,1024]{1,0:T(8,128)(2,1)S(1)}, bf16[64,1024]{1,0:T(8,128)(2,1)S(1)}, u32[]{:S(2)}, u32[]{:S(2)}) %collective-permute-start.2) | collective-permute-done | bytes 131104 | tf_op jit(solution)/shard_map/ppermute | solution.py:158
  25.0 5.3 %collective-permute-done.1 = bf16[64,1024]{1,0:T(8,128)(2,1)S(1)} collective-permute-done((bf16[64,1024]{1,0:T(8,128)(2,1)S(1)}, bf16[64,1024]{1,0:T(8,128)(2,1)S(1)}, u32[]{:S(2)}, u32[]{:S(2)}) %collective-permute-start.1) | collective-permute-done | bytes 131104 | tf_op jit(solution)/shard_map/ppermute | solution.py:158
  34.7 27.9 %collective-permute-done.8 = f32[1,16,128]{2,1,0:T(8,128)S(1)} collective-permute-done((f32[1,16,128]{2,1,0:T(8,128)S(1)}, f32[1,16,128]{2,1,0:T(8,128)S(1)}, u32[]{:S(2)}, u32[]{:S(2)}) %collective-permute-start.8) | collective-permute-done | bytes 8224 | tf_op jit(solution)/shard_map/ppermute | solution.py:155
  81.9 4.1 %coefficients.1 = (f32[1024,768]{1,0:T(8,128)S(1)}, f32[1024,768]{1,0:T(8,128)S(1)}, f32[1024,768]{1,0:T(8,128)S(1)}) custom-call(s32[1024,2]{1,0:T(8,128)S(1)} %bitcast.148, f32[1024,2]{1,0:T(8,128)S(1)} %bitcast.149, bf16[2,384,768]{2,1,0:T(8,128)(2,1)S(1)} %copy-done.11, bf16[2,384,768]{2,1,0:T(8,128)(2,1)S(1)} %copy-done.12), custom_call_target="tpu_custom_call" | custom-call | tf_op jit(solution)/shard_map/coefficients/pallas_call | solution.py:38
  89.0 8.1 %hidden.3 = (bf16[512,768]{1,0:T(8,128)(2,1)S(1)}, bf16[512,768]{1,0:T(8,128)(2,1)S(1)}, f32[512,2]{1,0:T(8,128)S(1)}) custom-call(s32[1]{0:T(128)} %bitcast.z_ref, bf16[2,4,64,1024]{3,2,1,0:T(8,128)(2,1)S(1)} %copy-done.4, bf16[2,4,64,1024]{3,2,1,0:T(8,128)(2,1)} %collective-permute-done.22.refs_1_, ...), custom_call_target="tpu_custom_call" | custom-call | tf_op jit(solution)/shard_map/hidden/pallas_call | solution.py:84
  97.9 10.1 %expand.3 = (bf16[4,4,64,1024]{3,2,1,0:T(8,128)(2,1)S(1)}, bf16[4,4,64,1024]{3,2,1,0:T(8,128)(2,1)}) custom-call(s32[1]{0:T(128)} %bitcast.z_ref, bf16[512,768]{1,0:T(8,128)(2,1)S(1)} %get-tuple-element.22.ag_ref, bf16[512,768]{1,0:T(8,128)(2,1)S(1)} %get-tuple-element.23.au_ref, bf16[768,4096]{1,0:T(8,128)(2,1)S(1)} %bitcast.146, bf16[768,4096]{1,0:T(8,128)(2,1)} %bitcast.152), custom_call_target="tpu_custom_call" | custom-call | tf_op jit(solution)/shard_map/expand/pallas_call | solution.py:119
  109.8 4.6 %collective-permute-done.7.refs_4_ = bf16[1,4,64,1024]{3,2,1,0:T(8,128)(2,1)S(1)} collective-permute-done((bf16[1,4,64,1024]{3,2,1,0:T(8,128)(2,1)}, bf16[1,4,64,1024]{3,2,1,0:T(8,128)(2,1)S(1)}, u32[]{:S(2)}, u32[]{:S(2)}) %collective-permute-start.7) | collective-permute-done | bytes 524320 | tf_op jit(solution)/shard_map/ppermute | solution.py:155
  114.4 7.9 %hidden.2 = (bf16[512,768]{1,0:T(8,128)(2,1)S(1)}, bf16[512,768]{1,0:T(8,128)(2,1)S(1)}, f32[512,2]{1,0:T(8,128)S(1)}) custom-call(s32[1]{0:T(128)} %bitcast.z_ref, bf16[2,4,64,1024]{3,2,1,0:T(8,128)(2,1)S(1)} %copy-done.2, bf16[2,4,64,1024]{3,2,1,0:T(8,128)(2,1)} %collective-permute-done.4.refs_1_, bf16[2,4,64,1024]{3,2,1,0:T(8,128)(2,1)} %collective-permute-done.5.refs_2_, ...), custom_call_target="tpu_custom_call" | custom-call | tf_op jit(solution)/shard_map/hidden/pallas_call | solution.py:84
  123.0 10.0 %expand.2 = (bf16[4,4,64,1024]{3,2,1,0:T(8,128)(2,1)S(1)}, bf16[4,4,64,1024]{3,2,1,0:T(8,128)(2,1)}) custom-call(s32[1]{0:T(128)} %bitcast.z_ref, bf16[512,768]{1,0:T(8,128)(2,1)S(1)} %get-tuple-element.18.ag_ref, bf16[512,768]{1,0:T(8,128)(2,1)S(1)} %get-tuple-element.19.au_ref, bf16[768,4096]{1,0:T(8,128)(2,1)S(1)} %bitcast.147, bf16[768,4096]{1,0:T(8,128)(2,1)} %bitcast.153), custom_call_target="tpu_custom_call" | custom-call | tf_op jit(solution)/shard_map/expand/pallas_call | solution.py:119
  134.9 3.3 %collective-permute-start.33 = (f32[8,128,2]{1,2,0:T(2,128)S(1)}, f32[8,128,2]{1,2,0:T(2,128)S(1)}, u32[]{:S(2)}, u32[]{:S(2)}) collective-permute-start(f32[8,128,2]{1,2,0:T(2,128)S(1)} %pad_maximum_fusion.12), channel_id=1, source_target_pairs={{0,8},{8,0},{16,24},{24,16},{1,9},{9,1},{17,25},{25,17},{2,10},{10... | collective-permute-start | bytes 24584 | tf_op jit(solution)/shard_map/ppermute | solution.py:226
  141.2 3.2 %collective-permute-done.34 = f32[8,128,2]{1,2,0:T(2,128)S(1)} collective-permute-done((f32[8,128,2]{1,2,0:T(2,128)S(1)}, f32[8,128,2]{1,2,0:T(2,128)S(1)}, u32[]{:S(2)}, u32[]{:S(2)}) %collective-permute-start.34) | collective-permute-done | bytes 8224 | tf_op jit(solution)/shard_map/ppermute | solution.py:226
  159.6 3.5 %collective-permute-done.27 = bf16[4,64,1024]{2,1,0:T(8,128)(2,1)S(1)} collective-permute-done((bf16[4,64,1024]{2,1,0:T(8,128)(2,1)S(1)}, bf16[4,64,1024]{2,1,0:T(8,128)(2,1)S(1)}, u32[]{:S(2)}, u32[]{:S(2)}) %collective-permute-start.27) | collective-permute-done | bytes 524320 | tf_op jit(solution)/shard_map/ppermute | solution.py:155
  165.0 8.5 %collective-permute-done.12 = bf16[4,64,1024]{2,1,0:T(8,128)(2,1)S(1)} collective-permute-done((bf16[4,64,1024]{2,1,0:T(8,128)(2,1)S(1)}, bf16[4,64,1024]{2,1,0:T(8,128)(2,1)S(1)}, u32[]{:S(2)}, u32[]{:S(2)}) %collective-permute-start.12) | collective-permute-done | bytes 524320 | tf_op jit(solution)/shard_map/ppermute | solution.py:155
  175.3 3.0 %collective-permute-done.28 = bf16[2,4,64,1024]{3,2,1,0:T(8,128)(2,1)S(1)} collective-permute-done((bf16[2,4,64,1024]{3,2,1,0:T(8,128)(2,1)S(1)}, bf16[2,4,64,1024]{3,2,1,0:T(8,128)(2,1)S(1)}, u32[]{:S(2)}, u32[]{:S(2)}) %collective-permute-start.28) | collective-permute-done | bytes 1048608 | tf_op jit(solution)/shard_map/ppermute | solution.py:155
  180.9 8.7 %collective-permute-done.13 = bf16[2,4,64,1024]{3,2,1,0:T(8,128)(2,1)S(1)} collective-permute-done((bf16[2,4,64,1024]{3,2,1,0:T(8,128)(2,1)S(1)}, bf16[2,4,64,1024]{3,2,1,0:T(8,128)(2,1)S(1)}, u32[]{:S(2)}, u32[]{:S(2)}) %collective-permute-start.13) | collective-permute-done | bytes 1048608 | tf_op jit(solution)/shard_map/ppermute | solution.py:155
  191.5 2.8 %collective-permute-start.32 = (bf16[64,1024]{1,0:T(8,128)(2,1)S(1)}, bf16[64,1024]{1,0:T(8,128)(2,1)S(1)}, u32[]{:S(2)}, u32[]{:S(2)}) collective-permute-start(bf16[64,1024]{1,0:T(8,128)(2,1)S(1)} %get-tuple-element.42), channel_id=1, source_target_pairs={{0,24},{8,0},{16,8},{24,16},{1,25},{9,1},{17,9},{25,17},{2,26},{10... | collective-permute-start | bytes 393224 | tf_op jit(solution)/shard_map/ppermute | solution.py:158
  195.4 3.9 %collective-permute-start.17 = (bf16[64,1024]{1,0:T(8,128)(2,1)S(1)}, bf16[64,1024]{1,0:T(8,128)(2,1)S(1)}, u32[]{:S(2)}, u32[]{:S(2)}) collective-permute-start(bf16[64,1024]{1,0:T(8,128)(2,1)S(1)} %get-tuple-element.37), channel_id=1, source_target_pairs={{0,24},{8,0},{16,8},{24,16},{1,25},{9,1},{17,9},{25,17},{2,26},{10... | collective-permute-start | bytes 393224 | tf_op jit(solution)/shard_map/ppermute | solution.py:158
  199.6 5.9 %collective-permute-start.15 = (bf16[64,1024]{1,0:T(8,128)(2,1)S(1)}, bf16[64,1024]{1,0:T(8,128)(2,1)S(1)}, u32[]{:S(2)}, u32[]{:S(2)}) collective-permute-start(bf16[64,1024]{1,0:T(8,128)(2,1)S(1)} %get-tuple-element.36), channel_id=1, source_target_pairs={{0,8},{8,16},{16,24},{24,0},{1,9},{9,17},{17,25},{25,1},{2,10},{10... | collective-permute-start | bytes 393224 | tf_op jit(solution)/shard_map/ppermute | solution.py:158
  205.6 7.9 %collective-permute-done.31 = bf16[64,1024]{1,0:T(8,128)(2,1)S(1)} collective-permute-done((bf16[64,1024]{1,0:T(8,128)(2,1)S(1)}, bf16[64,1024]{1,0:T(8,128)(2,1)S(1)}, u32[]{:S(2)}, u32[]{:S(2)}) %collective-permute-start.31) | collective-permute-done | bytes 131104 | tf_op jit(solution)/shard_map/ppermute | solution.py:158
  213.5 4.6 %collective-permute-done.16 = bf16[64,1024]{1,0:T(8,128)(2,1)S(1)} collective-permute-done((bf16[64,1024]{1,0:T(8,128)(2,1)S(1)}, bf16[64,1024]{1,0:T(8,128)(2,1)S(1)}, u32[]{:S(2)}, u32[]{:S(2)}) %collective-permute-start.16) | collective-permute-done | bytes 131104 | tf_op jit(solution)/shard_map/ppermute | solution.py:158
  (176 shorter events, 67.8 us)
Async XLA Ops:
  1.7 9.5 %collective-permute-start.20 = (bf16[64,1024]{1,0:T(8,128)(2,1)S(1)}, bf16[64,1024]{1,0:T(8,128)(2,1)S(1)}, u32[]{:S(2)}, u32[]{:S(2)}) collective-permute-start(bf16[64,1024]{1,0:T(8,128)(2,1)S(1)} %get-tuple-element.48), channel_id=1, source_target_pairs={{0,8},{8,16},{16,24},{24,0},{1,9},{9,17},{17,25},{25,1},{2,10},{10... | collective-permute-start | bytes 393224 | tf_op jit(solution)/shard_map/ppermute | solution.py:158
  4.7 11.2 %collective-permute-start.19 = (bf16[64,1024]{1,0:T(8,128)(2,1)S(1)}, bf16[64,1024]{1,0:T(8,128)(2,1)S(1)}, u32[]{:S(2)}, u32[]{:S(2)}) collective-permute-start(bf16[64,1024]{1,0:T(8,128)(2,1)S(1)} %get-tuple-element.48), channel_id=1, source_target_pairs={{0,16},{8,24},{16,0},{24,8},{1,17},{9,25},{17,1},{25,9},{2,18},{10... | collective-permute-start | bytes 393224 | tf_op jit(solution)/shard_map/ppermute | solution.py:158
  16.1 14.4 %collective-permute-start.21 = (bf16[4,64,1024]{2,1,0:T(8,128)(2,1)S(1)}, bf16[4,64,1024]{2,1,0:T(8,128)(2,1)S(1)}, u32[]{:S(2)}, u32[]{:S(2)}) collective-permute-start(bf16[4,64,1024]{2,1,0:T(8,128)(2,1)S(1)} %get-tuple-element.45), channel_id=1, source_target_pairs={{0,1},{1,0},{2,3},{3,2},{4,5},{5,4},{6,7},{7,6},{8,9},{9,8},{10,11... | collective-permute-start | bytes 1572872 | tf_op jit(solution)/shard_map/ppermute | solution.py:155
  19.5 10.9 %collective-permute-start.1 = (bf16[64,1024]{1,0:T(8,128)(2,1)S(1)}, bf16[64,1024]{1,0:T(8,128)(2,1)S(1)}, u32[]{:S(2)}, u32[]{:S(2)}) collective-permute-start(bf16[64,1024]{1,0:T(8,128)(2,1)S(1)} %get-tuple-element.49), channel_id=1, source_target_pairs={{0,16},{8,24},{16,0},{24,8},{1,17},{9,25},{17,1},{25,9},{2,18},{10... | collective-permute-start | bytes 393224 | tf_op jit(solution)/shard_map/ppermute | solution.py:158
  30.7 33.5 %collective-permute-start.22 = (bf16[2,4,64,1024]{3,2,1,0:T(8,128)(2,1)S(1)}, bf16[2,4,64,1024]{3,2,1,0:T(8,128)(2,1)}, u32[]{:S(2)}, u32[]{:S(2)}) collective-permute-start(bf16[2,4,64,1024]{3,2,1,0:T(8,128)(2,1)S(1)} %pad_maximum_fusion.2.refs_0_), channel_id=1, source_target_pairs={{0,2},{1,5},{2,0},{3,7},{4,6},{5,1},{6,4},{7,3},{8,10},{9,13},{10,... | collective-permute-start | bytes 3145736 | tf_op jit(solution)/shard_map/ppermute | solution.py:155
  32.5 36.2 %collective-permute-start.4 = (bf16[2,4,64,1024]{3,2,1,0:T(8,128)(2,1)S(1)}, bf16[2,4,64,1024]{3,2,1,0:T(8,128)(2,1)}, u32[]{:S(2)}, u32[]{:S(2)}) collective-permute-start(bf16[2,4,64,1024]{3,2,1,0:T(8,128)(2,1)S(1)} %pad_maximum_fusion.refs_0_), channel_id=1, source_target_pairs={{0,2},{1,5},{2,0},{3,7},{4,6},{5,1},{6,4},{7,3},{8,10},{9,13},{10,... | collective-permute-start | bytes 3145736 | tf_op jit(solution)/shard_map/ppermute | solution.py:155
  34.1 28.5 %collective-permute-start.8 = (f32[1,16,128]{2,1,0:T(8,128)S(1)}, f32[1,16,128]{2,1,0:T(8,128)S(1)}, u32[]{:S(2)}, u32[]{:S(2)}) collective-permute-start(f32[1,16,128]{2,1,0:T(8,128)S(1)} %maximum_bitcast_fusion), channel_id=1, source_target_pairs={{0,2},{1,3},{2,0},{3,1},{4,6},{5,7},{6,4},{7,5},{8,10},{9,11},{10,... | collective-permute-start | bytes 24584 | tf_op jit(solution)/shard_map/ppermute | solution.py:155
  65.2 9.4 %collective-permute-start.24 = (bf16[1,4,64,1024]{3,2,1,0:T(8,128)(2,1)S(1)}, bf16[1,4,64,1024]{3,2,1,0:T(8,128)(2,1)}, u32[]{:S(2)}, u32[]{:S(2)}) collective-permute-start(bf16[1,4,64,1024]{3,2,1,0:T(8,128)(2,1)S(1)} %slice.157), channel_id=1, source_target_pairs={{0,4},{1,3},{2,6},{3,1},{4,0},{5,7},{6,2},{7,5},{8,12},{9,11},{10,... | collective-permute-start | bytes 1572872 | tf_op jit(solution)/shard_map/ppermute | solution.py:155
  66.3 21.3 %collective-permute-start.23 = (bf16[2,4,64,1024]{3,2,1,0:T(8,128)(2,1)}, bf16[2,4,64,1024]{3,2,1,0:T(8,128)(2,1)}, u32[]{:S(2)}, u32[]{:S(2)}) collective-permute-start(bf16[2,4,64,1024]{3,2,1,0:T(8,128)(2,1)} %collective-permute-done.22.refs_1_), channel_id=1, source_target_pairs={{0,1},{1,0},{2,3},{3,2},{4,5},{5,4},{6,7},{7,6},{8,9},{9,8},{10,11... | collective-permute-start | bytes 3145736 | tf_op jit(solution)/shard_map/ppermute | solution.py:155
  70.6 39.2 %collective-permute-start.6 = (bf16[1,4,64,1024]{3,2,1,0:T(8,128)(2,1)}, bf16[1,4,64,1024]{3,2,1,0:T(8,128)(2,1)}, u32[]{:S(2)}, u32[]{:S(2)}) collective-permute-start(bf16[1,4,64,1024]{3,2,1,0:T(8,128)(2,1)} %slice.144), channel_id=1, source_target_pairs={{0,4},{1,3},{2,6},{3,1},{4,0},{5,7},{6,2},{7,5},{8,12},{9,11},{10,... | collective-permute-start | bytes 1572872 | tf_op jit(solution)/shard_map/ppermute | solution.py:155
  72.1 37.7 %collective-permute-start.5 = (bf16[2,4,64,1024]{3,2,1,0:T(8,128)(2,1)}, bf16[2,4,64,1024]{3,2,1,0:T(8,128)(2,1)}, u32[]{:S(2)}, u32[]{:S(2)}) collective-permute-start(bf16[2,4,64,1024]{3,2,1,0:T(8,128)(2,1)} %collective-permute-done.4.refs_1_), channel_id=1, source_target_pairs={{0,1},{1,0},{2,3},{3,2},{4,5},{5,4},{6,7},{7,6},{8,9},{9,8},{10,11... | collective-permute-start | bytes 3145736 | tf_op jit(solution)/shard_map/ppermute | solution.py:155
  74.6 13.1 %collective-permute-start.25 = (bf16[1,4,64,1024]{3,2,1,0:T(8,128)(2,1)}, bf16[1,4,64,1024]{3,2,1,0:T(8,128)(2,1)}, u32[]{:S(2)}, u32[]{:S(2)}) collective-permute-start(bf16[1,4,64,1024]{3,2,1,0:T(8,128)(2,1)} %collective-permute-done.24.refs_3_), channel_id=1, source_target_pairs={{0,1},{1,0},{2,3},{3,2},{4,5},{5,4},{6,7},{7,6},{8,9},{9,8},{10,11... | collective-permute-start | bytes 1572872 | tf_op jit(solution)/shard_map/ppermute | solution.py:155
  109.3 41.9 %collective-permute-start.26 = (bf16[4,4,64,1024]{3,2,1,0:T(8,128)(2,1)}, bf16[4,4,64,1024]{3,2,1,0:T(8,128)(2,1)}, u32[]{:S(2)}, u32[]{:S(2)}) collective-permute-start(bf16[4,4,64,1024]{3,2,1,0:T(8,128)(2,1)} %get-tuple-element.25), channel_id=1, source_target_pairs={{0,1},{1,0},{2,3},{3,2},{4,5},{5,4},{6,7},{7,6},{8,9},{9,8},{10,11... | collective-permute-start | bytes 6291464 | tf_op jit(solution)/shard_map/ppermute | solution.py:155
  134.4 21.1 %collective-permute-start.11 = (bf16[4,4,64,1024]{3,2,1,0:T(8,128)(2,1)}, bf16[4,4,64,1024]{3,2,1,0:T(8,128)(2,1)}, u32[]{:S(2)}, u32[]{:S(2)}) collective-permute-start(bf16[4,4,64,1024]{3,2,1,0:T(8,128)(2,1)} %get-tuple-element.21), channel_id=1, source_target_pairs={{0,1},{1,0},{2,3},{3,2},{4,5},{5,4},{6,7},{7,6},{8,9},{9,8},{10,11... | collective-permute-start | bytes 6291464 | tf_op jit(solution)/shard_map/ppermute | solution.py:155
  150.6 24.7 %collective-permute-start.37 = (f32[4,8,2,128]{3,2,1,0:T(2,128)S(1)}, f32[4,8,2,128]{3,2,1,0:T(2,128)S(1)}, u32[]{:S(2)}, u32[]{:S(2)}) collective-permute-start(f32[4,8,2,128]{3,2,1,0:T(2,128)S(1)} %pad_maximum_fusion.9), channel_id=1, source_target_pairs={{0,4},{1,5},{2,6},{3,7},{4,0},{5,1},{6,2},{7,3},{8,12},{9,13},{10,... | collective-permute-start | bytes 98312 | tf_op jit(solution)/shard_map/ppermute | solution.py:155
  158.1 15.3 %collective-permute-start.12 = (bf16[4,64,1024]{2,1,0:T(8,128)(2,1)S(1)}, bf16[4,64,1024]{2,1,0:T(8,128)(2,1)S(1)}, u32[]{:S(2)}, u32[]{:S(2)}) collective-permute-start(bf16[4,64,1024]{2,1,0:T(8,128)(2,1)S(1)} %get-tuple-element.32), channel_id=1, source_target_pairs={{0,4},{1,3},{2,6},{3,1},{4,0},{5,7},{6,2},{7,5},{8,12},{9,11},{10,... | collective-permute-start | bytes 1572872 | tf_op jit(solution)/shard_map/ppermute | solution.py:155
  163.4 14.9 %collective-permute-start.28 = (bf16[2,4,64,1024]{3,2,1,0:T(8,128)(2,1)S(1)}, bf16[2,4,64,1024]{3,2,1,0:T(8,128)(2,1)S(1)}, u32[]{:S(2)}, u32[]{:S(2)}) collective-permute-start(bf16[2,4,64,1024]{3,2,1,0:T(8,128)(2,1)S(1)} %pad_maximum_fusion.3), channel_id=1, source_target_pairs={{0,2},{1,5},{2,0},{3,7},{4,6},{5,1},{6,4},{7,3},{8,10},{9,13},{10,... | collective-permute-start | bytes 3145736 | tf_op jit(solution)/shard_map/ppermute | solution.py:155
  173.7 15.8 %collective-permute-start.13 = (bf16[2,4,64,1024]{3,2,1,0:T(8,128)(2,1)S(1)}, bf16[2,4,64,1024]{3,2,1,0:T(8,128)(2,1)S(1)}, u32[]{:S(2)}, u32[]{:S(2)}) collective-permute-start(bf16[2,4,64,1024]{3,2,1,0:T(8,128)(2,1)S(1)} %pad_maximum_fusion.1), channel_id=1, source_target_pairs={{0,2},{1,5},{2,0},{3,7},{4,6},{5,1},{6,4},{7,3},{8,10},{9,13},{10,... | collective-permute-start | bytes 3145736 | tf_op jit(solution)/shard_map/ppermute | solution.py:155
  178.3 12.8 %collective-permute-start.29 = (bf16[4,64,1024]{2,1,0:T(8,128)(2,1)S(1)}, bf16[4,64,1024]{2,1,0:T(8,128)(2,1)S(1)}, u32[]{:S(2)}, u32[]{:S(2)}) collective-permute-start(bf16[4,64,1024]{2,1,0:T(8,128)(2,1)S(1)} %slice_bitcast_fusion), channel_id=1, source_target_pairs={{0,1},{1,0},{2,3},{3,2},{4,5},{5,4},{6,7},{7,6},{8,9},{9,8},{10,11... | collective-permute-start | bytes 1572872 | tf_op jit(solution)/shard_map/ppermute | solution.py:155
  194.3 19.2 %collective-permute-start.31 = (bf16[64,1024]{1,0:T(8,128)(2,1)S(1)}, bf16[64,1024]{1,0:T(8,128)(2,1)S(1)}, u32[]{:S(2)}, u32[]{:S(2)}) collective-permute-start(bf16[64,1024]{1,0:T(8,128)(2,1)S(1)} %get-tuple-element.43), channel_id=1, source_target_pairs={{0,16},{8,24},{16,0},{24,8},{1,17},{9,25},{17,1},{25,9},{2,18},{10... | collective-permute-start | bytes 393224 | tf_op jit(solution)/shard_map/ppermute | solution.py:158
  195.0 18.4 %collective-permute-start.30 = (bf16[64,1024]{1,0:T(8,128)(2,1)S(1)}, bf16[64,1024]{1,0:T(8,128)(2,1)S(1)}, u32[]{:S(2)}, u32[]{:S(2)}) collective-permute-start(bf16[64,1024]{1,0:T(8,128)(2,1)S(1)} %get-tuple-element.41), channel_id=1, source_target_pairs={{0,8},{8,16},{16,24},{24,0},{1,9},{9,17},{17,25},{25,1},{2,10},{10... | collective-permute-start | bytes 393224 | tf_op jit(solution)/shard_map/ppermute | solution.py:158
  195.4 18.1 %collective-permute-start.17 = (bf16[64,1024]{1,0:T(8,128)(2,1)S(1)}, bf16[64,1024]{1,0:T(8,128)(2,1)S(1)}, u32[]{:S(2)}, u32[]{:S(2)}) collective-permute-start(bf16[64,1024]{1,0:T(8,128)(2,1)S(1)} %get-tuple-element.37), channel_id=1, source_target_pairs={{0,24},{8,0},{16,8},{24,16},{1,25},{9,1},{17,9},{25,17},{2,26},{10... | collective-permute-start | bytes 393224 | tf_op jit(solution)/shard_map/ppermute | solution.py:158
  199.2 18.9 %collective-permute-start.16 = (bf16[64,1024]{1,0:T(8,128)(2,1)S(1)}, bf16[64,1024]{1,0:T(8,128)(2,1)S(1)}, u32[]{:S(2)}, u32[]{:S(2)}) collective-permute-start(bf16[64,1024]{1,0:T(8,128)(2,1)S(1)} %get-tuple-element.38), channel_id=1, source_target_pairs={{0,16},{8,24},{16,0},{24,8},{1,17},{9,25},{17,1},{25,9},{2,18},{10... | collective-permute-start | bytes 393224 | tf_op jit(solution)/shard_map/ppermute | solution.py:158
  199.6 18.5 %collective-permute-start.15 = (bf16[64,1024]{1,0:T(8,128)(2,1)S(1)}, bf16[64,1024]{1,0:T(8,128)(2,1)S(1)}, u32[]{:S(2)}, u32[]{:S(2)}) collective-permute-start(bf16[64,1024]{1,0:T(8,128)(2,1)S(1)} %get-tuple-element.36), channel_id=1, source_target_pairs={{0,8},{8,16},{16,24},{24,0},{1,9},{9,17},{17,25},{25,1},{2,10},{10... | collective-permute-start | bytes 393224 | tf_op jit(solution)/shard_map/ppermute | solution.py:158
  (39 other events, 372.5 us)

commit v2 on v1

v2 whole, which is shorter than its diff:
```python
import functools

import jax
import jax.numpy as jnp
from jax import lax
from jax.experimental import pallas as pl
from jax.experimental.pallas import tpu as pltpu
from jax.sharding import PartitionSpec as P

F32, BF16 = jnp.float32, jnp.bfloat16
ROWS_BY_ROWS = (((1,), (1,)), ((), ()))
VMEM = 48 << 20


def coefficient_kernel(slot_ref, prob_ref, gate_ref, up_ref, cg_ref, cu_ref, cr_ref):
    rows, slots = slot_ref.shape[0], gate_ref.shape[2]
    width = gate_ref.shape[1]
    column = lax.broadcasted_iota(jnp.int32, (rows, slots), 1)
    for e in range(gate_ref.shape[0]):
        pick = jnp.where(slot_ref[:, e : e + 1] == column, 1.0, 0.0).astype(BF16)
        g = lax.dot_general(pick, gate_ref[e], ROWS_BY_ROWS, preferred_element_type=F32)
        u = lax.dot_general(pick, up_ref[e], ROWS_BY_ROWS, preferred_element_type=F32)
        p = prob_ref[:, e : e + 1]
        sg = 1.0 / (1.0 + jnp.exp(-g))
        silu = g * sg
        span = slice(e * width, (e + 1) * width)
        cg_ref[:, span] = u * sg * (1.0 + g * (1.0 - sg)) * p
        cu_ref[:, span] = silu * p
        cr_ref[:, span] = silu * u


def coefficients(slot, prob, saved_gate, saved_up, tile):
    total, experts = slot.shape
    width = saved_gate.shape[1]
    row = lambda n: pl.BlockSpec((tile, n), lambda i: (i, 0))
    whole = pl.BlockSpec(saved_gate.shape, lambda i: (0, 0, 0))
    return pl.pallas_call(
        coefficient_kernel,
        grid=(total // tile,),
        in_specs=[row(experts), row(experts), whole, whole],
        out_specs=[row(experts * width)] * 3,
        out_shape=[jax.ShapeDtypeStruct((total, experts * width), F32)] * 3,
        compiler_params=pltpu.CompilerParams(vmem_limit_bytes=VMEM),
        name="coefficients",
    )(slot, prob, saved_gate, saved_up)


def rows_of(refs, k):
    parts = [r[:, k].reshape(r.shape[0] * r.shape[2], r.shape[3]) for r in refs]
    return parts[0] if len(parts) == 1 else jnp.concatenate(parts, axis=0)


def products(groups, wd_refs):
    total, at = None, 0
    for refs in groups:
        for k in range(refs[0].shape[1]):
            part = lax.dot_general(
                rows_of(refs, k), wd_refs[at][...], ROWS_BY_ROWS, preferred_element_type=F32
            )
            total = part if total is None else total + part
            at += 1
    return total


def split(refs, sizes):
    out, at = [], 0
    for n in sizes:
        out.append(refs[at : at + n])
        at += n
    return out, refs[at:]


def early_kernel(sizes, pieces, z_ref, *refs):
    groups, refs = split(refs, sizes)
    wd_refs, (h_ref,) = refs[:pieces], refs[pieces:]
    h_ref[...] = products(groups, wd_refs)


def late_kernel(sizes, pieces, width, z_ref, *refs):
    groups, refs = split(refs, sizes)
    wd_refs, refs = refs[:pieces], refs[pieces:]
    h_ref, cg_ref, cu_ref, cr_ref, ag_ref, au_ref, r_ref = refs
    h = h_ref[...] + products(groups, wd_refs)
    ag_ref[...] = (h * cg_ref[...]).astype(BF16)
    au_ref[...] = (h * cu_ref[...]).astype(BF16)
    terms = h * cr_ref[...]
    tile = terms.shape[1]
    unit = pl.program_id(0) * tile + lax.broadcasted_iota(jnp.int32, terms.shape, 1)

    @pl.when(pl.program_id(0) == 0)
    def _():
        r_ref[...] = jnp.zeros_like(r_ref)

    for e in range(r_ref.shape[1]):
        own = (unit >= e * width) & (unit < (e + 1) * width)
        r_ref[:, e : e + 1] += jnp.sum(jnp.where(own, terms, 0.0), axis=1, keepdims=True)


def tile_of(n):
    return 256 if n % 256 == 0 else 128 if n % 128 == 0 else n


def hidden_specs(groups, w_down):
    units = w_down.shape[0]
    tile = tile_of(units)
    operands, specs, weights = [], [], []
    for first, blocks in groups:
        span = blocks[0].shape[3]
        for b in blocks:
            operands.append(b)
            specs.append(pl.BlockSpec(b.shape, lambda n, z: (0, 0, 0, 0)))
        for k in range(blocks[0].shape[1]):
            weights.append(pl.BlockSpec((tile, span), lambda n, z, i=first + k: (n, z[0] ^ i)))
    return operands + [w_down] * len(weights), specs + weights, len(weights), tile


def hidden_early(z, groups, w_down):
    operands, specs, pieces, tile = hidden_specs(groups, w_down)
    units = w_down.shape[0]
    total = sum(b.shape[0] * b.shape[2] for b in groups[0][1])
    return pl.pallas_call(
        functools.partial(early_kernel, [len(b) for _, b in groups], pieces),
        grid_spec=pltpu.PrefetchScalarGridSpec(
            num_scalar_prefetch=1,
            grid=(units // tile,),
            in_specs=specs,
            out_specs=pl.BlockSpec((total, tile), lambda n, z: (0, n)),
        ),
        out_shape=jax.ShapeDtypeStruct((total, units), F32),
        compiler_params=pltpu.CompilerParams(vmem_limit_bytes=VMEM),
        name="hidden_early",
    )(z, *operands)


def hidden_late(z, groups, w_down, early, coefs, experts):
    operands, specs, pieces, tile = hidden_specs(groups, w_down)
    total, units = early.shape
    column = pl.BlockSpec((total, tile), lambda n, z: (0, n))
    return pl.pallas_call(
        functools.partial(late_kernel, [len(b) for _, b in groups], pieces, units // experts),
        grid_spec=pltpu.PrefetchScalarGridSpec(
            num_scalar_prefetch=1,
            grid=(units // tile,),
            in_specs=specs + [column] * 4,
            out_specs=[column, column, pl.BlockSpec((total, experts), lambda n, z: (0, 0))],
        ),
        out_shape=[jax.ShapeDtypeStruct((total, units), BF16)] * 2
        + [jax.ShapeDtypeStruct((total, experts), F32)],
        compiler_params=pltpu.CompilerParams(vmem_limit_bytes=VMEM),
        name="hidden_late",
    )(z, *operands, early, *coefs)


def expand_kernel(places, z_ref, ag_ref, au_ref, wg_ref, wu_ref, *outs):
    rows, width = outs[0].shape[2:]
    tile = tile_of(width)
    for at in range(0, width, tile):
        span = slice(at, at + tile)
        y = jnp.dot(ag_ref[...], wg_ref[:, span], preferred_element_type=F32)
        y = (y + jnp.dot(au_ref[...], wu_ref[:, span], preferred_element_type=F32)).astype(BF16)
        for i, (out, j) in enumerate(places):
            outs[out][j, 0, :, span] = y[i * rows : (i + 1) * rows]


def expand(z, first, pieces, ag, au, w_gate, w_up, sections, rows, places):
    total, units = ag.shape
    span = w_gate.shape[1] // sections
    half = max(span // 2, 128)
    per = span // half
    counts = [sum(1 for o, _ in places if o == n) for n in range(1 + max(o for o, _ in places))]
    whole = pl.BlockSpec((total, units), lambda k, j, z: (0, 0))
    weight = pl.BlockSpec((units, half), lambda k, j, z: (0, (z[0] ^ (first + k)) * per + j))
    return pl.pallas_call(
        functools.partial(expand_kernel, places),
        grid_spec=pltpu.PrefetchScalarGridSpec(
            num_scalar_prefetch=1,
            grid=(pieces, per),
            in_specs=[whole, whole, weight, weight],
            out_specs=[pl.BlockSpec((n, 1, rows, half), lambda k, j, z: (0, k, 0, j)) for n in counts],
        ),
        out_shape=[jax.ShapeDtypeStruct((n, pieces, rows, span), BF16) for n in counts],
        compiler_params=pltpu.CompilerParams(vmem_limit_bytes=VMEM),
        name="expand",
    )(z, ag, au, w_gate, w_up)


def add(*terms):
    return functools.reduce(lambda a, b: a + b, [t.astype(F32) for t in terms])


def after(x, *others):
    return lax.optimization_barrier((x, *others))[0]


def local(grad_out, probs, expert_ids, w_gate, w_up, w_down, saved_gate, saved_up):
    groups, sections = lax.axis_size("expert"), lax.axis_size("section")
    me, z = lax.axis_index("expert"), lax.axis_index("section")
    experts, units, features = w_gate.shape
    slots = saved_gate.shape[2]
    capacity = slots // groups
    tokens, topk = expert_ids.shape
    square = groups == 8

    core = me % 2
    near = jnp.where(core == 0, 2, 4)
    far = 6 - near

    def swap(x, even, odd):
        return lax.ppermute(x, "expert", [(i, i ^ (even, odd)[i % 2]) for i in range(groups)])

    def across(x, by):
        return lax.ppermute(x, "section", [(i, i ^ by) for i in range(sections)])

    if square:
        owners = jnp.stack([me, me ^ 1, me ^ near, me ^ near ^ 1, me ^ 1 ^ far, me ^ far, me ^ 6, me ^ 7])
        places = ((0, 0), (1, 0), (0, 1), (0, 2), (1, 1), (1, 2), (0, 3), (1, 3))
    else:
        owners = jnp.arange(groups)
        places = tuple((0, i) for i in range(groups))

    def gather(own):
        if not square:
            return [lax.all_gather(own, "expert", axis=0, tiled=True)]
        pair = jnp.concatenate([own, swap(own, 1, 1)])
        first = swap(pair, 2, 4)
        second = swap(first[:1], 4, 2)
        return [pair, first, swap(first, 1, 1), second, swap(second, 1, 1)]

    start = z.astype(jnp.int32).reshape(1)
    piece = grad_out[None]
    received = [piece] + [across(piece, i) for i in (1, 2) if i < sections]
    for i in range(3, sections):
        received.append(across(after(piece, received[i - 2]), i))
    lots = ((0, 1), (1, 3), (3, sections))
    lots = [(a, gather(jnp.stack(received[a:b], axis=1))) for a, b in lots if a < b]

    routing = jnp.concatenate([expert_ids.T.astype(F32), probs.T], axis=0)[None]
    if square:
        for bit in (2, 4, 1):
            routing = jnp.concatenate([routing, swap(routing, bit, bit)], axis=0)
        even = routing[jnp.array([0, 4, 1, 5, 6, 2, 3, 7])]
        odd = routing[jnp.array([0, 4, 2, 6, 5, 1, 3, 7])]
        routing = jnp.where(core == 0, even, odd)
    else:
        routing = lax.all_gather(routing, "expert", axis=0, tiled=True)
    mine = (me * experts + jnp.arange(experts)).astype(F32)
    chosen = routing[:, None, :topk] == mine[None, :, None, None]
    weight = jnp.sum(jnp.where(chosen, routing[:, None, topk:], 0.0), axis=2)
    named = jnp.any(chosen, axis=2)
    earlier = jnp.arange(tokens)[:, None] < jnp.arange(tokens)[None, :]
    position = lax.dot_general(
        named.astype(BF16), earlier.astype(BF16), (((2,), (0,)), ((), ())), preferred_element_type=F32
    ).astype(jnp.int32)
    slot = jnp.where(named, owners[:, None, None] * capacity + position, -1)
    by_token = lambda x: x.transpose(0, 2, 1).reshape(groups * tokens, experts)
    coefs = coefficients(by_token(slot), by_token(weight), saved_gate, saved_up, min(512, groups * tokens))

    flat = lambda w: w.reshape(experts * units, features)
    early = hidden_early(start, lots[:2], flat(w_down))
    ag, au, router = hidden_late(start, lots[2:], flat(w_down), early, coefs, experts)

    def reduce(outs):
        if not square:
            return lax.psum_scatter(outs[0], "expert", scatter_dimension=0, tiled=True)[0]
        kept = add(outs[0], swap(outs[1], 1, 1)).astype(BF16)
        diagonal = swap(kept[3], 4, 2)
        sent = jnp.stack([add(kept[1], diagonal).astype(BF16), kept[2]])
        received = swap(sent, 2, 4)
        return add(kept[0], received[0], swap(received[1], 1, 1)).astype(BF16)

    parts = []
    for a, b in ((3, sections), (1, 3), (0, 1)):
        outs = expand(start, a, b - a, ag, au, flat(w_gate), flat(w_up), sections, tokens, places)
        sums = reduce(outs)
        parts += [sums[i - a] if i == 0 else across(sums[i - a], i) for i in range(a, b)]
    grad_in = add(*parts).astype(BF16)

    router = router.reshape(groups, tokens, experts)
    if square:
        for bit in range(sections.bit_length() - 1):
            router = router + across(router, 1 << bit)
        even = router[jnp.array([0, 1, 2, 3, 5, 4, 6, 7])]
        odd = router[jnp.array([0, 1, 5, 4, 2, 3, 6, 7])]
        router = jnp.where(core == 0, even, odd)
        router = router.transpose(0, 2, 1)
        gathered = router[None]
        for bit in (1, 2, 4):
            gathered = jnp.concatenate([gathered, swap(gathered, bit, bit)], axis=0)
        back = jnp.stack([gathered[q, q] for q in range(groups)])
        source = me ^ jnp.arange(groups)
    else:
        router = lax.psum(router, "section").transpose(0, 2, 1)
        back = lax.all_to_all(router, "expert", split_axis=0, concat_axis=0)
        source = jnp.arange(groups)
    number = (source[:, None] * experts + jnp.arange(experts)).reshape(-1)
    back = back.reshape(groups * experts, tokens)
    match = expert_ids[None] == number[:, None, None]
    grad_probs = jnp.sum(jnp.where(match, back[:, :, None], 0.0), axis=0).astype(BF16)
    return (grad_in, grad_probs)


def solution(mesh):
    placed = (
        P("expert", "section"),
        P("expert", None),
        P("expert", None),
        P("expert", "section", None),
        P("expert", "section", None),
        P("expert", "section", None),
        P("expert", "section", None),
        P("expert", "section", None),
    )
    return jax.shard_map(
        local,
        mesh=mesh,
        in_specs=placed,
        out_specs=(P("expert", "section"), P("expert", None)),
        check_vma=False,
    )
```

time: 219 us -> 205 us (0.936)
  starting transfers between devices: 51.6 us -> 36.8 us
  local copies, waits for them, and re-layouts: 21.1 us -> 15.9 us
  Pallas kernels: 40.2 us -> 45.3 us
    ppermute x14 -> x8, starting transfers between devices: 31.2 us -> 18.7 us  [across(): return lax.ppermute(x, 'section', [(i, i ^ by) for i in range(sections)])]
    ppermute x14 -> x8, waiting for transfers between devices: 32.9 us -> 41.3 us  [across(): return lax.ppermute(x, 'section', [(i, i ^ by) for i in range(sections)])]
    ppermute x24 -> x33, waiting for transfers between devices: 63.3 us -> 55.5 us  [swap(): lax.ppermute(x, 'expert', [(i, i ^ (even, odd)[i % 2]) for i in range(gro...]
    unnamed x57 -> x53, local copies, waits for them, and re-layouts: 11.8 us -> 7.25 us
    pallas_call x4 -> x5, Pallas kernels: 36.1 us -> 39.4 us  [the longest x3 22.1 us: expand(): pl.pallas_call(functools.partial(expand_kernel, places), grid_spec=pltpu....]
    ppermute x24 -> x33, starting transfers between devices: 20.4 us -> 18 us  [swap(): lax.ppermute(x, 'expert', [(i, i ^ (even, odd)[i % 2]) for i in range(gro...]
    convert_element_type x6 -> x5, other arithmetic: 5.83 us -> 5.62 us  [the longest x3 4.39 us: reduce(): kept = add(outs[0], swap(outs[1], 1, 1)).astype(BF16)]
  transfers between devices with their start and end apart: 38 -> 41, of which waited for: 20 -> 18; matrix products, arithmetic and copies ran while one was open for 7% -> 7% of each run, Pallas kernels for 18% -> 18%
where the time goes in v2:
time: 205 us
  waiting for transfers between devices  96.8 us (47%)
  Pallas kernels  45.3 us (22%)
  starting transfers between devices  36.8 us (18%)
  local copies, waits for them, and re-layouts  15.9 us (8%)
  other arithmetic  8.51 us (4%)
    ppermute x33, waiting for transfers between devices, swap(): lax.ppermute(x, 'expert', [(i, i ^ (even, odd)[i % 2]) for i in range(gro...  55.5 us
    ppermute x8, waiting for transfers between devices, across(): return lax.ppermute(x, 'section', [(i, i ^ by) for i in range(sections)])  41.3 us
    pallas_call x3, Pallas kernels, expand(): pl.pallas_call(functools.partial(expand_kernel, places), grid_spec=pltpu....  22.1 us
    ppermute x8, starting transfers between devices, across(): return lax.ppermute(x, 'section', [(i, i ^ by) for i in range(sections)])  18.7 us
    ppermute x33, starting transfers between devices, swap(): lax.ppermute(x, 'expert', [(i, i ^ (even, odd)[i % 2]) for i in range(gro...  18 us
    pallas_call x1, Pallas kernels, hidden_early(): pl.pallas_call(functools.partial(early_kernel, [len(b) for _, b in groups...  9.18 us
    pallas_call x1, Pallas kernels, hidden_late(): pl.pallas_call(functools.partial(late_kernel, [len(b) for _, b in groups]...  8.14 us
    unnamed x53, local copies, waits for them, and re-layouts  7.25 us
  transfers between devices with their start and end apart: 41, of which 18 were waited for; matrix products, arithmetic and copies ran while one was open for 7% of the time, Pallas kernels for 18%

profile of v2, /device:TPU:0, one launch (start us, length us, event | category | flops | bytes accessed | tf_op | source)
XLA Modules:
  0.0 204.6 jit_solution(16576365293056082503)
XLA Ops:
  0.7 3.1 %collective-permute-start = (bf16[1,128,1024]{2,1,0:T(8,128)(2,1)}, bf16[1,128,1024]{2,1,0:T(8,128)(2,1)S(1)}, u32[]{:S(2)}, u32[]{:S(2)}) collective-permute-start(bf16[1,128,1024]{2,1,0:T(8,128)(2,1)} %bitcast.147), channel_id=1, source_target_pairs={{0,8},{8,0},{16,24},{24,16},{1,9},{9,1},{17,25},{25,17},{2,10},{10... | collective-permute-start | bytes 786440 | tf_op jit(solution)/shard_map/ppermute | solution.py:212
  3.8 2.6 %collective-permute-start.12 = (bf16[1,128,1024]{2,1,0:T(8,128)(2,1)}, bf16[1,128,1024]{2,1,0:T(8,128)(2,1)S(1)}, u32[]{:S(2)}, u32[]{:S(2)}) collective-permute-start(bf16[1,128,1024]{2,1,0:T(8,128)(2,1)} %bitcast.148), channel_id=1, source_target_pairs={{0,16},{8,24},{16,0},{24,8},{1,17},{9,25},{17,1},{25,9},{2,18},{10... | collective-permute-start | bytes 786440 | tf_op jit(solution)/shard_map/ppermute | solution.py:212
  6.4 9.4 %collective-permute-done = bf16[1,128,1024]{2,1,0:T(8,128)(2,1)S(1)} collective-permute-done((bf16[1,128,1024]{2,1,0:T(8,128)(2,1)}, bf16[1,128,1024]{2,1,0:T(8,128)(2,1)S(1)}, u32[]{:S(2)}, u32[]{:S(2)}) %collective-permute-start) | collective-permute-done | bytes 262176 | tf_op jit(solution)/shard_map/ppermute | solution.py:212
  15.8 2.5 %collective-permute-done.12 = bf16[1,128,1024]{2,1,0:T(8,128)(2,1)S(1)} collective-permute-done((bf16[1,128,1024]{2,1,0:T(8,128)(2,1)}, bf16[1,128,1024]{2,1,0:T(8,128)(2,1)S(1)}, u32[]{:S(2)}, u32[]{:S(2)}) %collective-permute-start.12) | collective-permute-done | bytes 262176 | tf_op jit(solution)/shard_map/ppermute | solution.py:212
  22.6 2.5 %collective-permute-start.1 = (bf16[1,128,1024]{2,1,0:T(8,128)(2,1)S(1)}, bf16[1,128,1024]{2,1,0:T(8,128)(2,1)S(1)}, u32[]{:S(2)}, u32[]{:S(2)}) collective-permute-start(bf16[1,128,1024]{2,1,0:T(8,128)(2,1)S(1)} %bitcast.150), channel_id=1, source_target_pairs={{0,24},{8,16},{16,8},{24,0},{1,25},{9,17},{17,9},{25,1},{2,26},{10... | collective-permute-start | bytes 786440 | tf_op jit(solution)/shard_map/ppermute | solution.py:212
  25.2 8.1 %collective-permute-done.1 = bf16[1,128,1024]{2,1,0:T(8,128)(2,1)S(1)} collective-permute-done((bf16[1,128,1024]{2,1,0:T(8,128)(2,1)S(1)}, bf16[1,128,1024]{2,1,0:T(8,128)(2,1)S(1)}, u32[]{:S(2)}, u32[]{:S(2)}) %collective-permute-start.1) | collective-permute-done | bytes 262176 | tf_op jit(solution)/shard_map/ppermute | solution.py:212
  47.8 8.3 %collective-permute-done.3.refs_1_ = bf16[2,1,128,1024]{3,2,1,0:T(8,128)(2,1)} collective-permute-done((bf16[2,1,128,1024]{3,2,1,0:T(8,128)(2,1)S(1)}, bf16[2,1,128,1024]{3,2,1,0:T(8,128)(2,1)}, u32[]{:S(2)}, u32[]{:S(2)}) %collective-permute-start.3) | collective-permute-done | bytes 524320 | tf_op jit(solution)/shard_map/ppermute | solution.py:209
  58.7 4.8 %collective-permute-done.5.refs_3_ = bf16[1,1,128,1024]{3,2,1,0:T(8,128)(2,1)S(1)} collective-permute-done((bf16[1,1,128,1024]{3,2,1,0:T(8,128)(2,1)S(1)}, bf16[1,1,128,1024]{3,2,1,0:T(8,128)(2,1)S(1)}, u32[]{:S(2)}, u32[]{:S(2)}) %collective-permute-start.5) | collective-permute-done | bytes 262176 | tf_op jit(solution)/shard_map/ppermute | solution.py:209
  68.6 5.9 %coefficients.1 = (f32[1024,768]{1,0:T(8,128)}, f32[1024,768]{1,0:T(8,128)}, f32[1024,768]{1,0:T(8,128)}) custom-call(s32[1024,2]{1,0:T(8,128)S(1)} %bitcast.130, f32[1024,2]{1,0:T(8,128)S(1)} %bitcast.131, bf16[2,384,768]{2,1,0:T(8,128)(2,1)S(1)} %copy-done.7, bf16[2,384,768]{2,1,0:T(8,128)(2,1)S(1)} %copy-done.8), custom_call_target="tpu_custom_call" | custom-call | tf_op jit(solution)/shard_map/coefficients/pallas_call | solution.py:37
  74.6 9.2 %hidden_early.1.refs_6_ = f32[1024,768]{1,0:T(8,128)} custom-call(s32[1]{0:T(128)} %bitcast.z_ref, bf16[2,1,128,1024]{3,2,1,0:T(8,128)(2,1)S(1)} %copy-done.6, bf16[2,1,128,1024]{3,2,1,0:T(8,128)(2,1)} %collective-permute-done.8.refs_1_, bf16[2,1,128,1024]{3,2,1,0:T(8,128)(2,1)S(1)} %copy-done.15, bf16[1,1,128,1024]{3,2,1,0:T(8,128)(2,1)} %collective-permute-done.10.refs_3_, ...), custom_call_target="tpu_custom_call" | custom-call | tf_op jit(solution)/shard_map/hidden_early/pallas_call | solution.py:121
  83.8 8.1 %hidden_late.1 = (bf16[1024,768]{1,0:T(8,128)(2,1)S(1)}, bf16[1024,768]{1,0:T(8,128)(2,1)S(1)}, f32[1024,2]{1,0:T(8,128)S(1)}) custom-call(s32[1]{0:T(128)} %bitcast.z_ref, bf16[2,1,128,1024]{3,2,1,0:T(8,128)(2,1)S(1)} %copy-done.3, bf16[2,1,128,1024]{3,2,1,0:T(8,128)(2,1)} %collective-permute-done.3.refs_1_, ...), custom_call_target="tpu_custom_call" | custom-call | tf_op jit(solution)/shard_map/hidden_late/pallas_call | solution.py:139
  94.0 4.2 %collective-permute-start.36 = (f32[8,128,2]{1,2,0:T(2,128)S(1)}, f32[8,128,2]{1,2,0:T(2,128)S(1)}, u32[]{:S(2)}, u32[]{:S(2)}) collective-permute-start(f32[8,128,2]{1,2,0:T(2,128)S(1)} %copy.27), channel_id=1, source_target_pairs={{0,8},{8,0},{16,24},{24,16},{1,9},{9,1},{17,25},{25,17},{2,10},{10... | collective-permute-start | bytes 24584 | tf_op jit(solution)/shard_map/ppermute | solution.py:212
  101.8 9.5 %expand.4 = (bf16[4,2,128,1024]{3,2,1,0:T(8,128)(2,1)S(1)}, bf16[4,2,128,1024]{3,2,1,0:T(8,128)(2,1)}) custom-call(s32[1]{0:T(128)} %bitcast.z_ref, bf16[1024,768]{1,0:T(8,128)(2,1)S(1)} %get-tuple-element.19.ag_ref, bf16[1024,768]{1,0:T(8,128)(2,1)S(1)} %get-tuple-element.20.au_ref, bf16[768,4096]{1,0:T(8,128)(2,1)} %bitcast.137, bf16[768,4096]{1,0:T(8,128)(2,1)} %bitcast.140), custom_call_target="tpu_custom_call" | custom-call | tf_op jit(solution)/shard_map/expand/pallas_call | solution.py:173
  111.3 6.6 %expand.3 = (bf16[4,1,128,1024]{3,2,1,0:T(8,128)(2,1)S(1)}, bf16[4,1,128,1024]{3,2,1,0:T(8,128)(2,1)}) custom-call(s32[1]{0:T(128)} %bitcast.z_ref, bf16[1024,768]{1,0:T(8,128)(2,1)S(1)} %get-tuple-element.19.ag_ref, bf16[1024,768]{1,0:T(8,128)(2,1)S(1)} %get-tuple-element.20.au_ref, bf16[768,4096]{1,0:T(8,128)(2,1)} %bitcast.138, bf16[768,4096]{1,0:T(8,128)(2,1)} %bitcast.141), custom_call_target="tpu_custom_call" | custom-call | tf_op jit(solution)/shard_map/expand/pallas_call | solution.py:173
  118.9 5.9 %expand.5 = (bf16[4,1,128,1024]{3,2,1,0:T(8,128)(2,1)S(1)}, bf16[4,1,128,1024]{3,2,1,0:T(8,128)(2,1)}) custom-call(s32[1]{0:T(128)} %bitcast.z_ref, bf16[1024,768]{1,0:T(8,128)(2,1)S(1)} %get-tuple-element.19.ag_ref, bf16[1024,768]{1,0:T(8,128)(2,1)S(1)} %get-tuple-element.20.au_ref, bf16[768,4096]{1,0:T(8,128)(2,1)} %bitcast.139, bf16[768,4096]{1,0:T(8,128)(2,1)} %bitcast.142), custom_call_target="tpu_custom_call" | custom-call | tf_op jit(solution)/shard_map/expand/pallas_call | solution.py:173
  130.7 3.2 %collective-permute-done.39 = f32[2,8,2,128]{3,2,1,0:T(2,128)S(1)} collective-permute-done((f32[2,8,2,128]{3,2,1,0:T(2,128)S(1)}, f32[2,8,2,128]{3,2,1,0:T(2,128)S(1)}, u32[]{:S(2)}, u32[]{:S(2)}) %collective-permute-start.39) | collective-permute-done | bytes 16416 | tf_op jit(solution)/shard_map/ppermute | solution.py:209
  134.0 3.9 %collective-permute-done.40 = f32[4,8,2,128]{3,2,1,0:T(2,128)S(1)} collective-permute-done((f32[4,8,2,128]{3,2,1,0:T(2,128)S(1)}, f32[4,8,2,128]{3,2,1,0:T(2,128)S(1)}, u32[]{:S(2)}, u32[]{:S(2)}) %collective-permute-start.40) | collective-permute-done | bytes 32800 | tf_op jit(solution)/shard_map/ppermute | solution.py:209
  145.8 6.0 %collective-permute-done.27 = bf16[2,128,1024]{2,1,0:T(8,128)(2,1)S(1)} collective-permute-done((bf16[2,128,1024]{2,1,0:T(8,128)(2,1)S(1)}, bf16[2,128,1024]{2,1,0:T(8,128)(2,1)S(1)}, u32[]{:S(2)}, u32[]{:S(2)}) %collective-permute-start.27) | collective-permute-done | bytes 524320 | tf_op jit(solution)/shard_map/ppermute | solution.py:209
  154.4 3.0 %collective-permute-done.33 = bf16[1,128,1024]{2,1,0:T(8,128)(2,1)S(1)} collective-permute-done((bf16[1,128,1024]{2,1,0:T(8,128)(2,1)S(1)}, bf16[1,128,1024]{2,1,0:T(8,128)(2,1)S(1)}, u32[]{:S(2)}, u32[]{:S(2)}) %collective-permute-start.33) | collective-permute-done | bytes 262176 | tf_op jit(solution)/shard_map/ppermute | solution.py:209
  158.1 14.4 %collective-permute-done.23 = bf16[2,1,128,1024]{3,2,1,0:T(8,128)(2,1)S(1)} collective-permute-done((bf16[2,1,128,1024]{3,2,1,0:T(8,128)(2,1)S(1)}, bf16[2,1,128,1024]{3,2,1,0:T(8,128)(2,1)S(1)}, u32[]{:S(2)}, u32[]{:S(2)}) %collective-permute-start.23) | collective-permute-done | bytes 524320 | tf_op jit(solution)/shard_map/ppermute | solution.py:209
  173.3 4.9 %collective-permute-done.34 = bf16[2,1,128,1024]{3,2,1,0:T(8,128)(2,1)S(1)} collective-permute-done((bf16[2,1,128,1024]{3,2,1,0:T(8,128)(2,1)S(1)}, bf16[2,1,128,1024]{3,2,1,0:T(8,128)(2,1)S(1)}, u32[]{:S(2)}, u32[]{:S(2)}) %collective-permute-start.34) | collective-permute-done | bytes 524320 | tf_op jit(solution)/shard_map/ppermute | solution.py:209
  178.4 2.5 %collective-permute-start.25 = (bf16[128,1024]{1,0:T(8,128)(2,1)S(1)}, bf16[128,1024]{1,0:T(8,128)(2,1)S(1)}, u32[]{:S(2)}, u32[]{:S(2)}) collective-permute-start(bf16[128,1024]{1,0:T(8,128)(2,1)S(1)} %fusion.11), channel_id=1, source_target_pairs={{0,24},{8,16},{16,8},{24,0},{1,25},{9,17},{17,9},{25,1},{2,26},{10... | collective-permute-start | bytes 786440 | tf_op jit(solution)/shard_map/ppermute | solution.py:212
  183.9 5.6 %collective-permute-done.25 = bf16[128,1024]{1,0:T(8,128)(2,1)S(1)} collective-permute-done((bf16[128,1024]{1,0:T(8,128)(2,1)S(1)}, bf16[128,1024]{1,0:T(8,128)(2,1)S(1)}, u32[]{:S(2)}, u32[]{:S(2)}) %collective-permute-start.25) | collective-permute-done | bytes 262176 | tf_op jit(solution)/shard_map/ppermute | solution.py:212
  189.5 14.1 %collective-permute-done.31 = bf16[128,1024]{1,0:T(8,128)(2,1)S(1)} collective-permute-done((bf16[128,1024]{1,0:T(8,128)(2,1)S(1)}, bf16[128,1024]{1,0:T(8,128)(2,1)S(1)}, u32[]{:S(2)}, u32[]{:S(2)}) %collective-permute-start.31) | collective-permute-done | bytes 262176 | tf_op jit(solution)/shard_map/ppermute | solution.py:212
  (175 shorter events, 55.0 us)
Async XLA Ops:
  0.7 15.1 %collective-permute-start = (bf16[1,128,1024]{2,1,0:T(8,128)(2,1)}, bf16[1,128,1024]{2,1,0:T(8,128)(2,1)S(1)}, u32[]{:S(2)}, u32[]{:S(2)}) collective-permute-start(bf16[1,128,1024]{2,1,0:T(8,128)(2,1)} %bitcast.147), channel_id=1, source_target_pairs={{0,8},{8,0},{16,24},{24,16},{1,9},{9,1},{17,25},{25,17},{2,10},{10... | collective-permute-start | bytes 786440 | tf_op jit(solution)/shard_map/ppermute | solution.py:212
  3.8 14.6 %collective-permute-start.12 = (bf16[1,128,1024]{2,1,0:T(8,128)(2,1)}, bf16[1,128,1024]{2,1,0:T(8,128)(2,1)S(1)}, u32[]{:S(2)}, u32[]{:S(2)}) collective-permute-start(bf16[1,128,1024]{2,1,0:T(8,128)(2,1)} %bitcast.148), channel_id=1, source_target_pairs={{0,16},{8,24},{16,0},{24,8},{1,17},{9,25},{17,1},{25,9},{2,18},{10... | collective-permute-start | bytes 786440 | tf_op jit(solution)/shard_map/ppermute | solution.py:212
  18.5 14.9 %collective-permute-start.7 = (bf16[1,1,128,1024]{3,2,1,0:T(8,128)(2,1)}, bf16[1,1,128,1024]{3,2,1,0:T(8,128)(2,1)S(1)}, u32[]{:S(2)}, u32[]{:S(2)}) collective-permute-start(bf16[1,1,128,1024]{3,2,1,0:T(8,128)(2,1)} %bitcast.149), channel_id=1, source_target_pairs={{0,1},{1,0},{2,3},{3,2},{4,5},{5,4},{6,7},{7,6},{8,9},{9,8},{10,11... | collective-permute-start | bytes 786440 | tf_op jit(solution)/shard_map/ppermute | solution.py:209
  20.5 19.1 %collective-permute-start.14 = (bf16[2,2,128,1024]{3,2,1,0:T(8,128)(2,1)S(1)}, bf16[2,2,128,1024]{3,2,1,0:T(8,128)(2,1)S(1)}, u32[]{:S(2)}, u32[]{:S(2)}) collective-permute-start(bf16[2,2,128,1024]{3,2,1,0:T(8,128)(2,1)S(1)} %pad_maximum_fusion.refs_5_), channel_id=1, source_target_pairs={{0,2},{1,5},{2,0},{3,7},{4,6},{5,1},{6,4},{7,3},{8,10},{9,13},{10,... | collective-permute-start | bytes 3145736 | tf_op jit(solution)/shard_map/ppermute | solution.py:209
  22.0 13.5 %collective-permute-start.18 = (f32[1,16,128]{2,1,0:T(8,128)S(1)}, f32[1,16,128]{2,1,0:T(8,128)S(1)}, u32[]{:S(2)}, u32[]{:S(2)}) collective-permute-start(f32[1,16,128]{2,1,0:T(8,128)S(1)} %maximum_bitcast_fusion), channel_id=1, source_target_pairs={{0,2},{1,3},{2,0},{3,1},{4,6},{5,7},{6,4},{7,5},{8,10},{9,11},{10,... | collective-permute-start | bytes 24584 | tf_op jit(solution)/shard_map/ppermute | solution.py:209
  33.4 11.5 %collective-permute-start.8 = (bf16[2,1,128,1024]{3,2,1,0:T(8,128)(2,1)S(1)}, bf16[2,1,128,1024]{3,2,1,0:T(8,128)(2,1)}, u32[]{:S(2)}, u32[]{:S(2)}) collective-permute-start(bf16[2,1,128,1024]{3,2,1,0:T(8,128)(2,1)S(1)} %pad_maximum_fusion.3.refs_0_), channel_id=1, source_target_pairs={{0,2},{1,5},{2,0},{3,7},{4,6},{5,1},{6,4},{7,3},{8,10},{9,13},{10,... | collective-permute-start | bytes 1572872 | tf_op jit(solution)/shard_map/ppermute | solution.py:209
  38.0 18.1 %collective-permute-start.3 = (bf16[2,1,128,1024]{3,2,1,0:T(8,128)(2,1)S(1)}, bf16[2,1,128,1024]{3,2,1,0:T(8,128)(2,1)}, u32[]{:S(2)}, u32[]{:S(2)}) collective-permute-start(bf16[2,1,128,1024]{3,2,1,0:T(8,128)(2,1)S(1)} %pad_maximum_fusion.2.refs_0_), channel_id=1, source_target_pairs={{0,2},{1,5},{2,0},{3,7},{4,6},{5,1},{6,4},{7,3},{8,10},{9,13},{10,... | collective-permute-start | bytes 1572872 | tf_op jit(solution)/shard_map/ppermute | solution.py:209
  40.4 16.9 %collective-permute-start.16 = (bf16[1,2,128,1024]{3,2,1,0:T(8,128)(2,1)}, bf16[1,2,128,1024]{3,2,1,0:T(8,128)(2,1)}, u32[]{:S(2)}, u32[]{:S(2)}) collective-permute-start(bf16[1,2,128,1024]{3,2,1,0:T(8,128)(2,1)} %slice.142), channel_id=1, source_target_pairs={{0,4},{1,3},{2,6},{3,1},{4,0},{5,7},{6,2},{7,5},{8,12},{9,11},{10,... | collective-permute-start | bytes 1572872 | tf_op jit(solution)/shard_map/ppermute | solution.py:209
  42.8 31.8 %collective-permute-start.15 = (bf16[2,2,128,1024]{3,2,1,0:T(8,128)(2,1)S(1)}, bf16[2,2,128,1024]{3,2,1,0:T(8,128)(2,1)}, u32[]{:S(2)}, u32[]{:S(2)}) collective-permute-start(bf16[2,2,128,1024]{3,2,1,0:T(8,128)(2,1)S(1)} %collective-permute-done.14.refs_6_), channel_id=1, source_target_pairs={{0,1},{1,0},{2,3},{3,2},{4,5},{5,4},{6,7},{7,6},{8,9},{9,8},{10,11... | collective-permute-start | bytes 3145736 | tf_op jit(solution)/shard_map/ppermute | solution.py:209
  57.2 26.6 %collective-permute-start.4 = (bf16[2,1,128,1024]{3,2,1,0:T(8,128)(2,1)}, bf16[2,1,128,1024]{3,2,1,0:T(8,128)(2,1)}, u32[]{:S(2)}, u32[]{:S(2)}) collective-permute-start(bf16[2,1,128,1024]{3,2,1,0:T(8,128)(2,1)} %collective-permute-done.3.refs_1_), channel_id=1, source_target_pairs={{0,1},{1,0},{2,3},{3,2},{4,5},{5,4},{6,7},{7,6},{8,9},{9,8},{10,11... | collective-permute-start | bytes 1572872 | tf_op jit(solution)/shard_map/ppermute | solution.py:209
  57.2 17.3 %collective-permute-start.17 = (bf16[1,2,128,1024]{3,2,1,0:T(8,128)(2,1)}, bf16[1,2,128,1024]{3,2,1,0:T(8,128)(2,1)}, u32[]{:S(2)}, u32[]{:S(2)}) collective-permute-start(bf16[1,2,128,1024]{3,2,1,0:T(8,128)(2,1)} %collective-permute-done.16.refs_8_), channel_id=1, source_target_pairs={{0,1},{1,0},{2,3},{3,2},{4,5},{5,4},{6,7},{7,6},{8,9},{9,8},{10,11... | collective-permute-start | bytes 1572872 | tf_op jit(solution)/shard_map/ppermute | solution.py:209
  58.7 15.9 %collective-permute-start.11 = (bf16[1,1,128,1024]{3,2,1,0:T(8,128)(2,1)}, bf16[1,1,128,1024]{3,2,1,0:T(8,128)(2,1)}, u32[]{:S(2)}, u32[]{:S(2)}) collective-permute-start(bf16[1,1,128,1024]{3,2,1,0:T(8,128)(2,1)} %collective-permute-done.10.refs_3_), channel_id=1, source_target_pairs={{0,1},{1,0},{2,3},{3,2},{4,5},{5,4},{6,7},{7,6},{8,9},{9,8},{10,11... | collective-permute-start | bytes 786440 | tf_op jit(solution)/shard_map/ppermute | solution.py:209
  63.5 20.2 %collective-permute-start.6 = (bf16[1,1,128,1024]{3,2,1,0:T(8,128)(2,1)S(1)}, bf16[1,1,128,1024]{3,2,1,0:T(8,128)(2,1)}, u32[]{:S(2)}, u32[]{:S(2)}) collective-permute-start(bf16[1,1,128,1024]{3,2,1,0:T(8,128)(2,1)S(1)} %collective-permute-done.5.refs_3_), channel_id=1, source_target_pairs={{0,1},{1,0},{2,3},{3,2},{4,5},{5,4},{6,7},{7,6},{8,9},{9,8},{10,11... | collective-permute-start | bytes 786440 | tf_op jit(solution)/shard_map/ppermute | solution.py:209
  99.8 26.5 %collective-permute-start.37 = (f32[8,128,2]{1,2,0:T(2,128)S(1)}, f32[8,128,2]{1,2,0:T(2,128)S(1)}, u32[]{:S(2)}, u32[]{:S(2)}) collective-permute-start(f32[8,128,2]{1,2,0:T(2,128)S(1)} %add.161), channel_id=1, source_target_pairs={{0,16},{8,24},{16,0},{24,8},{1,17},{9,25},{17,1},{25,9},{2,18},{10... | collective-permute-start | bytes 24584 | tf_op jit(solution)/shard_map/ppermute | solution.py:212
  125.8 14.0 %collective-permute-start.26 = (bf16[4,2,128,1024]{3,2,1,0:T(8,128)(2,1)}, bf16[4,2,128,1024]{3,2,1,0:T(8,128)(2,1)S(1)}, u32[]{:S(2)}, u32[]{:S(2)}) collective-permute-start(bf16[4,2,128,1024]{3,2,1,0:T(8,128)(2,1)} %get-tuple-element.24), channel_id=1, source_target_pairs={{0,1},{1,0},{2,3},{3,2},{4,5},{5,4},{6,7},{7,6},{8,9},{9,8},{10,11... | collective-permute-start | bytes 6291464 | tf_op jit(solution)/shard_map/ppermute | solution.py:209
  125.8 12.1 %collective-permute-start.21 = (bf16[4,1,128,1024]{3,2,1,0:T(8,128)(2,1)}, bf16[4,1,128,1024]{3,2,1,0:T(8,128)(2,1)}, u32[]{:S(2)}, u32[]{:S(2)}) collective-permute-start(bf16[4,1,128,1024]{3,2,1,0:T(8,128)(2,1)} %get-tuple-element.22), channel_id=1, source_target_pairs={{0,1},{1,0},{2,3},{3,2},{4,5},{5,4},{6,7},{7,6},{8,9},{9,8},{10,11... | collective-permute-start | bytes 3145736 | tf_op jit(solution)/shard_map/ppermute | solution.py:209
  126.3 16.6 %collective-permute-start.32 = (bf16[4,1,128,1024]{3,2,1,0:T(8,128)(2,1)}, bf16[4,1,128,1024]{3,2,1,0:T(8,128)(2,1)}, u32[]{:S(2)}, u32[]{:S(2)}) collective-permute-start(bf16[4,1,128,1024]{3,2,1,0:T(8,128)(2,1)} %get-tuple-element.26), channel_id=1, source_target_pairs={{0,1},{1,0},{2,3},{3,2},{4,5},{5,4},{6,7},{7,6},{8,9},{9,8},{10,11... | collective-permute-start | bytes 3145736 | tf_op jit(solution)/shard_map/ppermute | solution.py:209
  139.7 13.0 %collective-permute-start.22 = (bf16[1,128,1024]{2,1,0:T(8,128)(2,1)S(1)}, bf16[1,128,1024]{2,1,0:T(8,128)(2,1)S(1)}, u32[]{:S(2)}, u32[]{:S(2)}) collective-permute-start(bf16[1,128,1024]{2,1,0:T(8,128)(2,1)S(1)} %get-tuple-element.32), channel_id=1, source_target_pairs={{0,4},{1,3},{2,6},{3,1},{4,0},{5,7},{6,2},{7,5},{8,12},{9,11},{10,... | collective-permute-start | bytes 786440 | tf_op jit(solution)/shard_map/ppermute | solution.py:209
  144.6 12.7 %collective-permute-start.33 = (bf16[1,128,1024]{2,1,0:T(8,128)(2,1)S(1)}, bf16[1,128,1024]{2,1,0:T(8,128)(2,1)S(1)}, u32[]{:S(2)}, u32[]{:S(2)}) collective-permute-start(bf16[1,128,1024]{2,1,0:T(8,128)(2,1)S(1)} %get-tuple-element.30), channel_id=1, source_target_pairs={{0,4},{1,3},{2,6},{3,1},{4,0},{5,7},{6,2},{7,5},{8,12},{9,11},{10,... | collective-permute-start | bytes 786440 | tf_op jit(solution)/shard_map/ppermute | solution.py:209
  152.1 20.6 %collective-permute-start.28 = (bf16[2,2,128,1024]{3,2,1,0:T(8,128)(2,1)S(1)}, bf16[2,2,128,1024]{3,2,1,0:T(8,128)(2,1)S(1)}, u32[]{:S(2)}, u32[]{:S(2)}) collective-permute-start(bf16[2,2,128,1024]{3,2,1,0:T(8,128)(2,1)S(1)} %pad_maximum_fusion.1), channel_id=1, source_target_pairs={{0,2},{1,5},{2,0},{3,7},{4,6},{5,1},{6,4},{7,3},{8,10},{9,13},{10,... | collective-permute-start | bytes 3145736 | tf_op jit(solution)/shard_map/ppermute | solution.py:209
  152.8 19.7 %collective-permute-start.23 = (bf16[2,1,128,1024]{3,2,1,0:T(8,128)(2,1)S(1)}, bf16[2,1,128,1024]{3,2,1,0:T(8,128)(2,1)S(1)}, u32[]{:S(2)}, u32[]{:S(2)}) collective-permute-start(bf16[2,1,128,1024]{3,2,1,0:T(8,128)(2,1)S(1)} %pad_maximum_fusion.5), channel_id=1, source_target_pairs={{0,2},{1,5},{2,0},{3,7},{4,6},{5,1},{6,4},{7,3},{8,10},{9,13},{10,... | collective-permute-start | bytes 1572872 | tf_op jit(solution)/shard_map/ppermute | solution.py:209
  157.5 20.7 %collective-permute-start.34 = (bf16[2,1,128,1024]{3,2,1,0:T(8,128)(2,1)S(1)}, bf16[2,1,128,1024]{3,2,1,0:T(8,128)(2,1)S(1)}, u32[]{:S(2)}, u32[]{:S(2)}) collective-permute-start(bf16[2,1,128,1024]{3,2,1,0:T(8,128)(2,1)S(1)} %pad_maximum_fusion.6), channel_id=1, source_target_pairs={{0,2},{1,5},{2,0},{3,7},{4,6},{5,1},{6,4},{7,3},{8,10},{9,13},{10,... | collective-permute-start | bytes 1572872 | tf_op jit(solution)/shard_map/ppermute | solution.py:209
  181.3 22.3 %collective-permute-start.31 = (bf16[128,1024]{1,0:T(8,128)(2,1)S(1)}, bf16[128,1024]{1,0:T(8,128)(2,1)S(1)}, u32[]{:S(2)}, u32[]{:S(2)}) collective-permute-start(bf16[128,1024]{1,0:T(8,128)(2,1)S(1)} %get-tuple-element.35), channel_id=1, source_target_pairs={{0,16},{8,24},{16,0},{24,8},{1,17},{9,25},{17,1},{25,9},{2,18},{10... | collective-permute-start | bytes 786440 | tf_op jit(solution)/shard_map/ppermute | solution.py:212
  181.3 22.3 %collective-permute-start.30 = (bf16[128,1024]{1,0:T(8,128)(2,1)S(1)}, bf16[128,1024]{1,0:T(8,128)(2,1)S(1)}, u32[]{:S(2)}, u32[]{:S(2)}) collective-permute-start(bf16[128,1024]{1,0:T(8,128)(2,1)S(1)} %get-tuple-element.34), channel_id=1, source_target_pairs={{0,8},{8,0},{16,24},{24,16},{1,9},{9,1},{17,25},{25,17},{2,10},{10... | collective-permute-start | bytes 786440 | tf_op jit(solution)/shard_map/ppermute | solution.py:212
  (40 other events, 379.5 us)

commit v3 on v0

v3 whole, which is shorter than its diff:
```python
import functools

import jax
import jax.numpy as jnp
from jax import lax
from jax.experimental import pallas as pl
from jax.experimental.pallas import tpu as pltpu
from jax.sharding import PartitionSpec as P

F32, BF16 = jnp.float32, jnp.bfloat16
ROWS_BY_ROWS = (((1,), (1,)), ((), ()))
VMEM = 48 << 20


def call(kernel, name, grid, in_specs, out_specs, out_shape, operands):
    return pl.pallas_call(
        kernel,
        grid_spec=pltpu.PrefetchScalarGridSpec(
            num_scalar_prefetch=1, grid=grid, in_specs=in_specs, out_specs=out_specs
        ),
        out_shape=out_shape,
        compiler_params=pltpu.CompilerParams(vmem_limit_bytes=VMEM),
        name=name,
    )(*operands)


def coefficient_kernel(capacity, topk, at_ref, info_ref, gate_ref, up_ref, cg_ref, cu_ref, cr_ref):
    blocks, _, tokens = info_ref.shape
    experts, width, slots = gate_ref.shape
    before = lax.broadcasted_iota(jnp.int32, (tokens, tokens), 0)
    earlier = (before < lax.broadcasted_iota(jnp.int32, (tokens, tokens), 1)).astype(BF16)
    columns = []
    for b in range(blocks):
        info = info_ref[b].astype(F32)
        ids, prob = info[:topk], info[topk : 2 * topk] + info[2 * topk : 3 * topk]
        named, weight = [], []
        for e in range(experts):
            chosen = ids == (at_ref[0] + e).astype(F32)
            named.append(jnp.max(jnp.where(chosen, 1.0, 0.0), axis=0, keepdims=True))
            weight.append(jnp.sum(jnp.where(chosen, prob, 0.0), axis=0, keepdims=True))
        named = jnp.concatenate(named, axis=0)
        position = jnp.dot(named.astype(BF16), earlier, preferred_element_type=F32)
        block = at_ref[1 + pl.program_id(0) * blocks + b]
        slot = jnp.where(named > 0.0, position + (block * capacity).astype(F32), -1.0)
        fill = jnp.zeros((8 - 2 * experts, tokens), F32)
        columns.append(jnp.transpose(jnp.concatenate([slot, *weight, fill], axis=0)))
    columns = jnp.concatenate(columns, axis=0)
    number = lax.broadcasted_iota(jnp.int32, (blocks * tokens, slots), 1).astype(F32)
    for e in range(experts):
        pick = jnp.where(columns[:, e : e + 1] == number, 1.0, 0.0).astype(BF16)
        g = lax.dot_general(pick, gate_ref[e], ROWS_BY_ROWS, preferred_element_type=F32)
        u = lax.dot_general(pick, up_ref[e], ROWS_BY_ROWS, preferred_element_type=F32)
        p = columns[:, experts + e : experts + e + 1]
        sg = 1.0 / (1.0 + jnp.exp(-g))
        silu = g * sg
        span = slice(e * width, (e + 1) * width)
        cg_ref[:, span] = (u * sg * (1.0 + g * (1.0 - sg)) * p).astype(BF16)
        cu_ref[:, span] = (silu * p).astype(BF16)
        cr_ref[:, span] = (silu * u).astype(BF16)


def coefficients(at, info, topk, saved_gate, saved_up, capacity):
    blocks, lines, tokens = info.shape
    experts, width, _ = saved_gate.shape
    per = 2 if blocks % 2 == 0 else 1
    whole = pl.BlockSpec(saved_gate.shape, lambda i, at: (0, 0, 0))
    out = pl.BlockSpec((per * tokens, experts * width), lambda i, at: (i, 0))
    return call(
        functools.partial(coefficient_kernel, capacity, topk),
        "coefficients",
        (blocks // per,),
        [pl.BlockSpec((per, lines, tokens), lambda i, at: (i, 0, 0)), whole, whole],
        [out] * 3,
        [jax.ShapeDtypeStruct((blocks * tokens, experts * width), BF16)] * 3,
        (at, info, saved_gate, saved_up),
    )


def products(refs, wd_refs):
    total = None
    for k, wd_ref in enumerate(wd_refs):
        parts = [r[:, k].reshape(r.shape[0] * r.shape[2], r.shape[3]) for r in refs]
        x = parts[0] if len(parts) == 1 else jnp.concatenate(parts, axis=0)
        part = lax.dot_general(x, wd_ref[...], ROWS_BY_ROWS, preferred_element_type=F32)
        total = part if total is None else total + part
    return total


def early_kernel(blocks, pieces, z_ref, *refs):
    rows, wd_refs, rest = refs[:blocks], refs[blocks : blocks + pieces], refs[blocks + pieces :]
    h = products(rows, wd_refs)
    rest[-1][...] = h if len(rest) == 1 else rest[0][...] + h


def late_kernel(blocks, pieces, width, moves, z_ref, *refs):
    rows, wd_refs, rest = refs[:blocks], refs[blocks : blocks + pieces], refs[blocks + pieces :]
    h_ref, cg_ref, cu_ref, cr_ref, ag_ref, au_ref, r_ref = rest
    h = h_ref[...] + products(rows, wd_refs)
    ag = (h * cg_ref[...].astype(F32)).astype(BF16)
    au = (h * cu_ref[...].astype(F32)).astype(BF16)
    tokens = h.shape[0] // len(moves)
    for i, j in enumerate(moves):
        to, of = slice(j * tokens, (j + 1) * tokens), slice(i * tokens, (i + 1) * tokens)
        ag_ref[to], au_ref[to] = ag[of], au[of]
    terms = h * cr_ref[...].astype(F32)
    unit = pl.program_id(0) * terms.shape[1] + lax.broadcasted_iota(jnp.int32, terms.shape, 1)

    @pl.when(pl.program_id(0) == 0)
    def _():
        r_ref[...] = jnp.zeros_like(r_ref)

    for e in range(r_ref.shape[1]):
        own = (unit >= e * width) & (unit < (e + 1) * width)
        r_ref[:, e : e + 1] += jnp.sum(jnp.where(own, terms, 0.0), axis=1, keepdims=True)


def tile_of(n):
    return 256 if n % 256 == 0 else 128 if n % 128 == 0 else n


def hidden(z, first, blocks, tokens, w_down, before=None, coefs=None, experts=None, moves=None):
    units = w_down.shape[0]
    tile = tile_of(units)
    pieces, span = blocks[0].shape[1], blocks[0].shape[3]
    total = tokens * sum(b.shape[0] for b in blocks)
    specs = [pl.BlockSpec((b.shape[0], pieces, tokens, span), lambda n, z: (0, 0, 0, 0)) for b in blocks]
    specs += [pl.BlockSpec((tile, span), lambda n, z, i=first + k: (n, z[0] ^ i)) for k in range(pieces)]
    operands = [z, *blocks] + [w_down] * pieces
    column = pl.BlockSpec((total, tile), lambda n, z: (0, n))
    if before is not None:
        specs, operands = specs + [column], operands + [before]
    grid = (units // tile,)
    if coefs is None:
        out = jax.ShapeDtypeStruct((total, units), F32)
        kernel = functools.partial(early_kernel, len(blocks), pieces)
        return call(kernel, "hidden_early", grid, specs, column, out, operands)
    kernel = functools.partial(late_kernel, len(blocks), pieces, units // experts, moves)
    outs = [column, column, pl.BlockSpec((total, experts), lambda n, z: (0, 0))]
    shapes = [jax.ShapeDtypeStruct((total, units), BF16)] * 2 + [jax.ShapeDtypeStruct((total, experts), F32)]
    return call(kernel, "hidden_late", grid, specs + [column] * 3, outs, shapes, [*operands, *coefs])


def expand_kernel(counts, adds, z_ref, ag_ref, au_ref, wg_ref, wu_ref, *refs):
    more, outs = refs[: int(adds)], refs[int(adds) :]
    rows, width = outs[0].shape[2:]
    tile = tile_of(width)
    for at in range(0, width, tile):
        span = slice(at, at + tile)
        y = jnp.dot(ag_ref[...], wg_ref[:, span], preferred_element_type=F32)
        y = y + jnp.dot(au_ref[...], wu_ref[:, span], preferred_element_type=F32)
        i = 0
        for out, count in zip(outs, counts):
            for j in range(count):
                part = y[i * rows : (i + 1) * rows]
                if adds:
                    part = part + more[0][i, 0, :, span].astype(F32)
                out[j, 0, :, span] = part.astype(BF16)
                i += 1


def expand(z, first, pieces, part, ag, au, w_gate, w_up, sections, rows, counts, more=None):
    units = ag.shape[1]
    number = sum(counts)
    span = w_gate.shape[1] // sections
    half = max(span // 2, 128)
    per = span // half
    some = pl.BlockSpec((number * rows, units), lambda k, j, z: (part, 0))
    weight = pl.BlockSpec((units, half), lambda k, j, z: (0, (z[0] ^ (first + k)) * per + j))
    block = lambda n: pl.BlockSpec((n, 1, rows, half), lambda k, j, z: (0, k, 0, j))
    extra = [] if more is None else [more]
    return call(
        functools.partial(expand_kernel, counts, more is not None),
        "expand",
        (pieces, per),
        [some, some, weight, weight] + [block(number)] * len(extra),
        [block(n) for n in counts],
        [jax.ShapeDtypeStruct((n, pieces, rows, span), BF16) for n in counts],
        [z, ag, au, w_gate, w_up, *extra],
    )


def add(*terms):
    return functools.reduce(lambda a, b: a + b, [t.astype(F32) for t in terms]).astype(BF16)


def after(x, *others):
    return lax.optimization_barrier((x, *others))[0]


def local(grad_out, probs, expert_ids, w_gate, w_up, w_down, saved_gate, saved_up):
    groups, sections = lax.axis_size("expert"), lax.axis_size("section")
    me, z = lax.axis_index("expert"), lax.axis_index("section")
    experts, units, features = w_gate.shape
    slots = saved_gate.shape[2]
    tokens, topk = expert_ids.shape
    span = grad_out.shape[1]
    square = groups == 8
    flat = lambda w: w.reshape(experts * units, features)
    w_gate, w_up, w_down = flat(w_gate), flat(w_up), flat(w_down)
    start = z.astype(jnp.int32).reshape(1)

    core = me % 2
    near = jnp.where(core == 0, 2, 4)
    far = 6 - near

    def swap(x, even, odd):
        return lax.ppermute(x, "expert", [(i, i ^ (even, odd)[i % 2]) for i in range(groups)])

    def across(x, by):
        return lax.ppermute(x, "section", [(i, i ^ by) for i in range(sections)])

    if square:
        owners = jnp.stack([me, me ^ 1, me ^ near, me ^ near ^ 1, me ^ 1 ^ far, me ^ far, me ^ 6, me ^ 7])
        moves = (0, 4, 1, 2, 5, 6, 3, 7)
    else:
        owners, moves = jnp.arange(groups), tuple(range(groups))

    high = lax.reduce_precision(probs, 8, 7)
    routing = jnp.concatenate([expert_ids.T.astype(F32), high.T, (probs - high).T], axis=0)
    lines = 3 * topk
    more = -(-lines * tokens // (16 * span)) * 16
    routing = jnp.pad(routing.reshape(-1), (0, more * span - lines * tokens)).reshape(more, span)
    own = jnp.concatenate([grad_out, routing.astype(BF16)], axis=0)[None, None]
    received = [None] + [across(grad_out[None], i) for i in (1, 2) if i < sections]
    if square:
        pair0 = jnp.concatenate([own, swap(own, 1, 1)])
        first0 = swap(pair0, 2, 4)
        second0 = swap(first0[:1], 4, 2)
        lot0 = [pair0, first0, swap(first0, 1, 1), second0, swap(second0, 1, 1)]
    else:
        first0 = lax.all_gather(own, "expert", axis=0, tiled=True)
        lot0 = [first0]
    for i in range(3, sections):
        received.append(across(after(grad_out[None], received[i - 2]), i))

    info = jnp.concatenate([b[:, 0, tokens:] for b in lot0], axis=0).reshape(groups, more * span)
    info = info[:, : lines * tokens].reshape(groups, lines, tokens)
    at = jnp.concatenate([(me * experts)[None], owners]).astype(jnp.int32)

    if square:
        own1 = after(jnp.stack(received[1:3], axis=1), first0)
        pair1 = jnp.concatenate([own1, swap(own1, 1, 1)])
        first1 = swap(after(pair1, second0), 2, 4)
        coefs = coefficients(at, info, topk, saved_gate, saved_up, slots // groups)
        h = hidden(start, 0, lot0, tokens, after(w_down, coefs[0]))
        own2 = jnp.stack(received[3:], axis=1)
        pair2 = jnp.concatenate([own2, swap(own2, 1, 1)])
        first1 = after(first1, h)
        second1 = swap(first1[:1], 4, 2)
        first2 = swap(after(pair2, first1), 2, 4)
        lot1 = [pair1, first1, swap(first1, 1, 1), second1, swap(second1, 1, 1)]
        h = hidden(start, 1, lot1, tokens, after(w_down, first2), h)
        second2 = swap(first2[:1], 4, 2)
        lot2 = [pair2, first2, swap(first2, 1, 1), second2, swap(second2, 1, 1)]
    else:
        coefs = coefficients(at, info, topk, saved_gate, saved_up, slots // groups)
        gather = lambda xs: [lax.all_gather(jnp.stack(xs, axis=1), "expert", axis=0, tiled=True)]
        h = hidden(start, 0, lot0, tokens, w_down)
        h = hidden(start, 1, gather(received[1:3]), tokens, w_down, h)
        lot2 = gather(received[3:])
    ag, au, router = hidden(start, 3, lot2, tokens, w_down, h, coefs, experts, moves)

    lots = ((3, sections), (1, 3), (0, 1))
    weights = (w_gate, w_up)
    half = groups // 2
    last = [router]
    theirs, kept, sent, parts = {}, {}, {}, {}

    def run_expand(n, part, counts, more=None):
        a, b = lots[n]
        outs = expand(start, a, b - a, part, after(ag, *last), au, *weights, sections, tokens, counts, more)
        last[0] = outs[0]
        return outs

    def theirs_step(n):
        theirs[n] = swap(run_expand(n, 1, (half,))[0], 1, 1)

    def mine_step(n):
        alone, two, one = run_expand(n, 0, (1, 2, 1), theirs[n])
        kept[n] = alone, two, swap(one, 4, 2)

    def sent_step(n):
        _, two, one = kept[n]
        two = after(two, *last)
        two = jnp.concatenate([add(two[:1], one), two[1:]])
        last[0] = two
        sent[n] = swap(two, 2, 4)

    def final_step(n):
        a, b = lots[n]
        mine = after(sent[n], *last)
        other = swap(mine[1:], 1, 1)
        sums = [add(kept[n][0][0, k], mine[0, k], other[0, k]) for k in range(b - a)]
        last[0] = sums[0]
        for k, x in enumerate(sums):
            parts[a + k] = x if a + k == 0 else across(x, a + k)

    if square:
        for step, n in (
            (theirs_step, 0),
            (theirs_step, 1),
            (mine_step, 0),
            (mine_step, 1),
            (theirs_step, 2),
            (sent_step, 0),
            (mine_step, 2),
            (sent_step, 1),
            (final_step, 0),
            (sent_step, 2),
            (final_step, 1),
            (final_step, 2),
        ):
            step(n)
    else:
        for n, (a, b) in enumerate(lots):
            sums = lax.psum_scatter(run_expand(n, 0, (groups,))[0], "expert", scatter_dimension=0, tiled=True)[0]
            for k in range(b - a):
                parts[a + k] = sums[k] if a + k == 0 else across(sums[k], a + k)
    grad_in = add(*parts.values())

    router = router.reshape(groups, tokens, experts)
    if square:
        router = after(router, kept[2][0])
        for bit in range(sections.bit_length() - 1):
            router = router + across(router, 1 << bit)
        even = router[jnp.array([0, 1, 2, 3, 5, 4, 6, 7])]
        odd = router[jnp.array([0, 1, 5, 4, 2, 3, 6, 7])]
        router = jnp.where(core == 0, even, odd)
        router = router.transpose(0, 2, 1)
        gathered = router[None]
        for bit in (1, 2, 4):
            gathered = jnp.concatenate([gathered, swap(gathered, bit, bit)], axis=0)
        back = jnp.stack([gathered[q, q] for q in range(groups)])
        source = me ^ jnp.arange(groups)
    else:
        router = lax.psum(router, "section").transpose(0, 2, 1)
        back = lax.all_to_all(router, "expert", split_axis=0, concat_axis=0)
        source = jnp.arange(groups)
    number = (source[:, None] * experts + jnp.arange(experts)).reshape(-1)
    back = back.reshape(groups * experts, tokens)
    match = expert_ids[None] == number[:, None, None]
    grad_probs = jnp.sum(jnp.where(match, back[:, :, None], 0.0), axis=0).astype(BF16)
    return (grad_in, grad_probs)


def solution(mesh):
    placed = (
        P("expert", "section"),
        P("expert", None),
        P("expert", None),
        P("expert", "section", None),
        P("expert", "section", None),
        P("expert", "section", None),
        P("expert", "section", None),
        P("expert", "section", None),
    )
    return jax.shard_map(
        local,
        mesh=mesh,
        in_specs=placed,
        out_specs=(P("expert", "section"), P("expert", None)),
        check_vma=False,
    )
```

time: 514 us -> 209 us (0.41)
  waiting for transfers between devices: 247 us -> 81.6 us
  blocking collectives: 154 us -> 0 us
  Pallas kernels: 0 us -> 52.3 us
  matrix products: 39 us -> 0 us
  starting transfers between devices: 7.39 us -> 36.7 us
  local copies, waits for them, and re-layouts: 43.7 us -> 26.2 us
  between operations: 14.2 us -> 1.14 us
    reduce_scatter x1 -> x0, waiting for transfers between devices: 195 us -> none  [local(): lax.psum_scatter(term.astype(jnp.bfloat16), 'section', scatter_dimension=...]
    all_to_all x1 -> x0, blocking collectives: 143 us -> none  [local(): lax.all_to_all(outgoing, 'expert', split_axis=0, concat_axis=1, tiled=True)]
    ppermute x0 -> x38, waiting for transfers between devices: none -> 81.6 us  [the longest x30 50.8 us: swap(): lax.ppermute(x, 'expert', [(i, i ^ (even, odd)[i % 2]) for i in range(gro...]
    pallas_call x0 -> x10, Pallas kernels: none -> 52.3 us  [call(): pl.pallas_call(kernel, grid_spec=pltpu.PrefetchScalarGridSpec(num_scalar_...]
    dot_general x3 -> x0, matrix products: 39 us -> none  [the longest x1 16.3 us: local(): jnp.einsum('efc,efs->esc', w_up, up_grad, preferred_element_type=jnp.floa...]
    ppermute x0 -> x38, starting transfers between devices: none -> 36.7 us  [the longest x30 20.9 us: swap(): lax.ppermute(x, 'expert', [(i, i ^ (even, odd)[i % 2]) for i in range(gro...]
    all_to_all x2 -> x0, waiting for transfers between devices: 30.1 us -> none  [the longest x1 30 us: local(): lax.all_to_all(shares, 'expert', split_axis=1, concat_axis=0, tiled=True)]
    all_gather x1 -> x0, waiting for transfers between devices: 21.1 us -> none  [local(): full_rows = lax.all_gather(grad_out, 'section', axis=1, tiled=True)]
  transfers between devices with their start and end apart: 4 -> 38, of which waited for: 3 -> 16; matrix products, arithmetic and copies ran while one was open for 5% -> 9% of each run, Pallas kernels for 0% -> 12%
where the time goes in v3:
time: 209 us; the launch traced here: 208 us
  waiting for transfers between devices  81.6 us (39%)
  Pallas kernels  52.3 us (25%)
  starting transfers between devices  36.7 us (18%)
  local copies, waits for them, and re-layouts  26.2 us (13%)
  other arithmetic  10.2 us (5%)
    pallas_call x10, Pallas kernels, call(): pl.pallas_call(kernel, grid_spec=pltpu.PrefetchScalarGridSpec(num_scalar_...  52.3 us
    ppermute x30, waiting for transfers between devices, swap(): lax.ppermute(x, 'expert', [(i, i ^ (even, odd)[i % 2]) for i in range(gro...  50.8 us
    ppermute x8, waiting for transfers between devices, across(): return lax.ppermute(x, 'section', [(i, i ^ by) for i in range(sections)])  30.8 us
    ppermute x30, starting transfers between devices, swap(): lax.ppermute(x, 'expert', [(i, i ^ (even, odd)[i % 2]) for i in range(gro...  20.9 us
    unnamed x71, local copies, waits for them, and re-layouts  19.4 us
    ppermute x8, starting transfers between devices, across(): return lax.ppermute(x, 'section', [(i, i ^ by) for i in range(sections)])  15.7 us
  transfers between devices with their start and end apart: 38, of which 16 were waited for; matrix products, arithmetic and copies ran while one was open for 9% of the time, Pallas kernels for 12%

profile of v3, /device:TPU:0, one launch (start us, length us, event | category | flops | bytes accessed | tf_op | source)
XLA Modules:
  0.0 208.1 jit_solution(30465743555068410)
XLA Ops:
  4.8 2.9 %collective-permute-start.5 = (bf16[2,1,144,1024]{3,2,1,0:T(8,128)(2,1)S(1)}, bf16[2,1,144,1024]{3,2,1,0:T(8,128)(2,1)}, u32[]{:S(2)}, u32[]{:S(2)}) collective-permute-start(bf16[2,1,144,1024]{3,2,1,0:T(8,128)(2,1)S(1)} %pad_maximum_fusion.1.refs_0_), channel_id=1, source_target_pairs={{0,2},{1,5},{2,0},{3,7},{4,6},{5,1},{6,4},{7,3},{8,10},{9,13},{10,... | collective-permute-start | bytes 1769480 | tf_op jit(solution)/shard_map/ppermute | solution.py:207
  9.3 2.6 %collective-permute-start.3 = (bf16[1,128,1024]{2,1,0:T(8,128)(2,1)}, bf16[1,128,1024]{2,1,0:T(8,128)(2,1)S(1)}, u32[]{:S(2)}, u32[]{:S(2)}) collective-permute-start(bf16[1,128,1024]{2,1,0:T(8,128)(2,1)} %bitcast.125), channel_id=1, source_target_pairs={{0,16},{8,24},{16,0},{24,8},{1,17},{9,25},{17,1},{25,9},{2,18},{10... | collective-permute-start | bytes 786440 | tf_op jit(solution)/shard_map/ppermute | solution.py:210
  11.9 9.6 %collective-permute-done = bf16[1,128,1024]{2,1,0:T(8,128)(2,1)S(1)} collective-permute-done((bf16[1,128,1024]{2,1,0:T(8,128)(2,1)}, bf16[1,128,1024]{2,1,0:T(8,128)(2,1)S(1)}, u32[]{:S(2)}, u32[]{:S(2)}) %collective-permute-start) | collective-permute-done | bytes 262176 | tf_op jit(solution)/shard_map/ppermute | solution.py:210
  24.2 6.7 %collective-permute-done.1 = bf16[1,128,1024]{2,1,0:T(8,128)(2,1)S(1)} collective-permute-done((bf16[1,128,1024]{2,1,0:T(8,128)(2,1)}, bf16[1,128,1024]{2,1,0:T(8,128)(2,1)S(1)}, u32[]{:S(2)}, u32[]{:S(2)}) %collective-permute-start.1) | collective-permute-done | bytes 262176 | tf_op jit(solution)/shard_map/ppermute | solution.py:210
  51.6 7.3 %coefficients.1 = (bf16[1024,768]{1,0:T(8,128)(2,1)S(1)}, bf16[1024,768]{1,0:T(8,128)(2,1)S(1)}, bf16[1024,768]{1,0:T(8,128)(2,1)}) custom-call(s32[9]{0:T(128)S(1)} %concatenate.54.at_ref, bf16[8,24,128]{2,1,0:T(8,128)(2,1)S(1)} %bitcast.102, bf16[2,384,768]{2,1,0:T(8,128)(2,1)S(1)} %copy-done.5, bf16[2,384,768]{2,1,0:T(8,128)(2,1)S(1)} %copy-done.6), custom_call_target="tpu_custom_call" | custom-call | tf_op jit(solution)/shard_map/coefficients/pallas_call | solution.py:16
  61.2 3.9 %hidden_early.2.refs_7_ = f32[1024,768]{1,0:T(8,128)S(1)} custom-call(s32[1]{0:T(128)} %bitcast.z_ref, bf16[2,1,144,1024]{3,2,1,0:T(8,128)(2,1)S(1)} %pad_maximum_fusion.1.refs_0_, bf16[2,1,144,1024]{3,2,1,0:T(8,128)(2,1)} %collective-permute-done.5.refs_1_, bf16[2,1,144,1024]{3,2,1,0:T(8,128)(2,1)S(1)} %copy-done.10, ...), custom_call_target="tpu_custom_call" | custom-call | tf_op jit(solution)/shard_map/hidden_early/pallas_call | solution.py:16
  68.6 12.4 %collective-permute-done.16.refs_3_ = bf16[1,2,128,1024]{3,2,1,0:T(8,128)(2,1)S(1)} collective-permute-done((bf16[1,2,128,1024]{3,2,1,0:T(8,128)(2,1)S(1)}, bf16[1,2,128,1024]{3,2,1,0:T(8,128)(2,1)S(1)}, u32[]{:S(2)}, u32[]{:S(2)}) %collective-permute-start.16) | collective-permute-done | bytes 524320 | tf_op jit(solution)/shard_map/ppermute | solution.py:207
  81.7 5.8 %collective-permute-done.13.refs_3_ = bf16[1,1,128,1024]{3,2,1,0:T(8,128)(2,1)S(1)} collective-permute-done((bf16[1,1,128,1024]{3,2,1,0:T(8,128)(2,1)S(1)}, bf16[1,1,128,1024]{3,2,1,0:T(8,128)(2,1)S(1)}, u32[]{:S(2)}, u32[]{:S(2)}) %collective-permute-start.13) | collective-permute-done | bytes 262176 | tf_op jit(solution)/shard_map/ppermute | solution.py:207
  87.5 7.1 %hidden_early.3.refs_6_ = f32[1024,768]{1,0:T(8,128)} custom-call(s32[1]{0:T(128)} %bitcast.z_ref, bf16[2,2,128,1024]{3,2,1,0:T(8,128)(2,1)S(1)} %constant_dynamic-update-slice_fusion.refs_0_, bf16[2,2,128,1024]{3,2,1,0:T(8,128)(2,1)S(1)} %collective-permute-done.8.refs_1_, bf16[2,2,128,1024]{3,2,1,0:T(8,128)(2,1)S(1)} %collective-permute-done.15.refs_2_, ...), custom_call_target="tpu_custom_call" | custom-call | tf_op jit(solution)/shard_map/hidden_early/pallas_call | solution.py:16
  94.6 6.3 %hidden_late.1 = (bf16[1024,768]{1,0:T(8,128)(2,1)S(1)}, bf16[1024,768]{1,0:T(8,128)(2,1)S(1)}, f32[1024,2]{1,0:T(8,128)S(1)}) custom-call(s32[1]{0:T(128)} %bitcast.z_ref, bf16[2,1,128,1024]{3,2,1,0:T(8,128)(2,1)S(1)} %copy-done.2, bf16[2,1,128,1024]{3,2,1,0:T(8,128)(2,1)S(1)} %collective-permute-done.11.refs_1_, ...), custom_call_target="tpu_custom_call" | custom-call | tf_op jit(solution)/shard_map/hidden_late/pallas_call | solution.py:16
  101.7 3.4 %expand.6 = bf16[4,1,128,1024]{3,2,1,0:T(8,128)(2,1)S(1)} custom-call(s32[1]{0:T(128)} %bitcast.z_ref, bf16[1024,768]{1,0:T(8,128)(2,1)S(1)} %get-tuple-element.61.ag_ref, bf16[1024,768]{1,0:T(8,128)(2,1)S(1)} %get-tuple-element.50.au_ref, bf16[768,4096]{1,0:T(8,128)(2,1)} %bitcast.103, bf16[768,4096]{1,0:T(8,128)(2,1)} %bitcast.109), custom_call_target="tpu_custom_call" | custom-call | tf_op jit(solution)/shard_map/expand/pallas_call | solution.py:16
  105.2 5.9 %expand.7 = bf16[4,2,128,1024]{3,2,1,0:T(8,128)(2,1)S(1)} custom-call(s32[1]{0:T(128)} %bitcast.z_ref, bf16[1024,768]{1,0:T(8,128)(2,1)S(1)} %get-tuple-element.61.ag_ref, bf16[1024,768]{1,0:T(8,128)(2,1)S(1)} %get-tuple-element.50.au_ref, bf16[768,4096]{1,0:T(8,128)(2,1)} %bitcast.104, bf16[768,4096]{1,0:T(8,128)(2,1)} %bitcast.110), custom_call_target="tpu_custom_call" | custom-call | tf_op jit(solution)/shard_map/expand/pallas_call | solution.py:16
  111.8 5.2 %collective-permute-done.18.refs_0_ = bf16[4,1,128,1024]{3,2,1,0:T(8,128)(2,1)S(1)} collective-permute-done((bf16[4,1,128,1024]{3,2,1,0:T(8,128)(2,1)S(1)}, bf16[4,1,128,1024]{3,2,1,0:T(8,128)(2,1)S(1)}, u32[]{:S(2)}, u32[]{:S(2)}) %collective-permute-start.18) | collective-permute-done | bytes 1048608 | tf_op jit(solution)/shard_map/ppermute | solution.py:207
  117.0 3.5 %expand.8 = (bf16[1,1,128,1024]{3,2,1,0:T(8,128)(2,1)S(1)}, bf16[2,1,128,1024]{3,2,1,0:T(8,128)(2,1)S(1)}, bf16[1,1,128,1024]{3,2,1,0:T(8,128)(2,1)S(1)}) custom-call(s32[1]{0:T(128)} %bitcast.z_ref, bf16[1024,768]{1,0:T(8,128)(2,1)S(1)} %get-tuple-element.61.ag_ref, bf16[1024,768]{1,0:T(8,128)(2,1)S(1)} %get-tuple-element.50.au_ref, ...), custom_call_target="tpu_custom_call" | custom-call | tf_op jit(solution)/shard_map/expand/pallas_call | solution.py:16
  122.5 7.0 %expand.9 = (bf16[1,2,128,1024]{3,2,1,0:T(8,128)(2,1)S(1)}, bf16[2,2,128,1024]{3,2,1,0:T(8,128)(2,1)S(1)}, bf16[1,2,128,1024]{3,2,1,0:T(8,128)(2,1)}) custom-call(s32[1]{0:T(128)} %bitcast.z_ref, bf16[1024,768]{1,0:T(8,128)(2,1)S(1)} %get-tuple-element.61.ag_ref, bf16[1024,768]{1,0:T(8,128)(2,1)S(1)} %get-tuple-element.50.au_ref, ...), custom_call_target="tpu_custom_call" | custom-call | tf_op jit(solution)/shard_map/expand/pallas_call | solution.py:16
  131.3 4.2 %expand.10 = bf16[4,1,128,1024]{3,2,1,0:T(8,128)(2,1)} custom-call(s32[1]{0:T(128)} %bitcast.z_ref, bf16[1024,768]{1,0:T(8,128)(2,1)S(1)} %get-tuple-element.61.ag_ref, bf16[1024,768]{1,0:T(8,128)(2,1)S(1)} %get-tuple-element.50.au_ref, bf16[768,4096]{1,0:T(8,128)(2,1)} %bitcast.107, bf16[768,4096]{1,0:T(8,128)(2,1)} %bitcast.113), custom_call_target="tpu_custom_call" | custom-call | tf_op jit(solution)/shard_map/expand/pallas_call | solution.py:16
  138.0 4.3 %collective-permute-done.20 = bf16[1,1,128,1024]{3,2,1,0:T(8,128)(2,1)S(1)} collective-permute-done((bf16[1,1,128,1024]{3,2,1,0:T(8,128)(2,1)S(1)}, bf16[1,1,128,1024]{3,2,1,0:T(8,128)(2,1)S(1)}, u32[]{:S(2)}, u32[]{:S(2)}) %collective-permute-start.20) | collective-permute-done | bytes 262176 | tf_op jit(solution)/shard_map/ppermute | solution.py:207
  143.8 3.6 %expand.11 = (bf16[1,1,128,1024]{3,2,1,0:T(8,128)(2,1)S(1)}, bf16[2,1,128,1024]{3,2,1,0:T(8,128)(2,1)S(1)}, bf16[1,1,128,1024]{3,2,1,0:T(8,128)(2,1)S(1)}) custom-call(s32[1]{0:T(128)} %bitcast.z_ref, bf16[1024,768]{1,0:T(8,128)(2,1)S(1)} %get-tuple-element.61.ag_ref, bf16[1024,768]{1,0:T(8,128)(2,1)S(1)} %get-tuple-element.50.au_ref, ...), custom_call_target="tpu_custom_call" | custom-call | tf_op jit(solution)/shard_map/expand/pallas_call | solution.py:16
  150.3 4.5 %collective-permute-start.33 = (f32[8,128,2]{1,2,0:T(2,128)S(1)}, f32[8,128,2]{1,2,0:T(2,128)S(1)}, u32[]{:S(2)}, u32[]{:S(2)}) collective-permute-start(f32[8,128,2]{1,2,0:T(2,128)S(1)} %copy.18), channel_id=1, source_target_pairs={{0,8},{8,0},{16,24},{24,16},{1,9},{9,1},{17,25},{25,17},{2,10},{10... | collective-permute-start | bytes 24584 | tf_op jit(solution)/shard_map/ppermute | solution.py:210
  156.4 3.1 %collective-permute-start.34 = (f32[8,128,2]{1,2,0:T(2,128)S(1)}, f32[8,128,2]{1,2,0:T(2,128)S(1)}, u32[]{:S(2)}, u32[]{:S(2)}) collective-permute-start(f32[8,128,2]{1,2,0:T(2,128)S(1)} %add.107), channel_id=1, source_target_pairs={{0,16},{8,24},{16,0},{24,8},{1,17},{9,25},{17,1},{25,9},{2,18},{10... | collective-permute-start | bytes 24584 | tf_op jit(solution)/shard_map/ppermute | solution.py:210
  167.5 11.2 %collective-permute-done.36 = f32[2,8,2,128]{3,2,1,0:T(2,128)S(1)} collective-permute-done((f32[2,8,2,128]{3,2,1,0:T(2,128)S(1)}, f32[2,8,2,128]{3,2,1,0:T(2,128)S(1)}, u32[]{:S(2)}, u32[]{:S(2)}) %collective-permute-start.36) | collective-permute-done | bytes 16416 | tf_op jit(solution)/shard_map/ppermute | solution.py:207
  186.0 5.9 %collective-permute-done.31 = bf16[2,1,128,1024]{3,2,1,0:T(8,128)(2,1)S(1)} collective-permute-done((bf16[2,1,128,1024]{3,2,1,0:T(8,128)(2,1)S(1)}, bf16[2,1,128,1024]{3,2,1,0:T(8,128)(2,1)S(1)}, u32[]{:S(2)}, u32[]{:S(2)}) %collective-permute-start.31) | collective-permute-done | bytes 524320 | tf_op jit(solution)/shard_map/ppermute | solution.py:207
  195.3 4.3 %collective-permute-done.29 = bf16[128,1024]{1,0:T(8,128)(2,1)S(1)} collective-permute-done((bf16[128,1024]{1,0:T(8,128)(2,1)S(1)}, bf16[128,1024]{1,0:T(8,128)(2,1)S(1)}, u32[]{:S(2)}, u32[]{:S(2)}) %collective-permute-start.29) | collective-permute-done | bytes 262176 | tf_op jit(solution)/shard_map/ppermute | solution.py:210
  199.6 7.5 %collective-permute-done.30 = bf16[128,1024]{1,0:T(8,128)(2,1)S(1)} collective-permute-done((bf16[128,1024]{1,0:T(8,128)(2,1)S(1)}, bf16[128,1024]{1,0:T(8,128)(2,1)S(1)}, u32[]{:S(2)}, u32[]{:S(2)}) %collective-permute-start.30) | collective-permute-done | bytes 262176 | tf_op jit(solution)/shard_map/ppermute | solution.py:210
  (178 shorter events, 68.5 us)
Async XLA Ops:
  4.8 19.3 %collective-permute-start.5 = (bf16[2,1,144,1024]{3,2,1,0:T(8,128)(2,1)S(1)}, bf16[2,1,144,1024]{3,2,1,0:T(8,128)(2,1)}, u32[]{:S(2)}, u32[]{:S(2)}) collective-permute-start(bf16[2,1,144,1024]{3,2,1,0:T(8,128)(2,1)S(1)} %pad_maximum_fusion.1.refs_0_), channel_id=1, source_target_pairs={{0,2},{1,5},{2,0},{3,7},{4,6},{5,1},{6,4},{7,3},{8,10},{9,13},{10,... | collective-permute-start | bytes 1769480 | tf_op jit(solution)/shard_map/ppermute | solution.py:207
  7.7 13.8 %collective-permute-start = (bf16[1,128,1024]{2,1,0:T(8,128)(2,1)}, bf16[1,128,1024]{2,1,0:T(8,128)(2,1)S(1)}, u32[]{:S(2)}, u32[]{:S(2)}) collective-permute-start(bf16[1,128,1024]{2,1,0:T(8,128)(2,1)} %bitcast.124), channel_id=1, source_target_pairs={{0,8},{8,0},{16,24},{24,16},{1,9},{9,1},{17,25},{25,17},{2,10},{10... | collective-permute-start | bytes 786440 | tf_op jit(solution)/shard_map/ppermute | solution.py:210
  9.3 14.7 %collective-permute-start.3 = (bf16[1,128,1024]{2,1,0:T(8,128)(2,1)}, bf16[1,128,1024]{2,1,0:T(8,128)(2,1)S(1)}, u32[]{:S(2)}, u32[]{:S(2)}) collective-permute-start(bf16[1,128,1024]{2,1,0:T(8,128)(2,1)} %bitcast.125), channel_id=1, source_target_pairs={{0,16},{8,24},{16,0},{24,8},{1,17},{9,25},{17,1},{25,9},{2,18},{10... | collective-permute-start | bytes 786440 | tf_op jit(solution)/shard_map/ppermute | solution.py:210
  21.5 9.3 %collective-permute-start.1 = (bf16[1,128,1024]{2,1,0:T(8,128)(2,1)}, bf16[1,128,1024]{2,1,0:T(8,128)(2,1)S(1)}, u32[]{:S(2)}, u32[]{:S(2)}) collective-permute-start(bf16[1,128,1024]{2,1,0:T(8,128)(2,1)} %bitcast.126), channel_id=1, source_target_pairs={{0,24},{8,16},{16,8},{24,0},{1,25},{9,17},{17,9},{25,1},{2,26},{10... | collective-permute-start | bytes 786440 | tf_op jit(solution)/shard_map/ppermute | solution.py:210
  24.1 14.8 %collective-permute-start.6 = (bf16[1,2,128,1024]{3,2,1,0:T(8,128)(2,1)S(1)}, bf16[1,2,128,1024]{3,2,1,0:T(8,128)(2,1)S(1)}, u32[]{:S(2)}, u32[]{:S(2)}) collective-permute-start(bf16[1,2,128,1024]{3,2,1,0:T(8,128)(2,1)S(1)} %pad_maximum_fusion.3), channel_id=1, source_target_pairs={{0,1},{1,0},{2,3},{3,2},{4,5},{5,4},{6,7},{7,6},{8,9},{9,8},{10,11... | collective-permute-start | bytes 1572872 | tf_op jit(solution)/shard_map/ppermute | solution.py:207
  33.7 11.0 %collective-permute-start.9 = (bf16[2,1,144,1024]{3,2,1,0:T(8,128)(2,1)}, bf16[2,1,144,1024]{3,2,1,0:T(8,128)(2,1)S(1)}, u32[]{:S(2)}, u32[]{:S(2)}) collective-permute-start(bf16[2,1,144,1024]{3,2,1,0:T(8,128)(2,1)} %collective-permute-done.5.refs_1_), channel_id=1, source_target_pairs={{0,1},{1,0},{2,3},{3,2},{4,5},{5,4},{6,7},{7,6},{8,9},{9,8},{10,11... | collective-permute-start | bytes 1769480 | tf_op jit(solution)/shard_map/ppermute | solution.py:207
  38.9 27.9 %collective-permute-start.8 = (bf16[2,2,128,1024]{3,2,1,0:T(8,128)(2,1)S(1)}, bf16[2,2,128,1024]{3,2,1,0:T(8,128)(2,1)S(1)}, u32[]{:S(2)}, u32[]{:S(2)}) collective-permute-start(bf16[2,2,128,1024]{3,2,1,0:T(8,128)(2,1)S(1)} %constant_dynamic-update-slice_fusion.refs_0_), channel_id=1, source_target_pairs={{0,2},{1,5},{2,0},{3,7},{4,6},{5,1},{6,4},{7,3},{8,10},{9,13},{10,... | collective-permute-start | bytes 3145736 | tf_op jit(solution)/shard_map/ppermute | solution.py:207
  66.9 14.2 %collective-permute-start.16 = (bf16[1,2,128,1024]{3,2,1,0:T(8,128)(2,1)S(1)}, bf16[1,2,128,1024]{3,2,1,0:T(8,128)(2,1)S(1)}, u32[]{:S(2)}, u32[]{:S(2)}) collective-permute-start(bf16[1,2,128,1024]{3,2,1,0:T(8,128)(2,1)S(1)} %slice.110), channel_id=1, source_target_pairs={{0,4},{1,3},{2,6},{3,1},{4,0},{5,7},{6,2},{7,5},{8,12},{9,11},{10,... | collective-permute-start | bytes 1572872 | tf_op jit(solution)/shard_map/ppermute | solution.py:207
  66.9 14.1 %collective-permute-start.11 = (bf16[2,1,128,1024]{3,2,1,0:T(8,128)(2,1)S(1)}, bf16[2,1,128,1024]{3,2,1,0:T(8,128)(2,1)S(1)}, u32[]{:S(2)}, u32[]{:S(2)}) collective-permute-start(bf16[2,1,128,1024]{3,2,1,0:T(8,128)(2,1)S(1)} %pad_maximum_fusion.2.refs_0_), channel_id=1, source_target_pairs={{0,2},{1,5},{2,0},{3,7},{4,6},{5,1},{6,4},{7,3},{8,10},{9,13},{10,... | collective-permute-start | bytes 1572872 | tf_op jit(solution)/shard_map/ppermute | solution.py:207
  67.0 20.5 %collective-permute-start.15 = (bf16[2,2,128,1024]{3,2,1,0:T(8,128)(2,1)S(1)}, bf16[2,2,128,1024]{3,2,1,0:T(8,128)(2,1)S(1)}, u32[]{:S(2)}, u32[]{:S(2)}) collective-permute-start(bf16[2,2,128,1024]{3,2,1,0:T(8,128)(2,1)S(1)} %collective-permute-done.8.refs_1_), channel_id=1, source_target_pairs={{0,1},{1,0},{2,3},{3,2},{4,5},{5,4},{6,7},{7,6},{8,9},{9,8},{10,11... | collective-permute-start | bytes 3145736 | tf_op jit(solution)/shard_map/ppermute | solution.py:207
  81.4 13.3 %collective-permute-start.12 = (bf16[2,1,128,1024]{3,2,1,0:T(8,128)(2,1)S(1)}, bf16[2,1,128,1024]{3,2,1,0:T(8,128)(2,1)S(1)}, u32[]{:S(2)}, u32[]{:S(2)}) collective-permute-start(bf16[2,1,128,1024]{3,2,1,0:T(8,128)(2,1)S(1)} %collective-permute-done.11.refs_1_), channel_id=1, source_target_pairs={{0,1},{1,0},{2,3},{3,2},{4,5},{5,4},{6,7},{7,6},{8,9},{9,8},{10,11... | collective-permute-start | bytes 1572872 | tf_op jit(solution)/shard_map/ppermute | solution.py:207
  111.1 10.0 %collective-permute-start.19 = (bf16[4,2,128,1024]{3,2,1,0:T(8,128)(2,1)S(1)}, bf16[4,2,128,1024]{3,2,1,0:T(8,128)(2,1)S(1)}, u32[]{:S(2)}, u32[]{:S(2)}) collective-permute-start(bf16[4,2,128,1024]{3,2,1,0:T(8,128)(2,1)S(1)} %expand.7), channel_id=1, source_target_pairs={{0,1},{1,0},{2,3},{3,2},{4,5},{5,4},{6,7},{7,6},{8,9},{9,8},{10,11... | collective-permute-start | bytes 6291464 | tf_op jit(solution)/shard_map/ppermute | solution.py:207
  135.6 8.2 %collective-permute-start.22 = (bf16[4,1,128,1024]{3,2,1,0:T(8,128)(2,1)}, bf16[4,1,128,1024]{3,2,1,0:T(8,128)(2,1)}, u32[]{:S(2)}, u32[]{:S(2)}) collective-permute-start(bf16[4,1,128,1024]{3,2,1,0:T(8,128)(2,1)} %expand.10), channel_id=1, source_target_pairs={{0,1},{1,0},{2,3},{3,2},{4,5},{5,4},{6,7},{7,6},{8,9},{9,8},{10,11... | collective-permute-start | bytes 3145736 | tf_op jit(solution)/shard_map/ppermute | solution.py:207
  136.2 18.6 %collective-permute-start.23 = (bf16[1,2,128,1024]{3,2,1,0:T(8,128)(2,1)}, bf16[1,2,128,1024]{3,2,1,0:T(8,128)(2,1)}, u32[]{:S(2)}, u32[]{:S(2)}) collective-permute-start(bf16[1,2,128,1024]{3,2,1,0:T(8,128)(2,1)} %get-tuple-element.64), channel_id=1, source_target_pairs={{0,4},{1,3},{2,6},{3,1},{4,0},{5,7},{6,2},{7,5},{8,12},{9,11},{10,... | collective-permute-start | bytes 1572872 | tf_op jit(solution)/shard_map/ppermute | solution.py:207
  143.3 18.8 %collective-permute-start.21 = (bf16[2,1,128,1024]{3,2,1,0:T(8,128)(2,1)}, bf16[2,1,128,1024]{3,2,1,0:T(8,128)(2,1)}, u32[]{:S(2)}, u32[]{:S(2)}) collective-permute-start(bf16[2,1,128,1024]{3,2,1,0:T(8,128)(2,1)} %pad_maximum_fusion.4), channel_id=1, source_target_pairs={{0,2},{1,5},{2,0},{3,7},{4,6},{5,1},{6,4},{7,3},{8,10},{9,13},{10,... | collective-permute-start | bytes 1572872 | tf_op jit(solution)/shard_map/ppermute | solution.py:207
  156.4 7.4 %collective-permute-start.34 = (f32[8,128,2]{1,2,0:T(2,128)S(1)}, f32[8,128,2]{1,2,0:T(2,128)S(1)}, u32[]{:S(2)}, u32[]{:S(2)}) collective-permute-start(f32[8,128,2]{1,2,0:T(2,128)S(1)} %add.107), channel_id=1, source_target_pairs={{0,16},{8,24},{16,0},{24,8},{1,17},{9,25},{17,1},{25,9},{2,18},{10... | collective-permute-start | bytes 24584 | tf_op jit(solution)/shard_map/ppermute | solution.py:210
  160.6 20.9 %collective-permute-start.26 = (bf16[2,2,128,1024]{3,2,1,0:T(8,128)(2,1)}, bf16[2,2,128,1024]{3,2,1,0:T(8,128)(2,1)S(1)}, u32[]{:S(2)}, u32[]{:S(2)}) collective-permute-start(bf16[2,2,128,1024]{3,2,1,0:T(8,128)(2,1)} %pad_maximum_fusion), channel_id=1, source_target_pairs={{0,2},{1,5},{2,0},{3,7},{4,6},{5,1},{6,4},{7,3},{8,10},{9,13},{10,... | collective-permute-start | bytes 3145736 | tf_op jit(solution)/shard_map/ppermute | solution.py:207
  163.0 17.1 %collective-permute-start.24 = (bf16[1,1,128,1024]{3,2,1,0:T(8,128)(2,1)S(1)}, bf16[1,1,128,1024]{3,2,1,0:T(8,128)(2,1)S(1)}, u32[]{:S(2)}, u32[]{:S(2)}) collective-permute-start(bf16[1,1,128,1024]{3,2,1,0:T(8,128)(2,1)S(1)} %slice.116), channel_id=1, source_target_pairs={{0,1},{1,0},{2,3},{3,2},{4,5},{5,4},{6,7},{7,6},{8,9},{9,8},{10,11... | collective-permute-start | bytes 786440 | tf_op jit(solution)/shard_map/ppermute | solution.py:207
  163.1 18.2 %collective-permute-start.27 = (bf16[1,1,128,1024]{3,2,1,0:T(8,128)(2,1)S(1)}, bf16[1,1,128,1024]{3,2,1,0:T(8,128)(2,1)S(1)}, u32[]{:S(2)}, u32[]{:S(2)}) collective-permute-start(bf16[1,1,128,1024]{3,2,1,0:T(8,128)(2,1)S(1)} %copy-done.21), channel_id=1, source_target_pairs={{0,4},{1,3},{2,6},{3,1},{4,0},{5,7},{6,2},{7,5},{8,12},{9,11},{10,... | collective-permute-start | bytes 786440 | tf_op jit(solution)/shard_map/ppermute | solution.py:207
  166.2 12.6 %collective-permute-start.36 = (f32[2,8,2,128]{3,2,1,0:T(2,128)S(1)}, f32[2,8,2,128]{3,2,1,0:T(2,128)S(1)}, u32[]{:S(2)}, u32[]{:S(2)}) collective-permute-start(f32[2,8,2,128]{3,2,1,0:T(2,128)S(1)} %pad_maximum_fusion.7), channel_id=1, source_target_pairs={{0,2},{1,3},{2,0},{3,1},{4,6},{5,7},{6,4},{7,5},{8,10},{9,11},{10,... | collective-permute-start | bytes 49160 | tf_op jit(solution)/shard_map/ppermute | solution.py:207
  182.8 9.2 %collective-permute-start.31 = (bf16[2,1,128,1024]{3,2,1,0:T(8,128)(2,1)S(1)}, bf16[2,1,128,1024]{3,2,1,0:T(8,128)(2,1)S(1)}, u32[]{:S(2)}, u32[]{:S(2)}) collective-permute-start(bf16[2,1,128,1024]{3,2,1,0:T(8,128)(2,1)S(1)} %pad_maximum_fusion.5), channel_id=1, source_target_pairs={{0,2},{1,5},{2,0},{3,7},{4,6},{5,1},{6,4},{7,3},{8,10},{9,13},{10,... | collective-permute-start | bytes 1572872 | tf_op jit(solution)/shard_map/ppermute | solution.py:207
  184.3 11.0 %collective-permute-start.25 = (bf16[128,1024]{1,0:T(8,128)(2,1)S(1)}, bf16[128,1024]{1,0:T(8,128)(2,1)S(1)}, u32[]{:S(2)}, u32[]{:S(2)}) collective-permute-start(bf16[128,1024]{1,0:T(8,128)(2,1)S(1)} %fusion.1), channel_id=1, source_target_pairs={{0,24},{8,16},{16,8},{24,0},{1,25},{9,17},{17,9},{25,1},{2,26},{10... | collective-permute-start | bytes 786440 | tf_op jit(solution)/shard_map/ppermute | solution.py:210
  185.9 13.7 %collective-permute-start.29 = (bf16[128,1024]{1,0:T(8,128)(2,1)S(1)}, bf16[128,1024]{1,0:T(8,128)(2,1)S(1)}, u32[]{:S(2)}, u32[]{:S(2)}) collective-permute-start(bf16[128,1024]{1,0:T(8,128)(2,1)S(1)} %get-tuple-element.72), channel_id=1, source_target_pairs={{0,8},{8,0},{16,24},{24,16},{1,9},{9,1},{17,25},{25,17},{2,10},{10... | collective-permute-start | bytes 786440 | tf_op jit(solution)/shard_map/ppermute | solution.py:210
  192.0 15.1 %collective-permute-start.30 = (bf16[128,1024]{1,0:T(8,128)(2,1)S(1)}, bf16[128,1024]{1,0:T(8,128)(2,1)S(1)}, u32[]{:S(2)}, u32[]{:S(2)}) collective-permute-start(bf16[128,1024]{1,0:T(8,128)(2,1)S(1)} %get-tuple-element.73), channel_id=1, source_target_pairs={{0,16},{8,24},{16,0},{24,8},{1,17},{9,25},{17,1},{25,9},{2,18},{10... | collective-permute-start | bytes 786440 | tf_op jit(solution)/shard_map/ppermute | solution.py:210
  (40 other events, 237.0 us)

commit v4 on v3

v4 whole, which is shorter than its diff:
```python
import functools

import jax
import jax.numpy as jnp
from jax import lax
from jax.experimental import pallas as pl
from jax.experimental.pallas import tpu as pltpu
from jax.sharding import PartitionSpec as P

F32, BF16 = jnp.float32, jnp.bfloat16
ROWS_BY_ROWS = (((1,), (1,)), ((), ()))
BASE = 10 << 20
WEIGHT = 40


def call(kernel, name, grid, in_specs, out_specs, out_shape, operands, flops, limit, scratch=()):
    outs = out_shape if isinstance(out_shape, list) else [out_shape]
    moved = sum(x.size * x.dtype.itemsize for x in [*operands, *outs])
    return pl.pallas_call(
        kernel,
        grid_spec=pltpu.PrefetchScalarGridSpec(
            num_scalar_prefetch=1,
            grid=grid,
            in_specs=in_specs,
            out_specs=out_specs,
            scratch_shapes=scratch,
        ),
        out_shape=out_shape,
        compiler_params=pltpu.CompilerParams(vmem_limit_bytes=min(limit, 56 << 20)),
        cost_estimate=pl.CostEstimate(flops=WEIGHT * flops, bytes_accessed=moved, transcendentals=0),
        name=name,
    )(*operands)


def coefficient_kernel(capacity, topk, tokens, count, at_ref, *refs):
    lots, (gate_ref, up_ref, cg_ref, cu_ref, cr_ref, columns_ref) = refs[:count], refs[count:]
    experts, width, slots = gate_ref.shape
    span = lots[0].shape[3]

    @pl.when(pl.program_id(0) == 0)
    def _():
        before = lax.broadcasted_iota(jnp.int32, (tokens, tokens), 0)
        earlier = (before < lax.broadcasted_iota(jnp.int32, (tokens, tokens), 1)).astype(BF16)
        infos = [ref[j, 0].astype(F32) for ref in lots for j in range(ref.shape[0])]
        for b, info in enumerate(infos):

            def line(n):
                row, at = divmod(n * tokens, span)
                return info[row : row + 1, at : at + tokens]

            lines = lambda n: jnp.concatenate([line(n * topk + k) for k in range(topk)], axis=0)
            ids, prob = lines(0), lines(1) + lines(2)
            named, weight = [], []
            for e in range(experts):
                chosen = ids == (at_ref[1] + e).astype(F32)
                named.append(jnp.max(jnp.where(chosen, 1.0, 0.0), axis=0, keepdims=True))
                weight.append(jnp.sum(jnp.where(chosen, prob, 0.0), axis=0, keepdims=True))
            named = jnp.concatenate(named, axis=0)
            position = jnp.dot(named.astype(BF16), earlier, preferred_element_type=F32)
            slot = jnp.where(named > 0.0, position + (at_ref[2 + b] * capacity).astype(F32), -1.0)
            fill = jnp.zeros((8 - 2 * experts, tokens), F32)
            columns_ref[b * tokens : (b + 1) * tokens] = jnp.transpose(
                jnp.concatenate([slot, *weight, fill], axis=0)
            )

    rows = cg_ref.shape[0]
    columns = columns_ref[pl.ds(pl.multiple_of(pl.program_id(0) * rows, rows), rows)]
    number = lax.broadcasted_iota(jnp.int32, (rows, slots), 1).astype(F32)
    for e in range(experts):
        pick = jnp.where(columns[:, e : e + 1] == number, 1.0, 0.0).astype(BF16)
        g = lax.dot_general(pick, gate_ref[e], ROWS_BY_ROWS, preferred_element_type=F32)
        u = lax.dot_general(pick, up_ref[e], ROWS_BY_ROWS, preferred_element_type=F32)
        p = columns[:, experts + e : experts + e + 1]
        sg = 1.0 / (1.0 + jnp.exp(-g))
        silu = g * sg
        span = slice(e * width, (e + 1) * width)
        cg_ref[:, span] = (u * sg * (1.0 + g * (1.0 - sg)) * p).astype(BF16)
        cu_ref[:, span] = (silu * p).astype(BF16)
        cr_ref[:, span] = (silu * u).astype(BF16)


def coefficients(at, lots, tokens, topk, saved_gate, saved_up, capacity):
    experts, width, slots = saved_gate.shape
    blocks = sum(x.shape[0] for x in lots)
    tile = (4 if blocks % 4 == 0 else 1) * tokens
    total = blocks * tokens
    more = lots[0].shape[2] - tokens
    whole = pl.BlockSpec(saved_gate.shape, lambda i, at: (0, 0, 0))
    info = lambda x: pl.BlockSpec((x.shape[0], 1, more, x.shape[3]), lambda i, at: (0, 0, tokens // more, 0))
    out = pl.BlockSpec((tile, experts * width), lambda i, at: (i, 0))
    return call(
        functools.partial(coefficient_kernel, capacity, topk, tokens, len(lots)),
        "coefficients",
        (total // tile,),
        [*[info(x) for x in lots], whole, whole],
        [out] * 3,
        [jax.ShapeDtypeStruct((total, experts * width), BF16)] * 3,
        (at, *lots, saved_gate, saved_up),
        4 * total * slots * experts * width,
        2 * BASE,
        [pltpu.VMEM((total, 8), F32)],
    )


def products(plan, refs):
    sums = []
    for before, lots in plan:
        total = None if before is None else refs[before][...]
        for blocks, weights in lots:
            for k, weight in enumerate(weights):
                xs = [refs[i][:, k] for i in blocks]
                xs = [x.reshape(x.shape[0] * x.shape[1], x.shape[2]) for x in xs]
                x = xs[0] if len(xs) == 1 else jnp.concatenate(xs, axis=0)
                y = lax.dot_general(x, refs[weight][...], ROWS_BY_ROWS, preferred_element_type=F32)
                total = y if total is None else total + y
        sums.append(total)
    return sums


def early_kernel(plan, at_ref, *refs):
    for out_ref, h in zip(refs[len(refs) - len(plan) :], products(plan, refs)):
        out_ref[...] = h


def late_kernel(plan, experts, width, moves, at_ref, *refs):
    cg_ref, cu_ref, cr_ref, ag_ref, au_ref, info_ref, r_ref = refs[len(refs) - 7 :]
    total, tile = ag_ref.shape
    tokens = total // len(moves)

    @pl.when(pl.program_id(0) == 0)
    def _():
        r_ref[...] = jnp.zeros_like(r_ref)

    at = 0
    for h in products(plan, refs):
        rows = slice(at, at + h.shape[0])
        ag = (h * cg_ref[rows].astype(F32)).astype(BF16)
        au = (h * cu_ref[rows].astype(F32)).astype(BF16)
        terms = h * cr_ref[rows].astype(F32)
        for i in range(h.shape[0] // tokens):
            j = moves[at // tokens + i]
            to, of = slice(j * tokens, (j + 1) * tokens), slice(i * tokens, (i + 1) * tokens)
            ag_ref[to], au_ref[to] = ag[of], au[of]
        unit = pl.program_id(0) * tile + lax.broadcasted_iota(jnp.int32, terms.shape, 1)
        for e in range(experts):
            own = (unit >= e * width) & (unit < (e + 1) * width)
            r_ref[rows, e : e + 1] += jnp.sum(jnp.where(own, terms, 0.0), axis=1, keepdims=True)
        at += h.shape[0]

    @pl.when(pl.program_id(0) == pl.num_programs(0) - 1)
    def _():
        more, span = info_ref.shape[1:]
        per, count = span // tokens, experts * len(moves)
        for i, j in enumerate(moves):
            value = jnp.transpose(r_ref[i * tokens : (i + 1) * tokens])
            high = value.astype(BF16).astype(F32)
            parts = []
            for x in (high, value - high):
                for n in range(count):
                    own = [jnp.where(at_ref[1] + e == n, x[e : e + 1], 0.0) for e in range(experts)]
                    parts.append(functools.reduce(lambda p, q: p + q, own))
            parts += [jnp.zeros((1, tokens), F32)] * (more * per - len(parts))
            lines = [jnp.concatenate(parts[n : n + per], axis=1) for n in range(0, more * per, per)]
            info_ref[j] = jnp.concatenate(lines, axis=0).astype(BF16)


def tile_of(n):
    return 256 if n % 256 == 0 else 128 if n % 128 == 0 else n


def hidden(at, parts, tokens, w_down, coefs=None, experts=None, moves=None, more=None):
    units = w_down.shape[0]
    tile = tile_of(units)
    specs, operands, weights, plan, sizes, work, held = [], [], {}, [], [], 0, 0

    def operand(x, spec):
        operands.append(x)
        specs.append(spec)
        return len(operands) - 1

    for before, lots in parts:
        size = tokens * sum(b.shape[0] for b in lots[0][1])
        of = None
        if before is not None:
            of = operand(before, pl.BlockSpec((size, tile), lambda n, at: (0, n)))
        steps = []
        for first, blocks in lots:
            pieces, span = blocks[0].shape[1], blocks[0].shape[3]
            whole = lambda b: pl.BlockSpec((b.shape[0], pieces, tokens, span), lambda n, at: (0, 0, 0, 0))
            rows = [operand(b, whole(b)) for b in blocks]
            for i in range(first, first + pieces):
                if i not in weights:
                    weights[i] = operand(w_down, pl.BlockSpec((tile, span), lambda n, at, i=i: (n, at[0] ^ i)))
            steps.append((rows, [weights[i] for i in range(first, first + pieces)]))
            work += size * units * pieces * span
            held += 4 * size * pieces * span
        plan.append((of, steps))
        sizes.append(size)
    total = sum(sizes)
    limit = BASE + held + 16 * total * tile
    grid = (units // tile,)
    column = lambda n: pl.BlockSpec((n, tile), lambda n, at: (0, n))
    if coefs is None:
        out = [jax.ShapeDtypeStruct((n, units), F32) for n in sizes]
        kernel = functools.partial(early_kernel, plan)
        return call(
            kernel, "hidden_early", grid, specs, [column(n) for n in sizes], out, [at, *operands], work, limit
        )
    kernel = functools.partial(late_kernel, plan, experts, units // experts, moves)
    outs = [column(total), column(total), pl.BlockSpec((len(moves), more, span), lambda n, at: (0, 0, 0))]
    shapes = [jax.ShapeDtypeStruct((total, units), BF16)] * 2
    shapes.append(jax.ShapeDtypeStruct((len(moves), more, span), BF16))
    return call(
        kernel,
        "hidden_late",
        grid,
        specs + [column(total)] * 3,
        outs,
        shapes,
        [at, *operands, *coefs],
        work,
        limit,
        [pltpu.VMEM((total, 8), F32)],
    )


def expand_kernel(counts, adds, carries, at_ref, ag_ref, au_ref, wg_ref, wu_ref, *refs):
    other, refs = refs[: int(adds)], refs[int(adds) :]
    info, outs = refs[: int(carries)], refs[int(carries) :]
    width = outs[0].shape[3]
    rows = ag_ref.shape[0] // sum(counts)
    tile = tile_of(width)
    for at in range(0, width, tile):
        span = slice(at, at + tile)
        y = jnp.dot(ag_ref[...], wg_ref[:, span], preferred_element_type=F32)
        y = y + jnp.dot(au_ref[...], wu_ref[:, span], preferred_element_type=F32)
        i = 0
        for out, count in zip(outs, counts):
            for j in range(count):
                part = y[i * rows : (i + 1) * rows]
                if adds:
                    part = part + other[0][i, 0, :rows, span].astype(F32)
                out[j, 0, :rows, span] = part.astype(BF16)
                if carries:
                    part = info[0][i, :, span]
                    if adds:
                        part = (part.astype(F32) + other[0][i, 0, rows:, span].astype(F32)).astype(BF16)
                    out[j, 0, rows:, span] = part
                i += 1


def expand(at, first, pieces, part, ag, au, w_gate, w_up, sections, rows, counts, info=None, other=None):
    units = ag.shape[1]
    number = sum(counts)
    span = w_gate.shape[1] // sections
    half = max(span // 2, 128)
    per = span // half
    more = 0 if info is None else info.shape[1]
    some = pl.BlockSpec((number * rows, units), lambda k, j, at: (part, 0))
    weight = pl.BlockSpec((units, half), lambda k, j, at: (0, (at[0] ^ (first + k)) * per + j))
    block = lambda n: pl.BlockSpec((n, 1, rows + more, half), lambda k, j, at: (0, k, 0, j))
    specs, operands = [some, some, weight, weight], [at, ag, au, w_gate, w_up]
    if other is not None:
        specs, operands = specs + [block(number)], operands + [other]
    if info is not None:
        specs.append(pl.BlockSpec((number, more, half), lambda k, j, at: (part, 0, j)))
        operands.append(info)
    return call(
        functools.partial(expand_kernel, counts, other is not None, info is not None),
        "expand",
        (pieces, per),
        specs,
        [block(n) for n in counts],
        [jax.ShapeDtypeStruct((n, pieces, rows + more, span), BF16) for n in counts],
        operands,
        2 * number * rows * units * pieces * span,
        BASE + 8 * number * rows * units + 4 * number * rows * half,
    )


def small(kernel, name, out_shape, operands, specs=None, aliases=None, scratch=(), out_spec=None):
    specs = [pl.BlockSpec(memory_space=pltpu.VMEM)] * len(operands) if specs is None else specs
    return pl.pallas_call(
        kernel,
        in_specs=specs,
        out_specs=pl.BlockSpec(memory_space=pltpu.VMEM) if out_spec is None else out_spec,
        out_shape=out_shape,
        scratch_shapes=scratch,
        input_output_aliases=aliases or {},
        compiler_params=pltpu.CompilerParams(vmem_limit_bytes=BASE),
        cost_estimate=pl.CostEstimate(flops=WEIGHT << 29, bytes_accessed=1 << 20, transcendentals=0),
        name=name,
    )(*operands)


def join_kernel(counts, *refs):
    xs, out, sems = refs[: sum(counts)], refs[-2], refs[-1]
    copies, n = [], 0
    for i, count in enumerate(counts):
        for k in range(count):
            copies.append(pltpu.make_async_copy(xs[n].at[0, 0], out.at[i, k], sems.at[n]))
            n += 1
    for c in copies:
        c.start()
    for c in copies:
        c.wait()


def join(*rows):
    counts = [len(r) for r in rows]
    xs = [x for r in rows for x in r]
    somewhere = pl.BlockSpec(memory_space=pl.ANY)
    return small(
        functools.partial(join_kernel, counts),
        "join",
        jax.ShapeDtypeStruct((len(rows), counts[0], *xs[0].shape[2:]), xs[0].dtype),
        xs,
        specs=[somewhere] * len(xs),
        scratch=[pltpu.SemaphoreType.DMA((len(xs),))],
        out_spec=somewhere,
    )


def pass_on_kernel(two_ref, one_ref, out_ref):
    out_ref[0] = (two_ref[0].astype(F32) + one_ref[0].astype(F32)).astype(BF16)
    out_ref[1] = two_ref[1]


def pass_on(two, one):
    return small(pass_on_kernel, "pass_on", jax.ShapeDtypeStruct(two.shape, BF16), (two, one))


def finish_kernel(a_ref, b_ref, c_ref, out_ref):
    for k in range(out_ref.shape[0]):
        y = a_ref[0, k].astype(F32) + b_ref[0, k].astype(F32) + c_ref[0, k].astype(F32)
        out_ref[k] = y.astype(BF16)


def finish(a, b, c):
    return small(finish_kernel, "finish", jax.ShapeDtypeStruct(a.shape[1:], BF16), (a, b, c))


def add(*terms):
    return functools.reduce(lambda a, b: a + b, [t.astype(F32) for t in terms]).astype(BF16)


def after(x, *others):
    return lax.optimization_barrier((x, *others))[0]


def local(grad_out, probs, expert_ids, w_gate, w_up, w_down, saved_gate, saved_up):
    groups, sections = lax.axis_size("expert"), lax.axis_size("section")
    me, z = lax.axis_index("expert"), lax.axis_index("section")
    experts, units, features = w_gate.shape
    slots = saved_gate.shape[2]
    tokens, topk = expert_ids.shape
    span = grad_out.shape[1]
    square = groups == 8
    flat = lambda w: w.reshape(experts * units, features)
    w_gate, w_up, w_down = flat(w_gate), flat(w_up), flat(w_down)
    core = me % 2
    near = jnp.where(core == 0, 2, 4)
    far = 6 - near

    def swap(x, even, odd):
        return lax.ppermute(x, "expert", [(i, i ^ (even, odd)[i % 2]) for i in range(groups)])

    def across(x, by):
        return lax.ppermute(x, "section", [(i, i ^ by) for i in range(sections)])

    if square:
        owners = jnp.stack([me, me ^ 1, me ^ near, me ^ near ^ 1, me ^ 1 ^ far, me ^ far, me ^ 6, me ^ 7])
        moves = (0, 4, 1, 2, 5, 6, 3, 7)
    else:
        owners, moves = jnp.arange(groups), tuple(range(groups))

    high = lax.reduce_precision(probs, 8, 7)
    routing = jnp.concatenate([expert_ids.T.astype(F32), high.T, (probs - high).T], axis=0)
    lines = 3 * topk
    more = -(-lines * tokens // (16 * span)) * 16
    routing = jnp.pad(routing.reshape(-1), (0, more * span - lines * tokens)).reshape(more, span)
    own = jnp.concatenate([grad_out, routing.astype(BF16)], axis=0)[None, None]
    received = [None] + [across(grad_out[None], i) for i in (1, 2) if i < sections]
    if square:
        pair0 = join([own], [swap(own, 1, 1)])
        first0 = after(swap(pair0, 2, 4), *received[1:3])
        second0 = swap(first0[:1], 4, 2)
        lot0 = [pair0, first0, swap(first0, 1, 1), second0, swap(second0, 1, 1)]
    else:
        first0 = lax.all_gather(own, "expert", axis=0, tiled=True)
        lot0 = [first0]
    for i in range(3, sections):
        received.append(across(after(grad_out[None], received[i - 2]), i))

    at = jnp.concatenate([jnp.stack([z, me * experts]), owners]).astype(jnp.int32)
    gated = lambda at: coefficients(at, lot0, tokens, topk, saved_gate, saved_up, slots // groups)
    if square:
        got = [x[None] for x in received[1:3]]
        pair1 = join(got, [swap(x, 1, 1) for x in got])
        first1 = swap(pair1, 2, 4)
        coefs = gated(after(at, pair1))
        got = [after(x[None], coefs[0]) for x in received[3:]]
        theirs2 = [swap(x, 1, 1) for x in got]
        most, few = hidden(at, [(None, [(0, lot0[:3])]), (None, [(0, lot0[3:])])], tokens, after(w_down, coefs[0]))
        pair2 = join([after(got[0], most), *got[1:]], theirs2)
        first1 = after(first1, pair2)
        second1 = swap(first1[:1], 4, 2)
        first2 = swap(after(pair2, first1), 2, 4)
        lot1 = [pair1, first1, swap(first1, 1, 1)]
        (most,) = hidden(at, [(most, [(1, lot1)])], tokens, w_down)
        second1, first2 = after(second1, most), after(first2, most)
        second2 = swap(first2[:1], 4, 2)
        lot1 = [second1, swap(second1, 1, 1)]
        lot2 = [pair2, first2, swap(first2, 1, 1)], [second2, swap(second2, 1, 1)]
        parts = [(most, [(3, lot2[0])]), (few, [(1, lot1), (3, lot2[1])])]
    else:
        coefs = gated(at)
        gather = lambda xs: [lax.all_gather(jnp.stack(xs, axis=1), "expert", axis=0, tiled=True)]
        (h,) = hidden(at, [(None, [(0, lot0)])], tokens, w_down)
        (h,) = hidden(at, [(h, [(1, gather(received[1:3]))])], tokens, w_down)
        parts = [(h, [(3, gather(received[3:]))])]
    more = -(-2 * groups * experts * tokens // (16 * span)) * 16
    ag, au, info = hidden(at, parts, tokens, w_down, coefs, experts, moves, more)

    lots = ((3, sections), (2, 3), (1, 2), (0, 1))
    half = groups // 2
    last = [info]
    theirs, kept, sent, parts, routers = {}, {}, {}, {}, {}

    def run_expand(n, part, counts, other=None):
        a, b = lots[n]
        outs = expand(
            at, a, b - a, part, after(ag, *last), au, w_gate, w_up, sections, tokens, counts,
            info if n == 0 else None, other,
        )
        last[0] = outs[0]
        return outs

    def theirs_step(n):
        theirs[n] = swap(run_expand(n, 1, (half,))[0], 1, 1)

    def mine_step(n):
        alone, two, one = run_expand(n, 0, (1, 2, 1), theirs[n])
        kept[n] = alone, two, swap(one, 4, 2)

    def sent_step(n):
        _, two, one = kept[n]
        last[0] = pass_on(two, after(one, *last))
        sent[n] = swap(last[0], 2, 4)

    def hand_out(n, sums):
        a = lots[n][0]
        for k, x in enumerate(sums):
            parts[a + k] = x if a + k == 0 else across(x, a + k)
        if n == 0:
            routers[0] = sums[0][tokens:]
            routers.update({i: across(routers[0], i) for i in range(1, 3)})
            for i in range(3, sections):
                routers[i], parts[i] = parts[i][tokens:], parts[i][:tokens]

    def final_step(n):
        mine = sent[n][:1], swap(sent[n][1:], 1, 1)
        last[0] = finish(after(kept[n][0], *last), *mine)
        hand_out(n, list(last[0]))

    if square:
        for step, n in (
            (theirs_step, 0),
            (theirs_step, 1),
            (mine_step, 0),
            (theirs_step, 2),
            (sent_step, 0),
            (mine_step, 1),
            (theirs_step, 3),
            (sent_step, 1),
            (mine_step, 2),
            (final_step, 0),
            (sent_step, 2),
            (mine_step, 3),
            (final_step, 1),
            (sent_step, 3),
            (final_step, 2),
            (final_step, 3),
        ):
            step(n)
    else:
        for n in range(len(lots)):
            outs = run_expand(n, 0, (groups,))
            sums = lax.psum_scatter(outs[0], "expert", scatter_dimension=0, tiled=True)[0]
            hand_out(n, list(sums))
    grad_in = add(*parts.values())

    router = functools.reduce(lambda a, b: a + b, [r.astype(F32) for r in routers.values()])
    count = groups * experts
    router = jnp.sum(router.reshape(-1)[: 2 * count * tokens].reshape(2, count, tokens), axis=0)
    match = expert_ids[None] == jnp.arange(count)[:, None, None]
    grad_probs = jnp.sum(jnp.where(match, router[:, :, None], 0.0), axis=0).astype(BF16)
    return (grad_in, grad_probs)


def solution(mesh):
    placed = (
        P("expert", "section"),
        P("expert", None),
        P("expert", None),
        P("expert", "section", None),
        P("expert", "section", None),
        P("expert", "section", None),
        P("expert", "section", None),
        P("expert", "section", None),
    )
    return jax.shard_map(
        local,
        mesh=mesh,
        in_specs=placed,
        out_specs=(P("expert", "section"), P("expert", None)),
        check_vma=False,
    )
```

time: 209 us -> 155 us (0.74)
  local copies, waits for them, and re-layouts: 26.2 us -> 1.45 us
  waiting for transfers between devices: 81.6 us -> 62.6 us
  other arithmetic: 10.2 us -> 3.85 us
  Pallas kernels: 52.3 us -> 46.9 us
  starting transfers between devices: 36.7 us -> 38.8 us
    unnamed x71 -> x20, local copies, waits for them, and re-layouts: 19.4 us -> 0.06 us
    ppermute x30 -> x32, waiting for transfers between devices: 50.8 us -> 39.5 us  [swap(): lax.ppermute(x, 'expert', [(i, i ^ (even, odd)[i % 2]) for i in range(gro...]
    ppermute x8, waiting for transfers between devices: 30.8 us -> 23 us  [across(): return lax.ppermute(x, 'section', [(i, i ^ by) for i in range(sections)])]
    pallas_call x10 -> x12, Pallas kernels: 52.3 us -> 44.9 us  [call(): pl.pallas_call(kernel, grid_spec=pltpu.PrefetchScalarGridSpec(num_scalar_...]
    concatenate x7 -> x0, other arithmetic: 3.1 us -> none  [the longest x3 2.02 us: sent_step(): two = jnp.concatenate([add(two[:1], one), two[1:]])]
    convert_element_type x6 -> x1, other arithmetic: 3.88 us -> 0.87 us  [add(): functools.reduce(lambda a, b: a + b, [t.astype(F32) for t in terms])]
    ppermute x30 -> x32, starting transfers between devices: 20.9 us -> 21.7 us  [swap(): lax.ppermute(x, 'expert', [(i, i ^ (even, odd)[i % 2]) for i in range(gro...]
  transfers between devices with their start and end apart: 38 -> 40, of which waited for: 16 -> 17; matrix products, arithmetic and copies ran while one was open for 9% -> 1% of each run, Pallas kernels for 12% -> 24%
where the time goes in v4:
time: 155 us
  waiting for transfers between devices  62.6 us (40%)
  Pallas kernels  46.9 us (30%)
  starting transfers between devices  38.8 us (25%)
  other arithmetic  3.85 us (2%)
    pallas_call x12, Pallas kernels, call(): pl.pallas_call(kernel, grid_spec=pltpu.PrefetchScalarGridSpec(num_scalar_...  44.9 us
    ppermute x32, waiting for transfers between devices, swap(): lax.ppermute(x, 'expert', [(i, i ^ (even, odd)[i % 2]) for i in range(gro...  39.5 us
    ppermute x8, waiting for transfers between devices, across(): return lax.ppermute(x, 'section', [(i, i ^ by) for i in range(sections)])  23 us
    ppermute x32, starting transfers between devices, swap(): lax.ppermute(x, 'expert', [(i, i ^ (even, odd)[i % 2]) for i in range(gro...  21.7 us
    ppermute x8, starting transfers between devices, across(): return lax.ppermute(x, 'section', [(i, i ^ by) for i in range(sections)])  17.1 us
  transfers between devices with their start and end apart: 40, of which 17 were waited for; matrix products, arithmetic and copies ran while one was open for 1% of the time, Pallas kernels for 24%

profile of v4, /device:TPU:0, one launch (start us, length us, event | category | flops | bytes accessed | tf_op | source)
XLA Modules:
  0.0 154.7 jit_solution(5883910363088784702)
XLA Ops:
  4.9 2.9 %collective-permute-start.1 = (bf16[2,1,144,1024]{3,2,1,0:T(8,128)(2,1)S(1)}, bf16[2,1,144,1024]{3,2,1,0:T(8,128)(2,1)S(1)}, u32[]{:S(2)}, u32[]{:S(2)}) collective-permute-start(bf16[2,1,144,1024]{3,2,1,0:T(8,128)(2,1)S(1)} %join.3.refs_0_), channel_id=1, source_target_pairs={{0,2},{1,5},{2,0},{3,7},{4,6},{5,1},{6,4},{7,3},{8,10},{9,13},{10,... | collective-permute-start | bytes 1769480 | tf_op jit(solution)/shard_map/ppermute | solution.py:366
  12.0 9.4 %collective-permute-done.2 = bf16[1,128,1024]{2,1,0:T(8,128)(2,1)S(1)} collective-permute-done((bf16[1,128,1024]{2,1,0:T(8,128)(2,1)S(1)}, bf16[1,128,1024]{2,1,0:T(8,128)(2,1)S(1)}, u32[]{:S(2)}, u32[]{:S(2)}) %collective-permute-start.2) | collective-permute-done | bytes 262176 | tf_op jit(solution)/shard_map/ppermute | solution.py:369
  27.8 2.9 %collective-permute-done.7.refs_3_.refs_4_ = bf16[1,1,144,1024]{3,2,1,0:T(8,128)(2,1)S(1)} collective-permute-done((bf16[1,1,144,1024]{3,2,1,0:T(8,128)(2,1)S(1)}, bf16[1,1,144,1024]{3,2,1,0:T(8,128)(2,1)S(1)}, u32[]{:S(2)}, u32[]{:S(2)}) %collective-permute-start.7) | collective-permute-done | bytes 294944 | tf_op jit(solution)/shard_map/ppermute | solution.py:366
  33.3 5.1 %coefficients.1 = (bf16[1024,768]{1,0:T(8,128)(2,1)S(1)}, bf16[1024,768]{1,0:T(8,128)(2,1)S(1)}, bf16[1024,768]{1,0:T(8,128)(2,1)S(1)}) custom-call(s32[10]{0:T(128)S(1)} %concatenate.10.at_ref, bf16[2,1,144,1024]{3,2,1,0:T(8,128)(2,1)S(1)} %join.3.refs_0_, bf16[2,1,144,1024]{3,2,1,0:T(8,128)(2,1)S(1)} %collective-permute-done.1.refs_1_, ...), custom_call_target="tpu_custom_call" | custom-call | flops 96636764160 | bytes 9437224 | tf_op jit(solution)/shard_map/coefficients/pallas_call | solution.py:19
  38.6 3.3 %hidden_early.2 = (f32[768,768]{1,0:T(8,128)S(1)}, f32[256,768]{1,0:T(8,128)S(1)}) custom-call(s32[10]{0:T(128)S(1)} %concatenate.10.at_ref, bf16[2,1,144,1024]{3,2,1,0:T(8,128)(2,1)S(1)} %join.3.refs_0_, bf16[2,1,144,1024]{3,2,1,0:T(8,128)(2,1)S(1)} %collective-permute-done.1.refs_1_, bf16[2,1,144,1024]{3,2,1,0:T(8,128)(2,1)S(1)} %collective-permute-done.4.refs_2_, ...), custom_call_target="tpu_custom_call" | custom-call | flops 32212254720 | bytes 11796520 | tf_op jit(solution)/shard_map/hidden_early/pallas_call | solution.py:19
  42.0 5.0 %collective-permute-done.9.refs_2_ = bf16[2,2,128,1024]{3,2,1,0:T(8,128)(2,1)} collective-permute-done((bf16[2,2,128,1024]{3,2,1,0:T(8,128)(2,1)}, bf16[2,2,128,1024]{3,2,1,0:T(8,128)(2,1)}, u32[]{:S(2)}, u32[]{:S(2)}) %collective-permute-start.9) | collective-permute-done | bytes 1048608 | tf_op jit(solution)/shard_map/ppermute | solution.py:366
  50.1 6.0 %hidden_early.3.refs_0_ = f32[768,768]{1,0:T(8,128)S(1)} custom-call(s32[10]{0:T(128)S(1)} %concatenate.10.at_ref, f32[768,768]{1,0:T(8,128)S(1)} %get-tuple-element.52.refs_0_, bf16[2,2,128,1024]{3,2,1,0:T(8,128)(2,1)} %join.4.refs_1_, bf16[2,2,128,1024]{3,2,1,0:T(8,128)(2,1)} %collective-permute-done.9.refs_2_, ...), custom_call_target="tpu_custom_call" | custom-call | flops 48318382080 | bytes 20447272 | tf_op jit(solution)/shard_map/hidden_early/pallas_call | solution.py:19
  56.1 6.1 %collective-permute-done.15.refs_6_ = bf16[1,2,128,1024]{3,2,1,0:T(8,128)(2,1)S(1)} collective-permute-done((bf16[1,2,128,1024]{3,2,1,0:T(8,128)(2,1)S(1)}, bf16[1,2,128,1024]{3,2,1,0:T(8,128)(2,1)S(1)}, u32[]{:S(2)}, u32[]{:S(2)}) %collective-permute-start.15) | collective-permute-done | bytes 524320 | tf_op jit(solution)/shard_map/ppermute | solution.py:366
  64.5 4.4 %collective-permute-done.17.refs_10_ = bf16[1,1,128,1024]{3,2,1,0:T(8,128)(2,1)S(1)} collective-permute-done((bf16[1,1,128,1024]{3,2,1,0:T(8,128)(2,1)S(1)}, bf16[1,1,128,1024]{3,2,1,0:T(8,128)(2,1)S(1)}, u32[]{:S(2)}, u32[]{:S(2)}) %collective-permute-start.17) | collective-permute-done | bytes 262176 | tf_op jit(solution)/shard_map/ppermute | solution.py:366
  70.4 6.9 %hidden_late.1 = (bf16[1024,768]{1,0:T(8,128)(2,1)S(1)}, bf16[1024,768]{1,0:T(8,128)(2,1)S(1)}, bf16[8,16,1024]{2,1,0:T(8,128)(2,1)S(1)}) custom-call(s32[10]{0:T(128)S(1)} %concatenate.10.at_ref, f32[768,768]{1,0:T(8,128)S(1)} %hidden_early.3.refs_0_, bf16[2,1,128,1024]{3,2,1,0:T(8,128)(2,1)S(1)} %join.5.refs_1_, ...), custom_call_target="tpu_custom_call" | custom-call | flops 48318382080 | bytes 33292328 | tf_op jit(solution)/shard_map/hidden_late/pallas_call | solution.py:19
  77.3 2.9 %expand.8 = bf16[4,1,144,1024]{3,2,1,0:T(8,128)(2,1)S(1)} custom-call(s32[10]{0:T(128)S(1)} %concatenate.10.at_ref, bf16[1024,768]{1,0:T(8,128)(2,1)S(1)} %get-tuple-element.86.ag_ref, bf16[1024,768]{1,0:T(8,128)(2,1)S(1)} %get-tuple-element.66.au_ref, bf16[768,4096]{1,0:T(8,128)(2,1)S(1)} %bitcast.46, bf16[768,4096]{1,0:T(8,128)(2,1)S(1)} %bitcast.56, ...), custom_call_target="tpu_custom_call" | custom-call | flops 32212254720 | bytes 17170472 | tf_op jit(solution)/shard_map/expand/pallas_call | solution.py:19
  80.4 2.9 %expand.9 = bf16[4,1,128,1024]{3,2,1,0:T(8,128)(2,1)S(1)} custom-call(s32[10]{0:T(128)S(1)} %concatenate.10.at_ref, bf16[1024,768]{1,0:T(8,128)(2,1)S(1)} %get-tuple-element.86.ag_ref, bf16[1024,768]{1,0:T(8,128)(2,1)S(1)} %get-tuple-element.66.au_ref, bf16[768,4096]{1,0:T(8,128)(2,1)S(1)} %bitcast.47, bf16[768,4096]{1,0:T(8,128)(2,1)S(1)} %bitcast.57), custom_call_target="tpu_custom_call" | custom-call | flops 32212254720 | bytes 16777256 | tf_op jit(solution)/shard_map/expand/pallas_call | solution.py:19
  83.8 3.0 %expand.10 = (bf16[1,1,144,1024]{3,2,1,0:T(8,128)(2,1)S(1)}, bf16[2,1,144,1024]{3,2,1,0:T(8,128)(2,1)S(1)}, bf16[1,1,144,1024]{3,2,1,0:T(8,128)(2,1)S(1)}) custom-call(s32[10]{0:T(128)S(1)} %concatenate.10.at_ref, bf16[1024,768]{1,0:T(8,128)(2,1)S(1)} %get-tuple-element.86.ag_ref, bf16[1024,768]{1,0:T(8,128)(2,1)S(1)} %get-tuple-element.66.au_ref, ...), custom_call_target="tpu_custom_call" | custom-call | flops 32212254720 | bytes 18350120 | tf_op jit(solution)/shard_map/expand/pallas_call | solution.py:19
  87.3 2.9 %expand.11 = bf16[4,1,128,1024]{3,2,1,0:T(8,128)(2,1)S(1)} custom-call(s32[10]{0:T(128)S(1)} %concatenate.10.at_ref, bf16[1024,768]{1,0:T(8,128)(2,1)S(1)} %get-tuple-element.86.ag_ref, bf16[1024,768]{1,0:T(8,128)(2,1)S(1)} %get-tuple-element.66.au_ref, bf16[768,4096]{1,0:T(8,128)(2,1)S(1)} %bitcast.49, bf16[768,4096]{1,0:T(8,128)(2,1)S(1)} %bitcast.59), custom_call_target="tpu_custom_call" | custom-call | flops 32212254720 | bytes 16777256 | tf_op jit(solution)/shard_map/expand/pallas_call | solution.py:19
  95.5 3.0 %expand.12 = (bf16[1,1,128,1024]{3,2,1,0:T(8,128)(2,1)S(1)}, bf16[2,1,128,1024]{3,2,1,0:T(8,128)(2,1)S(1)}, bf16[1,1,128,1024]{3,2,1,0:T(8,128)(2,1)S(1)}) custom-call(s32[10]{0:T(128)S(1)} %concatenate.10.at_ref, bf16[1024,768]{1,0:T(8,128)(2,1)S(1)} %get-tuple-element.86.ag_ref, bf16[1024,768]{1,0:T(8,128)(2,1)S(1)} %get-tuple-element.66.au_ref, ...), custom_call_target="tpu_custom_call" | custom-call | flops 32212254720 | bytes 17825832 | tf_op jit(solution)/shard_map/expand/pallas_call | solution.py:19
  99.0 3.1 %expand.13 = bf16[4,1,128,1024]{3,2,1,0:T(8,128)(2,1)S(1)} custom-call(s32[10]{0:T(128)S(1)} %concatenate.10.at_ref, bf16[1024,768]{1,0:T(8,128)(2,1)S(1)} %get-tuple-element.86.ag_ref, bf16[1024,768]{1,0:T(8,128)(2,1)S(1)} %get-tuple-element.66.au_ref, bf16[768,4096]{1,0:T(8,128)(2,1)S(1)} %bitcast.51, bf16[768,4096]{1,0:T(8,128)(2,1)S(1)} %bitcast.61), custom_call_target="tpu_custom_call" | custom-call | flops 32212254720 | bytes 16777256 | tf_op jit(solution)/shard_map/expand/pallas_call | solution.py:19
  102.2 2.7 %collective-permute-done.22.one_ref = bf16[1,1,128,1024]{3,2,1,0:T(8,128)(2,1)S(1)} collective-permute-done((bf16[1,1,128,1024]{3,2,1,0:T(8,128)(2,1)S(1)}, bf16[1,1,128,1024]{3,2,1,0:T(8,128)(2,1)S(1)}, u32[]{:S(2)}, u32[]{:S(2)}) %collective-permute-start.22) | collective-permute-done | bytes 262176 | tf_op jit(solution)/shard_map/ppermute | solution.py:366
  106.7 3.0 %expand.14 = (bf16[1,1,128,1024]{3,2,1,0:T(8,128)(2,1)S(1)}, bf16[2,1,128,1024]{3,2,1,0:T(8,128)(2,1)S(1)}, bf16[1,1,128,1024]{3,2,1,0:T(8,128)(2,1)S(1)}) custom-call(s32[10]{0:T(128)S(1)} %concatenate.10.at_ref, bf16[1024,768]{1,0:T(8,128)(2,1)S(1)} %get-tuple-element.86.ag_ref, bf16[1024,768]{1,0:T(8,128)(2,1)S(1)} %get-tuple-element.66.au_ref, ...), custom_call_target="tpu_custom_call" | custom-call | flops 32212254720 | bytes 17825832 | tf_op jit(solution)/shard_map/expand/pallas_call | solution.py:19
  110.3 5.2 %collective-permute-done.29 = bf16[2,1,128,1024]{3,2,1,0:T(8,128)(2,1)S(1)} collective-permute-done((bf16[2,1,128,1024]{3,2,1,0:T(8,128)(2,1)S(1)}, bf16[2,1,128,1024]{3,2,1,0:T(8,128)(2,1)S(1)}, u32[]{:S(2)}, u32[]{:S(2)}) %collective-permute-start.29) | collective-permute-done | bytes 524320 | tf_op jit(solution)/shard_map/ppermute | solution.py:366
  122.0 3.0 %expand.15 = (bf16[1,1,128,1024]{3,2,1,0:T(8,128)(2,1)S(1)}, bf16[2,1,128,1024]{3,2,1,0:T(8,128)(2,1)S(1)}, bf16[1,1,128,1024]{3,2,1,0:T(8,128)(2,1)S(1)}) custom-call(s32[10]{0:T(128)S(1)} %concatenate.10.at_ref, bf16[1024,768]{1,0:T(8,128)(2,1)S(1)} %get-tuple-element.86.ag_ref, bf16[1024,768]{1,0:T(8,128)(2,1)S(1)} %get-tuple-element.66.au_ref, ...), custom_call_target="tpu_custom_call" | custom-call | flops 32212254720 | bytes 17825832 | tf_op jit(solution)/shard_map/expand/pallas_call | solution.py:19
  125.6 4.0 %collective-permute-done.26 = bf16[144,1024]{1,0:T(8,128)(2,1)S(1)} collective-permute-done((bf16[144,1024]{1,0:T(8,128)(2,1)S(1)}, bf16[144,1024]{1,0:T(8,128)(2,1)S(1)}, u32[]{:S(2)}, u32[]{:S(2)}) %collective-permute-start.26) | collective-permute-done | bytes 294944 | tf_op jit(solution)/shard_map/ppermute | solution.py:369
  129.6 5.9 %collective-permute-start.31 = (bf16[128,1024]{1,0:T(8,128)(2,1)S(1)}, bf16[128,1024]{1,0:T(8,128)(2,1)S(1)}, u32[]{:S(2)}, u32[]{:S(2)}) collective-permute-start(bf16[128,1024]{1,0:T(8,128)(2,1)S(1)} %bitcast.68), channel_id=1, source_target_pairs={{0,16},{8,24},{16,0},{24,8},{1,17},{9,25},{17,1},{25,9},{2,18},{10... | collective-permute-start | bytes 786440 | tf_op jit(solution)/shard_map/ppermute | solution.py:369
  138.0 6.8 %collective-permute-done.36 = bf16[2,1,128,1024]{3,2,1,0:T(8,128)(2,1)S(1)} collective-permute-done((bf16[2,1,128,1024]{3,2,1,0:T(8,128)(2,1)S(1)}, bf16[2,1,128,1024]{3,2,1,0:T(8,128)(2,1)S(1)}, u32[]{:S(2)}, u32[]{:S(2)}) %collective-permute-start.36) | collective-permute-done | bytes 524320 | tf_op jit(solution)/shard_map/ppermute | solution.py:366
  147.1 6.7 %collective-permute-done.35 = bf16[128,1024]{1,0:T(8,128)(2,1)S(1)} collective-permute-done((bf16[128,1024]{1,0:T(8,128)(2,1)S(1)}, bf16[128,1024]{1,0:T(8,128)(2,1)S(1)}, u32[]{:S(2)}, u32[]{:S(2)}) %collective-permute-start.35) | collective-permute-done | bytes 262176 | tf_op jit(solution)/shard_map/ppermute | solution.py:369
  (123 shorter events, 46.8 us)
Async XLA Ops:
  4.9 18.9 %collective-permute-start.1 = (bf16[2,1,144,1024]{3,2,1,0:T(8,128)(2,1)S(1)}, bf16[2,1,144,1024]{3,2,1,0:T(8,128)(2,1)S(1)}, u32[]{:S(2)}, u32[]{:S(2)}) collective-permute-start(bf16[2,1,144,1024]{3,2,1,0:T(8,128)(2,1)S(1)} %join.3.refs_0_), channel_id=1, source_target_pairs={{0,2},{1,5},{2,0},{3,7},{4,6},{5,1},{6,4},{7,3},{8,10},{9,13},{10,... | collective-permute-start | bytes 1769480 | tf_op jit(solution)/shard_map/ppermute | solution.py:366
  7.8 13.6 %collective-permute-start.2 = (bf16[1,128,1024]{2,1,0:T(8,128)(2,1)S(1)}, bf16[1,128,1024]{2,1,0:T(8,128)(2,1)S(1)}, u32[]{:S(2)}, u32[]{:S(2)}) collective-permute-start(bf16[1,128,1024]{2,1,0:T(8,128)(2,1)S(1)} %bitcast.72), channel_id=1, source_target_pairs={{0,8},{8,0},{16,24},{24,16},{1,9},{9,1},{17,25},{25,17},{2,10},{10... | collective-permute-start | bytes 786440 | tf_op jit(solution)/shard_map/ppermute | solution.py:369
  9.4 14.4 %collective-permute-start.3 = (bf16[1,128,1024]{2,1,0:T(8,128)(2,1)S(1)}, bf16[1,128,1024]{2,1,0:T(8,128)(2,1)S(1)}, u32[]{:S(2)}, u32[]{:S(2)}) collective-permute-start(bf16[1,128,1024]{2,1,0:T(8,128)(2,1)S(1)} %bitcast.73), channel_id=1, source_target_pairs={{0,16},{8,24},{16,0},{24,8},{1,17},{9,25},{17,1},{25,9},{2,18},{10... | collective-permute-start | bytes 786440 | tf_op jit(solution)/shard_map/ppermute | solution.py:369
  25.0 13.5 %collective-permute-start.10 = (bf16[1,128,1024]{2,1,0:T(8,128)(2,1)S(1)}, bf16[1,128,1024]{2,1,0:T(8,128)(2,1)S(1)}, u32[]{:S(2)}, u32[]{:S(2)}) collective-permute-start(bf16[1,128,1024]{2,1,0:T(8,128)(2,1)S(1)} %bitcast.74), channel_id=1, source_target_pairs={{0,24},{8,16},{16,8},{24,0},{1,25},{9,17},{17,9},{25,1},{2,26},{10... | collective-permute-start | bytes 786440 | tf_op jit(solution)/shard_map/ppermute | solution.py:369
  31.7 15.2 %collective-permute-start.9 = (bf16[2,2,128,1024]{3,2,1,0:T(8,128)(2,1)}, bf16[2,2,128,1024]{3,2,1,0:T(8,128)(2,1)}, u32[]{:S(2)}, u32[]{:S(2)}) collective-permute-start(bf16[2,2,128,1024]{3,2,1,0:T(8,128)(2,1)} %join.4.refs_1_), channel_id=1, source_target_pairs={{0,2},{1,5},{2,0},{3,7},{4,6},{5,1},{6,4},{7,3},{8,10},{9,13},{10,... | collective-permute-start | bytes 3145736 | tf_op jit(solution)/shard_map/ppermute | solution.py:366
  48.0 14.2 %collective-permute-start.15 = (bf16[1,2,128,1024]{3,2,1,0:T(8,128)(2,1)S(1)}, bf16[1,2,128,1024]{3,2,1,0:T(8,128)(2,1)S(1)}, u32[]{:S(2)}, u32[]{:S(2)}) collective-permute-start(bf16[1,2,128,1024]{3,2,1,0:T(8,128)(2,1)S(1)} %slice.50), channel_id=1, source_target_pairs={{0,4},{1,3},{2,6},{3,1},{4,0},{5,7},{6,2},{7,5},{8,12},{9,11},{10,... | collective-permute-start | bytes 1572872 | tf_op jit(solution)/shard_map/ppermute | solution.py:366
  48.6 13.8 %collective-permute-start.13 = (bf16[2,1,128,1024]{3,2,1,0:T(8,128)(2,1)S(1)}, bf16[2,1,128,1024]{3,2,1,0:T(8,128)(2,1)S(1)}, u32[]{:S(2)}, u32[]{:S(2)}) collective-permute-start(bf16[2,1,128,1024]{3,2,1,0:T(8,128)(2,1)S(1)} %join.5.refs_1_), channel_id=1, source_target_pairs={{0,2},{1,5},{2,0},{3,7},{4,6},{5,1},{6,4},{7,3},{8,10},{9,13},{10,... | collective-permute-start | bytes 1572872 | tf_op jit(solution)/shard_map/ppermute | solution.py:366
  83.3 12.1 %collective-permute-start.21 = (bf16[4,1,128,1024]{3,2,1,0:T(8,128)(2,1)S(1)}, bf16[4,1,128,1024]{3,2,1,0:T(8,128)(2,1)S(1)}, u32[]{:S(2)}, u32[]{:S(2)}) collective-permute-start(bf16[4,1,128,1024]{3,2,1,0:T(8,128)(2,1)S(1)} %expand.9), channel_id=1, source_target_pairs={{0,1},{1,0},{2,3},{3,2},{4,5},{5,4},{6,7},{7,6},{8,9},{9,8},{10,11... | collective-permute-start | bytes 3145736 | tf_op jit(solution)/shard_map/ppermute | solution.py:366
  90.2 16.5 %collective-permute-start.23 = (bf16[4,1,128,1024]{3,2,1,0:T(8,128)(2,1)S(1)}, bf16[4,1,128,1024]{3,2,1,0:T(8,128)(2,1)S(1)}, u32[]{:S(2)}, u32[]{:S(2)}) collective-permute-start(bf16[4,1,128,1024]{3,2,1,0:T(8,128)(2,1)S(1)} %expand.11), channel_id=1, source_target_pairs={{0,1},{1,0},{2,3},{3,2},{4,5},{5,4},{6,7},{7,6},{8,9},{9,8},{10,11... | collective-permute-start | bytes 3145736 | tf_op jit(solution)/shard_map/ppermute | solution.py:366
  93.6 13.0 %collective-permute-start.24 = (bf16[2,1,144,1024]{3,2,1,0:T(8,128)(2,1)S(1)}, bf16[2,1,144,1024]{3,2,1,0:T(8,128)(2,1)S(1)}, u32[]{:S(2)}, u32[]{:S(2)}) collective-permute-start(bf16[2,1,144,1024]{3,2,1,0:T(8,128)(2,1)S(1)} %pass_on.4), channel_id=1, source_target_pairs={{0,2},{1,5},{2,0},{3,7},{4,6},{5,1},{6,4},{7,3},{8,10},{9,13},{10,... | collective-permute-start | bytes 1769480 | tf_op jit(solution)/shard_map/ppermute | solution.py:366
  102.1 18.2 %collective-permute-start.28 = (bf16[4,1,128,1024]{3,2,1,0:T(8,128)(2,1)S(1)}, bf16[4,1,128,1024]{3,2,1,0:T(8,128)(2,1)S(1)}, u32[]{:S(2)}, u32[]{:S(2)}) collective-permute-start(bf16[4,1,128,1024]{3,2,1,0:T(8,128)(2,1)S(1)} %expand.13), channel_id=1, source_target_pairs={{0,1},{1,0},{2,3},{3,2},{4,5},{5,4},{6,7},{7,6},{8,9},{9,8},{10,11... | collective-permute-start | bytes 3145736 | tf_op jit(solution)/shard_map/ppermute | solution.py:366
  105.0 10.5 %collective-permute-start.29 = (bf16[2,1,128,1024]{3,2,1,0:T(8,128)(2,1)S(1)}, bf16[2,1,128,1024]{3,2,1,0:T(8,128)(2,1)S(1)}, u32[]{:S(2)}, u32[]{:S(2)}) collective-permute-start(bf16[2,1,128,1024]{3,2,1,0:T(8,128)(2,1)S(1)} %pass_on.5), channel_id=1, source_target_pairs={{0,2},{1,5},{2,0},{3,7},{4,6},{5,1},{6,4},{7,3},{8,10},{9,13},{10,... | collective-permute-start | bytes 1572872 | tf_op jit(solution)/shard_map/ppermute | solution.py:366
  106.7 8.9 %collective-permute-start.25 = (bf16[1,1,144,1024]{3,2,1,0:T(8,128)(2,1)S(1)}, bf16[1,1,144,1024]{3,2,1,0:T(8,128)(2,1)S(1)}, u32[]{:S(2)}, u32[]{:S(2)}) collective-permute-start(bf16[1,1,144,1024]{3,2,1,0:T(8,128)(2,1)S(1)} %get-tuple-element.94), channel_id=1, source_target_pairs={{0,1},{1,0},{2,3},{3,2},{4,5},{5,4},{6,7},{7,6},{8,9},{9,8},{10,11... | collective-permute-start | bytes 884744 | tf_op jit(solution)/shard_map/ppermute | solution.py:366
  109.7 9.1 %collective-permute-start.27 = (bf16[1,1,128,1024]{3,2,1,0:T(8,128)(2,1)S(1)}, bf16[1,1,128,1024]{3,2,1,0:T(8,128)(2,1)S(1)}, u32[]{:S(2)}, u32[]{:S(2)}) collective-permute-start(bf16[1,1,128,1024]{3,2,1,0:T(8,128)(2,1)S(1)} %get-tuple-element.84), channel_id=1, source_target_pairs={{0,4},{1,3},{2,6},{3,1},{4,0},{5,7},{6,2},{7,5},{8,12},{9,11},{10,... | collective-permute-start | bytes 786440 | tf_op jit(solution)/shard_map/ppermute | solution.py:366
  115.5 9.4 %collective-permute-start.30 = (bf16[1,1,128,1024]{3,2,1,0:T(8,128)(2,1)S(1)}, bf16[1,1,128,1024]{3,2,1,0:T(8,128)(2,1)S(1)}, u32[]{:S(2)}, u32[]{:S(2)}) collective-permute-start(bf16[1,1,128,1024]{3,2,1,0:T(8,128)(2,1)S(1)} %get-tuple-element.100), channel_id=1, source_target_pairs={{0,1},{1,0},{2,3},{3,2},{4,5},{5,4},{6,7},{7,6},{8,9},{9,8},{10,11... | collective-permute-start | bytes 786440 | tf_op jit(solution)/shard_map/ppermute | solution.py:366
  115.7 21.5 %collective-permute-start.38 = (bf16[16,1024]{1,0:T(8,128)(2,1)S(1)}, bf16[16,1024]{1,0:T(8,128)(2,1)S(1)}, u32[]{:S(2)}, u32[]{:S(2)}) collective-permute-start(bf16[16,1024]{1,0:T(8,128)(2,1)S(1)} %slice_bitcast_fusion), channel_id=1, source_target_pairs={{0,8},{8,0},{16,24},{24,16},{1,9},{9,1},{17,25},{25,17},{2,10},{10... | collective-permute-start | bytes 98312 | tf_op jit(solution)/shard_map/ppermute | solution.py:369
  116.3 21.0 %collective-permute-start.39 = (bf16[16,1024]{1,0:T(8,128)(2,1)S(1)}, bf16[16,1024]{1,0:T(8,128)(2,1)S(1)}, u32[]{:S(2)}, u32[]{:S(2)}) collective-permute-start(bf16[16,1024]{1,0:T(8,128)(2,1)S(1)} %slice_bitcast_fusion), channel_id=1, source_target_pairs={{0,16},{8,24},{16,0},{24,8},{1,17},{9,25},{17,1},{25,9},{2,18},{10... | collective-permute-start | bytes 98312 | tf_op jit(solution)/shard_map/ppermute | solution.py:369
  118.9 10.7 %collective-permute-start.26 = (bf16[144,1024]{1,0:T(8,128)(2,1)S(1)}, bf16[144,1024]{1,0:T(8,128)(2,1)S(1)}, u32[]{:S(2)}, u32[]{:S(2)}) collective-permute-start(bf16[144,1024]{1,0:T(8,128)(2,1)S(1)} %bitcast.35), channel_id=1, source_target_pairs={{0,24},{8,16},{16,8},{24,0},{1,25},{9,17},{17,9},{25,1},{2,26},{10... | collective-permute-start | bytes 884744 | tf_op jit(solution)/shard_map/ppermute | solution.py:369
  120.3 17.0 %collective-permute-start.33 = (bf16[2,1,128,1024]{3,2,1,0:T(8,128)(2,1)S(1)}, bf16[2,1,128,1024]{3,2,1,0:T(8,128)(2,1)S(1)}, u32[]{:S(2)}, u32[]{:S(2)}) collective-permute-start(bf16[2,1,128,1024]{3,2,1,0:T(8,128)(2,1)S(1)} %pass_on.6), channel_id=1, source_target_pairs={{0,2},{1,5},{2,0},{3,7},{4,6},{5,1},{6,4},{7,3},{8,10},{9,13},{10,... | collective-permute-start | bytes 1572872 | tf_op jit(solution)/shard_map/ppermute | solution.py:366
  124.9 10.6 %collective-permute-start.32 = (bf16[1,1,128,1024]{3,2,1,0:T(8,128)(2,1)S(1)}, bf16[1,1,128,1024]{3,2,1,0:T(8,128)(2,1)S(1)}, u32[]{:S(2)}, u32[]{:S(2)}) collective-permute-start(bf16[1,1,128,1024]{3,2,1,0:T(8,128)(2,1)S(1)} %get-tuple-element.90), channel_id=1, source_target_pairs={{0,4},{1,3},{2,6},{3,1},{4,0},{5,7},{6,2},{7,5},{8,12},{9,11},{10,... | collective-permute-start | bytes 786440 | tf_op jit(solution)/shard_map/ppermute | solution.py:366
  129.6 17.5 %collective-permute-start.31 = (bf16[128,1024]{1,0:T(8,128)(2,1)S(1)}, bf16[128,1024]{1,0:T(8,128)(2,1)S(1)}, u32[]{:S(2)}, u32[]{:S(2)}) collective-permute-start(bf16[128,1024]{1,0:T(8,128)(2,1)S(1)} %bitcast.68), channel_id=1, source_target_pairs={{0,16},{8,24},{16,0},{24,8},{1,17},{9,25},{17,1},{25,9},{2,18},{10... | collective-permute-start | bytes 786440 | tf_op jit(solution)/shard_map/ppermute | solution.py:369
  135.6 9.2 %collective-permute-start.36 = (bf16[2,1,128,1024]{3,2,1,0:T(8,128)(2,1)S(1)}, bf16[2,1,128,1024]{3,2,1,0:T(8,128)(2,1)S(1)}, u32[]{:S(2)}, u32[]{:S(2)}) collective-permute-start(bf16[2,1,128,1024]{3,2,1,0:T(8,128)(2,1)S(1)} %pass_on.7), channel_id=1, source_target_pairs={{0,2},{1,5},{2,0},{3,7},{4,6},{5,1},{6,4},{7,3},{8,10},{9,13},{10,... | collective-permute-start | bytes 1572872 | tf_op jit(solution)/shard_map/ppermute | solution.py:366
  137.3 7.6 %collective-permute-start.34 = (bf16[1,1,128,1024]{3,2,1,0:T(8,128)(2,1)S(1)}, bf16[1,1,128,1024]{3,2,1,0:T(8,128)(2,1)S(1)}, u32[]{:S(2)}, u32[]{:S(2)}) collective-permute-start(bf16[1,1,128,1024]{3,2,1,0:T(8,128)(2,1)S(1)} %get-tuple-element.98), channel_id=1, source_target_pairs={{0,1},{1,0},{2,3},{3,2},{4,5},{5,4},{6,7},{7,6},{8,9},{9,8},{10,11... | collective-permute-start | bytes 786440 | tf_op jit(solution)/shard_map/ppermute | solution.py:366
  145.1 8.8 %collective-permute-start.35 = (bf16[128,1024]{1,0:T(8,128)(2,1)S(1)}, bf16[128,1024]{1,0:T(8,128)(2,1)S(1)}, u32[]{:S(2)}, u32[]{:S(2)}) collective-permute-start(bf16[128,1024]{1,0:T(8,128)(2,1)S(1)} %bitcast.71), channel_id=1, source_target_pairs={{0,8},{8,0},{16,24},{24,16},{1,9},{9,1},{17,25},{25,17},{2,10},{10... | collective-permute-start | bytes 786440 | tf_op jit(solution)/shard_map/ppermute | solution.py:369
  (26 other events, 211.5 us)

commit v5 on v4

--- a/solution.py
+++ b/solution.py
@@ -10,7 +10,7 @@
 F32, BF16 = jnp.float32, jnp.bfloat16
 ROWS_BY_ROWS = (((1,), (1,)), ((), ()))
 BASE = 10 << 20
-WEIGHT = 40
+WEIGHT = 16
 
 
 def call(kernel, name, grid, in_specs, out_specs, out_shape, operands, flops, limit, scratch=()):
@@ -32,24 +32,17 @@
     )(*operands)
 
 
-def coefficient_kernel(capacity, topk, tokens, count, at_ref, *refs):
-    lots, (gate_ref, up_ref, cg_ref, cu_ref, cr_ref, columns_ref) = refs[:count], refs[count:]
+def coefficient_kernel(capacity, topk, at_ref, info_ref, gate_ref, up_ref, cg_ref, cu_ref, cr_ref, columns_ref):
     experts, width, slots = gate_ref.shape
-    span = lots[0].shape[3]
+    blocks, _, tokens = info_ref.shape
 
     @pl.when(pl.program_id(0) == 0)
     def _():
         before = lax.broadcasted_iota(jnp.int32, (tokens, tokens), 0)
         earlier = (before < lax.broadcasted_iota(jnp.int32, (tokens, tokens), 1)).astype(BF16)
-        infos = [ref[j, 0].astype(F32) for ref in lots for j in range(ref.shape[0])]
-        for b, info in enumerate(infos):
-
-            def line(n):
-                row, at = divmod(n * tokens, span)
-                return info[row : row + 1, at : at + tokens]
-
-            lines = lambda n: jnp.concatenate([line(n * topk + k) for k in range(topk)], axis=0)
-            ids, prob = lines(0), lines(1) + lines(2)
+        for b in range(blocks):
+            info = info_ref[at_ref[2 + blocks + b]]
+            ids, prob = info[:topk], info[topk:]
             named, weight = [], []
             for e in range(experts):
                 chosen = ids == (at_ref[1] + e).astype(F32)
@@ -79,23 +72,21 @@
         cr_ref[:, span] = (silu * u).astype(BF16)
 
 
-def coefficients(at, lots, tokens, topk, saved_gate, saved_up, capacity):
+def coefficients(at, info, topk, saved_gate, saved_up, capacity):
     experts, width, slots = saved_gate.shape
-    blocks = sum(x.shape[0] for x in lots)
+    blocks, _, tokens = info.shape
     tile = (4 if blocks % 4 == 0 else 1) * tokens
     total = blocks * tokens
-    more = lots[0].shape[2] - tokens
-    whole = pl.BlockSpec(saved_gate.shape, lambda i, at: (0, 0, 0))
-    info = lambda x: pl.BlockSpec((x.shape[0], 1, more, x.shape[3]), lambda i, at: (0, 0, tokens // more, 0))
+    whole = lambda x: pl.BlockSpec(x.shape, lambda i, at: (0, 0, 0))
     out = pl.BlockSpec((tile, experts * width), lambda i, at: (i, 0))
     return call(
-        functools.partial(coefficient_kernel, capacity, topk, tokens, len(lots)),
+        functools.partial(coefficient_kernel, capacity, topk),
         "coefficients",
         (total // tile,),
-        [*[info(x) for x in lots], whole, whole],
+        [whole(info), whole(saved_gate), whole(saved_up)],
         [out] * 3,
         [jax.ShapeDtypeStruct((total, experts * width), BF16)] * 3,
-        (at, *lots, saved_gate, saved_up),
+        (at, info, saved_gate, saved_up),
         4 * total * slots * experts * width,
         2 * BASE,
         [pltpu.VMEM((total, 8), F32)],
@@ -278,7 +269,7 @@
     )
 
 
-def small(kernel, name, out_shape, operands, specs=None, aliases=None, scratch=(), out_spec=None):
+def small(kernel, name, out_shape, operands, specs=None, scratch=(), out_spec=None, flops=1 << 30):
     specs = [pl.BlockSpec(memory_space=pltpu.VMEM)] * len(operands) if specs is None else specs
     return pl.pallas_call(
         kernel,
@@ -286,9 +277,8 @@
         out_specs=pl.BlockSpec(memory_space=pltpu.VMEM) if out_spec is None else out_spec,
         out_shape=out_shape,
         scratch_shapes=scratch,
-        input_output_aliases=aliases or {},
         compiler_params=pltpu.CompilerParams(vmem_limit_bytes=BASE),
-        cost_estimate=pl.CostEstimate(flops=WEIGHT << 29, bytes_accessed=1 << 20, transcendentals=0),
+        cost_estimate=pl.CostEstimate(flops=flops, bytes_accessed=0, transcendentals=0),
         name=name,
     )(*operands)
 
@@ -318,6 +308,7 @@
         specs=[somewhere] * len(xs),
         scratch=[pltpu.SemaphoreType.DMA((len(xs),))],
         out_spec=somewhere,
+        flops=0,
     )
 
 
@@ -330,14 +321,20 @@
     return small(pass_on_kernel, "pass_on", jax.ShapeDtypeStruct(two.shape, BF16), (two, one))
 
 
-def finish_kernel(a_ref, b_ref, c_ref, out_ref):
+def finish_kernel(a_ref, b_ref, c_ref, *refs):
+    extra, out_ref = refs[:-1], refs[-1]
+    rows = a_ref.shape[2]
     for k in range(out_ref.shape[0]):
         y = a_ref[0, k].astype(F32) + b_ref[0, k].astype(F32) + c_ref[0, k].astype(F32)
-        out_ref[k] = y.astype(BF16)
-
-
-def finish(a, b, c):
-    return small(finish_kernel, "finish", jax.ShapeDtypeStruct(a.shape[1:], BF16), (a, b, c))
+        out_ref[k, :rows] = y.astype(BF16)
+        if extra:
+            out_ref[k, rows:] = extra[0][...]
+
+
+def finish(a, b, c, *extra):
+    more = extra[0].shape[0] if extra else 0
+    shape = (a.shape[1], a.shape[2] + more, a.shape[3])
+    return small(finish_kernel, "finish", jax.ShapeDtypeStruct(shape, BF16), (a, b, c, *extra))
 
 
 def add(*terms):
@@ -374,50 +371,44 @@
     else:
         owners, moves = jnp.arange(groups), tuple(range(groups))
 
-    high = lax.reduce_precision(probs, 8, 7)
-    routing = jnp.concatenate([expert_ids.T.astype(F32), high.T, (probs - high).T], axis=0)
-    lines = 3 * topk
-    more = -(-lines * tokens // (16 * span)) * 16
-    routing = jnp.pad(routing.reshape(-1), (0, more * span - lines * tokens)).reshape(more, span)
-    own = jnp.concatenate([grad_out, routing.astype(BF16)], axis=0)[None, None]
-    received = [None] + [across(grad_out[None], i) for i in (1, 2) if i < sections]
+    piece = grad_out[None, None]
+    received = [piece] + [across(piece, i) for i in (1, 2) if i < sections]
+    for i in range(3, sections):
+        received.append(across(after(piece, *received[1:3]), i))
+    info = jnp.concatenate([expert_ids.T.astype(F32), probs.T], axis=0)[None]
     if square:
-        pair0 = join([own], [swap(own, 1, 1)])
-        first0 = after(swap(pair0, 2, 4), *received[1:3])
-        second0 = swap(first0[:1], 4, 2)
-        lot0 = [pair0, first0, swap(first0, 1, 1), second0, swap(second0, 1, 1)]
+        for bit in (2, 4, 1):
+            info = jnp.concatenate([info, swap(info, bit, bit)], axis=0)
+        place = owners ^ me
+        place = place // 2 + place % 2 * 4
     else:
-        first0 = lax.all_gather(own, "expert", axis=0, tiled=True)
-        lot0 = [first0]
-    for i in range(3, sections):
-        received.append(across(after(grad_out[None], received[i - 2]), i))
-
-    at = jnp.concatenate([jnp.stack([z, me * experts]), owners]).astype(jnp.int32)
-    gated = lambda at: coefficients(at, lot0, tokens, topk, saved_gate, saved_up, slots // groups)
+        info = lax.all_gather(info, "expert", axis=0, tiled=True)
+        place = owners
+    at = jnp.concatenate([jnp.stack([z, me * experts]), owners, place]).astype(jnp.int32)
+    gated = lambda at: coefficients(at, info, topk, saved_gate, saved_up, slots // groups)
     if square:
-        got = [x[None] for x in received[1:3]]
-        pair1 = join(got, [swap(x, 1, 1) for x in got])
+        sibs = [swap(x, 1, 1) for x in received[:3]]
+        pair1 = join([after(piece, info), *received[1:3]], sibs)
         first1 = swap(pair1, 2, 4)
         coefs = gated(after(at, pair1))
-        got = [after(x[None], coefs[0]) for x in received[3:]]
-        theirs2 = [swap(x, 1, 1) for x in got]
-        most, few = hidden(at, [(None, [(0, lot0[:3])]), (None, [(0, lot0[3:])])], tokens, after(w_down, coefs[0]))
-        pair2 = join([after(got[0], most), *got[1:]], theirs2)
+        got = [after(x, coefs[0]) for x in received[3:]]
+        pair2 = join(got, [swap(x, 1, 1) for x in got])
         first1 = after(first1, pair2)
         second1 = swap(first1[:1], 4, 2)
         first2 = swap(after(pair2, first1), 2, 4)
         lot1 = [pair1, first1, swap(first1, 1, 1)]
-        (most,) = hidden(at, [(most, [(1, lot1)])], tokens, w_down)
-        second1, first2 = after(second1, most), after(first2, most)
+        (most,) = hidden(at, [(None, [(0, lot1)])], tokens, after(w_down, coefs[0]))
+        second1, first2, _ = lax.optimization_barrier((second1, first2, most))
         second2 = swap(first2[:1], 4, 2)
         lot1 = [second1, swap(second1, 1, 1)]
+        (few,) = hidden(at, [(None, [(0, lot1)])], tokens, w_down)
+        second2 = after(second2, few)
         lot2 = [pair2, first2, swap(first2, 1, 1)], [second2, swap(second2, 1, 1)]
-        parts = [(most, [(3, lot2[0])]), (few, [(1, lot1), (3, lot2[1])])]
+        parts = [(most, [(3, lot2[0])]), (few, [(3, lot2[1])])]
     else:
         coefs = gated(at)
-        gather = lambda xs: [lax.all_gather(jnp.stack(xs, axis=1), "expert", axis=0, tiled=True)]
-        (h,) = hidden(at, [(None, [(0, lot0)])], tokens, w_down)
-        (h,) = hidden(at, [(h, [(1, gather(received[1:3]))])], tokens, w_down)
+        gather = lambda xs: [lax.all_gather(jnp.concatenate(xs, axis=1), "expert", axis=0, tiled=True)]
+        (h,) = hidden(at, [(None, [(0, gather(received[:3]))])], tokens, w_down)
         parts = [(h, [(3, gather(received[3:]))])]
     more = -(-2 * groups * experts * tokens // (16 * span)) * 16
     ag, au, info = hidden(at, parts, tokens, w_down, coefs, experts, moves, more)
@@ -451,16 +442,24 @@
     def hand_out(n, sums):
         a = lots[n][0]
         for k, x in enumerate(sums):
-            parts[a + k] = x if a + k == 0 else across(x, a + k)
+            if a + k == 0:
+                parts[0] = x
+                continue
+            if n == 0 and k == 0:
+                routers[0] = x[tokens:]
+            x = across(x, a + k)
+            parts[a + k] = x[:tokens]
+            if n == 0:
+                routers[a + k] = x[tokens:]
         if n == 0:
-            routers[0] = sums[0][tokens:]
-            routers.update({i: across(routers[0], i) for i in range(1, 3)})
-            for i in range(3, sections):
-                routers[i], parts[i] = parts[i][tokens:], parts[i][:tokens]
+            routers.update({i: across(routers[0], i) for i in range(1, 3) if i < sections})
+
+    def receive_step(n):
+        got = after(sent[n], *last)
+        sent[n] = got[:1], swap(got[1:], 1, 1)
 
     def final_step(n):
-        mine = sent[n][:1], swap(sent[n][1:], 1, 1)
-        last[0] = finish(after(kept[n][0], *last), *mine)
+        last[0] = finish(after(kept[n][0], *last), *sent[n])
         hand_out(n, list(last[0]))
 
     if square:
@@ -468,23 +467,27 @@
             (theirs_step, 0),
             (theirs_step, 1),
             (mine_step, 0),
+            (mine_step, 1),
+            (sent_step, 0),
             (theirs_step, 2),
-            (sent_step, 0),
-            (mine_step, 1),
             (theirs_step, 3),
             (sent_step, 1),
             (mine_step, 2),
+            (mine_step, 3),
+            (receive_step, 0),
+            (sent_step, 2),
             (final_step, 0),
-            (sent_step, 2),
-            (mine_step, 3),
+            (receive_step, 1),
             (final_step, 1),
+            (receive_step, 2),
             (sent_step, 3),
+            (receive_step, 3),
             (final_step, 2),
             (final_step, 3),
         ):
             step(n)
     else:
-        for n in range(len(lots)):
+        for n, (a, b) in enumerate(lots):
             outs = run_expand(n, 0, (groups,))
             sums = lax.psum_scatter(outs[0], "expert", scatter_dimension=0, tiled=True)[0]
             hand_out(n, list(sums))

time: 155 us -> 143 us (0.923)
  waiting for transfers between devices: 62.6 us -> 55.3 us
  Pallas kernels: 46.9 us -> 43.5 us
  starting transfers between devices: 38.8 us -> 35.8 us
  local copies, waits for them, and re-layouts: 1.45 us -> 4.06 us
    ppermute x8, waiting for transfers between devices: 23 us -> 11.3 us  [across(): return lax.ppermute(x, 'section', [(i, i ^ by) for i in range(sections)])]
    ppermute x32 -> x31, waiting for transfers between devices: 39.5 us -> 44 us  [swap(): lax.ppermute(x, 'expert', [(i, i ^ (even, odd)[i % 2]) for i in range(gro...]
    unnamed x20, local copies, waits for them, and re-layouts: 0.06 us -> 3.65 us
    pallas_call x12, Pallas kernels: 44.9 us -> 42.6 us  [call(): pl.pallas_call(kernel, grid_spec=pltpu.PrefetchScalarGridSpec(num_scalar_...]
    ppermute x8, starting transfers between devices: 17.1 us -> 15 us  [across(): return lax.ppermute(x, 'section', [(i, i ^ by) for i in range(sections)])]
    ppermute x32 -> x31, starting transfers between devices: 21.7 us -> 20.7 us  [swap(): lax.ppermute(x, 'expert', [(i, i ^ (even, odd)[i % 2]) for i in range(gro...]
  transfers between devices with their start and end apart: 40 -> 39, of which waited for: 17 -> 19; matrix products, arithmetic and copies ran while one was open for 1% -> 2% of each run, Pallas kernels for 24% -> 24%
where the time goes in v5:
time: 143 us
  waiting for transfers between devices  55.3 us (39%)
  Pallas kernels  43.5 us (30%)
  starting transfers between devices  35.8 us (25%)
  local copies, waits for them, and re-layouts  4.06 us (3%)
  other arithmetic  2.89 us (2%)
    ppermute x31, waiting for transfers between devices, swap(): lax.ppermute(x, 'expert', [(i, i ^ (even, odd)[i % 2]) for i in range(gro...  44 us
    pallas_call x12, Pallas kernels, call(): pl.pallas_call(kernel, grid_spec=pltpu.PrefetchScalarGridSpec(num_scalar_...  42.6 us
    ppermute x31, starting transfers between devices, swap(): lax.ppermute(x, 'expert', [(i, i ^ (even, odd)[i % 2]) for i in range(gro...  20.7 us
    ppermute x8, starting transfers between devices, across(): return lax.ppermute(x, 'section', [(i, i ^ by) for i in range(sections)])  15 us
    ppermute x8, waiting for transfers between devices, across(): return lax.ppermute(x, 'section', [(i, i ^ by) for i in range(sections)])  11.3 us
    unnamed x20, local copies, waits for them, and re-layouts  3.65 us
  transfers between devices with their start and end apart: 39, of which 19 were waited for; matrix products, arithmetic and copies ran while one was open for 2% of the time, Pallas kernels for 24%

profile of v5, /device:TPU:0, one launch (start us, length us, event | category | flops | bytes accessed | tf_op | source)
XLA Modules:
  0.0 142.6 jit_solution(5058549722381487662)
XLA Ops:
  0.6 3.1 %collective-permute-start.3 = (bf16[1,1,128,1024]{3,2,1,0:T(8,128)(2,1)}, bf16[1,1,128,1024]{3,2,1,0:T(8,128)(2,1)S(1)}, u32[]{:S(2)}, u32[]{:S(2)}) collective-permute-start(bf16[1,1,128,1024]{3,2,1,0:T(8,128)(2,1)} %bitcast.27), channel_id=1, source_target_pairs={{0,8},{8,0},{16,24},{24,16},{1,9},{9,1},{17,25},{25,17},{2,10},{10... | collective-permute-start | bytes 786440 | tf_op jit(solution)/shard_map/ppermute | solution.py:366
  3.7 2.6 %collective-permute-start.4 = (bf16[1,1,128,1024]{3,2,1,0:T(8,128)(2,1)}, bf16[1,1,128,1024]{3,2,1,0:T(8,128)(2,1)S(1)}, u32[]{:S(2)}, u32[]{:S(2)}) collective-permute-start(bf16[1,1,128,1024]{3,2,1,0:T(8,128)(2,1)} %bitcast.28), channel_id=1, source_target_pairs={{0,16},{8,24},{16,0},{24,8},{1,17},{9,25},{17,1},{25,9},{2,18},{10... | collective-permute-start | bytes 786440 | tf_op jit(solution)/shard_map/ppermute | solution.py:366
  9.2 2.2 %collective-permute-done = f32[1,16,128]{2,1,0:T(8,128)S(1)} collective-permute-done((f32[1,16,128]{2,1,0:T(8,128)S(1)}, f32[1,16,128]{2,1,0:T(8,128)S(1)}, u32[]{:S(2)}, u32[]{:S(2)}) %collective-permute-start) | collective-permute-done | bytes 8224 | tf_op jit(solution)/shard_map/ppermute | solution.py:363
  15.7 2.5 %collective-permute-done.4.refs_2_ = bf16[1,1,128,1024]{3,2,1,0:T(8,128)(2,1)S(1)} collective-permute-done((bf16[1,1,128,1024]{3,2,1,0:T(8,128)(2,1)}, bf16[1,1,128,1024]{3,2,1,0:T(8,128)(2,1)S(1)}, u32[]{:S(2)}, u32[]{:S(2)}) %collective-permute-start.4) | collective-permute-done | bytes 262176 | tf_op jit(solution)/shard_map/ppermute | solution.py:366
  18.4 2.5 %collective-permute-start.9 = (bf16[1,1,128,1024]{3,2,1,0:T(8,128)(2,1)}, bf16[1,1,128,1024]{3,2,1,0:T(8,128)(2,1)S(1)}, u32[]{:S(2)}, u32[]{:S(2)}) collective-permute-start(bf16[1,1,128,1024]{3,2,1,0:T(8,128)(2,1)} %bitcast.30), channel_id=1, source_target_pairs={{0,24},{8,16},{16,8},{24,0},{1,25},{9,17},{17,9},{25,1},{2,26},{10... | collective-permute-start | bytes 786440 | tf_op jit(solution)/shard_map/ppermute | solution.py:366
  26.3 5.1 %coefficients.1 = (bf16[1024,768]{1,0:T(8,128)(2,1)S(1)}, bf16[1024,768]{1,0:T(8,128)(2,1)S(1)}, bf16[1024,768]{1,0:T(8,128)(2,1)S(1)}) custom-call(s32[18]{0:T(128)S(1)} %concatenate.18.at_ref, f32[8,16,128]{2,1,0:T(8,128)S(1)} %pad_maximum_fusion.info_ref, bf16[2,384,768]{2,1,0:T(8,128)(2,1)S(1)} %copy-done.1, bf16[2,384,768]{2,1,0:T(8,128)(2,1)S(1)} %copy-done.2), custom_call_target="tpu_custom_call" | custom-call | flops 38654705664 | bytes 7143496 | tf_op jit(solution)/shard_map/coefficients/pallas_call | solution.py:19
  33.1 9.5 %collective-permute-done.8.refs_1_ = bf16[2,3,128,1024]{3,2,1,0:T(8,128)(2,1)S(1)} collective-permute-done((bf16[2,3,128,1024]{3,2,1,0:T(8,128)(2,1)S(1)}, bf16[2,3,128,1024]{3,2,1,0:T(8,128)(2,1)S(1)}, u32[]{:S(2)}, u32[]{:S(2)}) %collective-permute-start.8) | collective-permute-done | bytes 1572896 | tf_op jit(solution)/shard_map/ppermute | solution.py:363
  46.0 5.4 %hidden_early.2.refs_0_ = f32[768,768]{1,0:T(8,128)S(1)} custom-call(s32[18]{0:T(128)S(1)} %concatenate.18.at_ref, bf16[2,3,128,1024]{3,2,1,0:T(8,128)(2,1)S(1)} %join.2.refs_0_, bf16[2,3,128,1024]{3,2,1,0:T(8,128)(2,1)S(1)} %collective-permute-done.8.refs_1_, bf16[2,3,128,1024]{3,2,1,0:T(8,128)(2,1)S(1)} %collective-permute-done.11.refs_2_, ...), custom_call_target="tpu_custom_call" | custom-call | flops 28991029248 | bytes 25952328 | tf_op jit(solution)/shard_map/hidden_early/pallas_call | solution.py:19
  51.4 5.4 %collective-permute-done.13.refs_2_ = bf16[2,1,128,1024]{3,2,1,0:T(8,128)(2,1)S(1)} collective-permute-done((bf16[2,1,128,1024]{3,2,1,0:T(8,128)(2,1)S(1)}, bf16[2,1,128,1024]{3,2,1,0:T(8,128)(2,1)S(1)}, u32[]{:S(2)}, u32[]{:S(2)}) %collective-permute-start.13) | collective-permute-done | bytes 524320 | tf_op jit(solution)/shard_map/ppermute | solution.py:363
  56.8 3.1 %collective-permute-done.12.refs_0_ = bf16[1,3,128,1024]{3,2,1,0:T(8,128)(2,1)S(1)} collective-permute-done((bf16[1,3,128,1024]{3,2,1,0:T(8,128)(2,1)S(1)}, bf16[1,3,128,1024]{3,2,1,0:T(8,128)(2,1)S(1)}, u32[]{:S(2)}, u32[]{:S(2)}) %collective-permute-start.12) | collective-permute-done | bytes 786464 | tf_op jit(solution)/shard_map/ppermute | solution.py:363
  62.2 2.8 %hidden_early.3.refs_5_ = f32[256,768]{1,0:T(8,128)S(1)} custom-call(s32[18]{0:T(128)S(1)} %concatenate.18.at_ref, bf16[1,3,128,1024]{3,2,1,0:T(8,128)(2,1)S(1)} %collective-permute-done.12.refs_0_, bf16[1,3,128,1024]{3,2,1,0:T(8,128)(2,1)S(1)} %collective-permute-done.15.refs_1_, bf16[768,4096]{1,0:T(8,128)(2,1)S(1)} %bitcast.38, ...), custom_call_target="tpu_custom_call" | custom-call | flops 9663676416 | bytes 21233736 | tf_op jit(solution)/shard_map/hidden_early/pallas_call | solution.py:19
  68.4 5.7 %hidden_late.1 = (bf16[1024,768]{1,0:T(8,128)(2,1)S(1)}, bf16[1024,768]{1,0:T(8,128)(2,1)S(1)}, bf16[8,16,1024]{2,1,0:T(8,128)(2,1)S(1)}) custom-call(s32[18]{0:T(128)S(1)} %concatenate.18.at_ref, f32[768,768]{1,0:T(8,128)S(1)} %hidden_early.2.refs_0_, bf16[2,1,128,1024]{3,2,1,0:T(8,128)(2,1)S(1)} %join.3.refs_1_, ...), custom_call_target="tpu_custom_call" | custom-call | flops 12884901888 | bytes 19660872 | tf_op jit(solution)/shard_map/hidden_late/pallas_call | solution.py:19
  74.2 2.9 %expand.8 = bf16[4,1,144,1024]{3,2,1,0:T(8,128)(2,1)S(1)} custom-call(s32[18]{0:T(128)S(1)} %concatenate.18.at_ref, bf16[1024,768]{1,0:T(8,128)(2,1)S(1)} %get-tuple-element.84.ag_ref, bf16[1024,768]{1,0:T(8,128)(2,1)S(1)} %get-tuple-element.66.au_ref, bf16[768,4096]{1,0:T(8,128)(2,1)S(1)} %bitcast.44, bf16[768,4096]{1,0:T(8,128)(2,1)S(1)} %bitcast.54, ...), custom_call_target="tpu_custom_call" | custom-call | flops 12884901888 | bytes 17170504 | tf_op jit(solution)/shard_map/expand/pallas_call | solution.py:19
  77.3 2.9 %expand.9 = bf16[4,1,128,1024]{3,2,1,0:T(8,128)(2,1)S(1)} custom-call(s32[18]{0:T(128)S(1)} %concatenate.18.at_ref, bf16[1024,768]{1,0:T(8,128)(2,1)S(1)} %get-tuple-element.84.ag_ref, bf16[1024,768]{1,0:T(8,128)(2,1)S(1)} %get-tuple-element.66.au_ref, bf16[768,4096]{1,0:T(8,128)(2,1)S(1)} %bitcast.45, bf16[768,4096]{1,0:T(8,128)(2,1)S(1)} %bitcast.55), custom_call_target="tpu_custom_call" | custom-call | flops 12884901888 | bytes 16777288 | tf_op jit(solution)/shard_map/expand/pallas_call | solution.py:19
  80.6 3.0 %expand.10 = (bf16[1,1,144,1024]{3,2,1,0:T(8,128)(2,1)S(1)}, bf16[2,1,144,1024]{3,2,1,0:T(8,128)(2,1)S(1)}, bf16[1,1,144,1024]{3,2,1,0:T(8,128)(2,1)S(1)}) custom-call(s32[18]{0:T(128)S(1)} %concatenate.18.at_ref, bf16[1024,768]{1,0:T(8,128)(2,1)S(1)} %get-tuple-element.84.ag_ref, bf16[1024,768]{1,0:T(8,128)(2,1)S(1)} %get-tuple-element.66.au_ref, ...), custom_call_target="tpu_custom_call" | custom-call | flops 12884901888 | bytes 18350152 | tf_op jit(solution)/shard_map/expand/pallas_call | solution.py:19
  85.2 3.0 %expand.11 = (bf16[1,1,128,1024]{3,2,1,0:T(8,128)(2,1)S(1)}, bf16[2,1,128,1024]{3,2,1,0:T(8,128)(2,1)S(1)}, bf16[1,1,128,1024]{3,2,1,0:T(8,128)(2,1)S(1)}) custom-call(s32[18]{0:T(128)S(1)} %concatenate.18.at_ref, bf16[1024,768]{1,0:T(8,128)(2,1)S(1)} %get-tuple-element.84.ag_ref, bf16[1024,768]{1,0:T(8,128)(2,1)S(1)} %get-tuple-element.66.au_ref, ...), custom_call_target="tpu_custom_call" | custom-call | flops 12884901888 | bytes 17825864 | tf_op jit(solution)/shard_map/expand/pallas_call | solution.py:19
  90.5 2.9 %expand.12 = bf16[4,1,128,1024]{3,2,1,0:T(8,128)(2,1)S(1)} custom-call(s32[18]{0:T(128)S(1)} %concatenate.18.at_ref, bf16[1024,768]{1,0:T(8,128)(2,1)S(1)} %get-tuple-element.84.ag_ref, bf16[1024,768]{1,0:T(8,128)(2,1)S(1)} %get-tuple-element.66.au_ref, bf16[768,4096]{1,0:T(8,128)(2,1)S(1)} %bitcast.48, bf16[768,4096]{1,0:T(8,128)(2,1)S(1)} %bitcast.58), custom_call_target="tpu_custom_call" | custom-call | flops 12884901888 | bytes 16777288 | tf_op jit(solution)/shard_map/expand/pallas_call | solution.py:19
  95.0 2.9 %expand.13 = bf16[4,1,128,1024]{3,2,1,0:T(8,128)(2,1)S(1)} custom-call(s32[18]{0:T(128)S(1)} %concatenate.18.at_ref, bf16[1024,768]{1,0:T(8,128)(2,1)S(1)} %get-tuple-element.84.ag_ref, bf16[1024,768]{1,0:T(8,128)(2,1)S(1)} %get-tuple-element.66.au_ref, bf16[768,4096]{1,0:T(8,128)(2,1)S(1)} %bitcast.49, bf16[768,4096]{1,0:T(8,128)(2,1)S(1)} %bitcast.59), custom_call_target="tpu_custom_call" | custom-call | flops 12884901888 | bytes 16777288 | tf_op jit(solution)/shard_map/expand/pallas_call | solution.py:19
  99.7 3.0 %expand.14 = (bf16[1,1,128,1024]{3,2,1,0:T(8,128)(2,1)S(1)}, bf16[2,1,128,1024]{3,2,1,0:T(8,128)(2,1)S(1)}, bf16[1,1,128,1024]{3,2,1,0:T(8,128)(2,1)S(1)}) custom-call(s32[18]{0:T(128)S(1)} %concatenate.18.at_ref, bf16[1024,768]{1,0:T(8,128)(2,1)S(1)} %get-tuple-element.84.ag_ref, bf16[1024,768]{1,0:T(8,128)(2,1)S(1)} %get-tuple-element.66.au_ref, ...), custom_call_target="tpu_custom_call" | custom-call | flops 12884901888 | bytes 17825864 | tf_op jit(solution)/shard_map/expand/pallas_call | solution.py:19
  102.7 3.2 %expand.15 = (bf16[1,1,128,1024]{3,2,1,0:T(8,128)(2,1)S(1)}, bf16[2,1,128,1024]{3,2,1,0:T(8,128)(2,1)S(1)}, bf16[1,1,128,1024]{3,2,1,0:T(8,128)(2,1)S(1)}) custom-call(s32[18]{0:T(128)S(1)} %concatenate.18.at_ref, bf16[1024,768]{1,0:T(8,128)(2,1)S(1)} %get-tuple-element.84.ag_ref, bf16[1024,768]{1,0:T(8,128)(2,1)S(1)} %get-tuple-element.66.au_ref, ...), custom_call_target="tpu_custom_call" | custom-call | flops 12884901888 | bytes 17825864 | tf_op jit(solution)/shard_map/expand/pallas_call | solution.py:19
  106.6 5.7 %collective-permute-done.23.one_ref = bf16[1,1,128,1024]{3,2,1,0:T(8,128)(2,1)S(1)} collective-permute-done((bf16[1,1,128,1024]{3,2,1,0:T(8,128)(2,1)S(1)}, bf16[1,1,128,1024]{3,2,1,0:T(8,128)(2,1)S(1)}, u32[]{:S(2)}, u32[]{:S(2)}) %collective-permute-start.23) | collective-permute-done | bytes 262176 | tf_op jit(solution)/shard_map/ppermute | solution.py:363
  116.2 6.4 %collective-permute-done.31.one_ref = bf16[1,1,128,1024]{3,2,1,0:T(8,128)(2,1)S(1)} collective-permute-done((bf16[1,1,128,1024]{3,2,1,0:T(8,128)(2,1)S(1)}, bf16[1,1,128,1024]{3,2,1,0:T(8,128)(2,1)S(1)}, u32[]{:S(2)}, u32[]{:S(2)}) %collective-permute-start.31) | collective-permute-done | bytes 262176 | tf_op jit(solution)/shard_map/ppermute | solution.py:363
  126.6 3.4 %collective-permute-start.30 = (bf16[128,1024]{1,0:T(8,128)(2,1)S(1)}, bf16[128,1024]{1,0:T(8,128)(2,1)S(1)}, u32[]{:S(2)}, u32[]{:S(2)}) collective-permute-start(bf16[128,1024]{1,0:T(8,128)(2,1)S(1)} %bitcast.62), channel_id=1, source_target_pairs={{0,16},{8,24},{16,0},{24,8},{1,17},{9,25},{17,1},{25,9},{2,18},{10... | collective-permute-start | bytes 786440 | tf_op jit(solution)/shard_map/ppermute | solution.py:366
  133.6 8.1 %collective-permute-done.30 = bf16[128,1024]{1,0:T(8,128)(2,1)S(1)} collective-permute-done((bf16[128,1024]{1,0:T(8,128)(2,1)S(1)}, bf16[128,1024]{1,0:T(8,128)(2,1)S(1)}, u32[]{:S(2)}, u32[]{:S(2)}) %collective-permute-start.30) | collective-permute-done | bytes 262176 | tf_op jit(solution)/shard_map/ppermute | solution.py:366
  (120 shorter events, 44.4 us)
Async XLA Ops:
  0.6 15.1 %collective-permute-start.3 = (bf16[1,1,128,1024]{3,2,1,0:T(8,128)(2,1)}, bf16[1,1,128,1024]{3,2,1,0:T(8,128)(2,1)S(1)}, u32[]{:S(2)}, u32[]{:S(2)}) collective-permute-start(bf16[1,1,128,1024]{3,2,1,0:T(8,128)(2,1)} %bitcast.27), channel_id=1, source_target_pairs={{0,8},{8,0},{16,24},{24,16},{1,9},{9,1},{17,25},{25,17},{2,10},{10... | collective-permute-start | bytes 786440 | tf_op jit(solution)/shard_map/ppermute | solution.py:366
  3.7 14.6 %collective-permute-start.4 = (bf16[1,1,128,1024]{3,2,1,0:T(8,128)(2,1)}, bf16[1,1,128,1024]{3,2,1,0:T(8,128)(2,1)S(1)}, u32[]{:S(2)}, u32[]{:S(2)}) collective-permute-start(bf16[1,1,128,1024]{3,2,1,0:T(8,128)(2,1)} %bitcast.28), channel_id=1, source_target_pairs={{0,16},{8,24},{16,0},{24,8},{1,17},{9,25},{17,1},{25,9},{2,18},{10... | collective-permute-start | bytes 786440 | tf_op jit(solution)/shard_map/ppermute | solution.py:366
  12.9 8.1 %collective-permute-start.5 = (bf16[1,1,128,1024]{3,2,1,0:T(8,128)(2,1)}, bf16[1,1,128,1024]{3,2,1,0:T(8,128)(2,1)S(1)}, u32[]{:S(2)}, u32[]{:S(2)}) collective-permute-start(bf16[1,1,128,1024]{3,2,1,0:T(8,128)(2,1)} %bitcast.29), channel_id=1, source_target_pairs={{0,1},{1,0},{2,3},{3,2},{4,5},{5,4},{6,7},{7,6},{8,9},{9,8},{10,11... | collective-permute-start | bytes 786440 | tf_op jit(solution)/shard_map/ppermute | solution.py:363
  18.4 13.0 %collective-permute-start.9 = (bf16[1,1,128,1024]{3,2,1,0:T(8,128)(2,1)}, bf16[1,1,128,1024]{3,2,1,0:T(8,128)(2,1)S(1)}, u32[]{:S(2)}, u32[]{:S(2)}) collective-permute-start(bf16[1,1,128,1024]{3,2,1,0:T(8,128)(2,1)} %bitcast.30), channel_id=1, source_target_pairs={{0,24},{8,16},{16,8},{24,0},{1,25},{9,17},{17,9},{25,1},{2,26},{10... | collective-permute-start | bytes 786440 | tf_op jit(solution)/shard_map/ppermute | solution.py:366
  22.1 20.5 %collective-permute-start.8 = (bf16[2,3,128,1024]{3,2,1,0:T(8,128)(2,1)S(1)}, bf16[2,3,128,1024]{3,2,1,0:T(8,128)(2,1)S(1)}, u32[]{:S(2)}, u32[]{:S(2)}) collective-permute-start(bf16[2,3,128,1024]{3,2,1,0:T(8,128)(2,1)S(1)} %join.2.refs_0_), channel_id=1, source_target_pairs={{0,2},{1,5},{2,0},{3,7},{4,6},{5,1},{6,4},{7,3},{8,10},{9,13},{10,... | collective-permute-start | bytes 4718600 | tf_op jit(solution)/shard_map/ppermute | solution.py:363
  42.7 14.1 %collective-permute-start.13 = (bf16[2,1,128,1024]{3,2,1,0:T(8,128)(2,1)S(1)}, bf16[2,1,128,1024]{3,2,1,0:T(8,128)(2,1)S(1)}, u32[]{:S(2)}, u32[]{:S(2)}) collective-permute-start(bf16[2,1,128,1024]{3,2,1,0:T(8,128)(2,1)S(1)} %join.3.refs_1_), channel_id=1, source_target_pairs={{0,2},{1,5},{2,0},{3,7},{4,6},{5,1},{6,4},{7,3},{8,10},{9,13},{10,... | collective-permute-start | bytes 1572872 | tf_op jit(solution)/shard_map/ppermute | solution.py:363
  44.2 15.7 %collective-permute-start.12 = (bf16[1,3,128,1024]{3,2,1,0:T(8,128)(2,1)S(1)}, bf16[1,3,128,1024]{3,2,1,0:T(8,128)(2,1)S(1)}, u32[]{:S(2)}, u32[]{:S(2)}) collective-permute-start(bf16[1,3,128,1024]{3,2,1,0:T(8,128)(2,1)S(1)} %slice.46), channel_id=1, source_target_pairs={{0,4},{1,3},{2,6},{3,1},{4,0},{5,7},{6,2},{7,5},{8,12},{9,11},{10,... | collective-permute-start | bytes 2359304 | tf_op jit(solution)/shard_map/ppermute | solution.py:363
  60.2 6.7 %collective-permute-start.14 = (bf16[2,1,128,1024]{3,2,1,0:T(8,128)(2,1)S(1)}, bf16[2,1,128,1024]{3,2,1,0:T(8,128)(2,1)S(1)}, u32[]{:S(2)}, u32[]{:S(2)}) collective-permute-start(bf16[2,1,128,1024]{3,2,1,0:T(8,128)(2,1)S(1)} %collective-permute-done.13.refs_2_), channel_id=1, source_target_pairs={{0,1},{1,0},{2,3},{3,2},{4,5},{5,4},{6,7},{7,6},{8,9},{9,8},{10,11... | collective-permute-start | bytes 1572872 | tf_op jit(solution)/shard_map/ppermute | solution.py:363
  60.5 6.4 %collective-permute-start.16 = (bf16[1,1,128,1024]{3,2,1,0:T(8,128)(2,1)S(1)}, bf16[1,1,128,1024]{3,2,1,0:T(8,128)(2,1)S(1)}, u32[]{:S(2)}, u32[]{:S(2)}) collective-permute-start(bf16[1,1,128,1024]{3,2,1,0:T(8,128)(2,1)S(1)} %slice.47), channel_id=1, source_target_pairs={{0,4},{1,3},{2,6},{3,1},{4,0},{5,7},{6,2},{7,5},{8,12},{9,11},{10,... | collective-permute-start | bytes 786440 | tf_op jit(solution)/shard_map/ppermute | solution.py:363
  83.6 6.8 %collective-permute-start.21 = (bf16[1,1,144,1024]{3,2,1,0:T(8,128)(2,1)S(1)}, bf16[1,1,144,1024]{3,2,1,0:T(8,128)(2,1)S(1)}, u32[]{:S(2)}, u32[]{:S(2)}) collective-permute-start(bf16[1,1,144,1024]{3,2,1,0:T(8,128)(2,1)S(1)} %get-tuple-element.74), channel_id=1, source_target_pairs={{0,4},{1,3},{2,6},{3,1},{4,0},{5,7},{6,2},{7,5},{8,12},{9,11},{10,... | collective-permute-start | bytes 884744 | tf_op jit(solution)/shard_map/ppermute | solution.py:363
  88.2 9.9 %collective-permute-start.20 = (bf16[1,1,128,1024]{3,2,1,0:T(8,128)(2,1)S(1)}, bf16[1,1,128,1024]{3,2,1,0:T(8,128)(2,1)S(1)}, u32[]{:S(2)}, u32[]{:S(2)}) collective-permute-start(bf16[1,1,128,1024]{3,2,1,0:T(8,128)(2,1)S(1)} %get-tuple-element.72), channel_id=1, source_target_pairs={{0,4},{1,3},{2,6},{3,1},{4,0},{5,7},{6,2},{7,5},{8,12},{9,11},{10,... | collective-permute-start | bytes 786440 | tf_op jit(solution)/shard_map/ppermute | solution.py:363
  93.4 6.4 %collective-permute-start.22 = (bf16[4,1,128,1024]{3,2,1,0:T(8,128)(2,1)S(1)}, bf16[4,1,128,1024]{3,2,1,0:T(8,128)(2,1)S(1)}, u32[]{:S(2)}, u32[]{:S(2)}) collective-permute-start(bf16[4,1,128,1024]{3,2,1,0:T(8,128)(2,1)S(1)} %expand.12), channel_id=1, source_target_pairs={{0,1},{1,0},{2,3},{3,2},{4,5},{5,4},{6,7},{7,6},{8,9},{9,8},{10,11... | collective-permute-start | bytes 3145736 | tf_op jit(solution)/shard_map/ppermute | solution.py:363
  93.4 12.5 %collective-permute-start.25 = (bf16[2,1,144,1024]{3,2,1,0:T(8,128)(2,1)S(1)}, bf16[2,1,144,1024]{3,2,1,0:T(8,128)(2,1)S(1)}, u32[]{:S(2)}, u32[]{:S(2)}) collective-permute-start(bf16[2,1,144,1024]{3,2,1,0:T(8,128)(2,1)S(1)} %pass_on.4), channel_id=1, source_target_pairs={{0,2},{1,5},{2,0},{3,7},{4,6},{5,1},{6,4},{7,3},{8,10},{9,13},{10,... | collective-permute-start | bytes 1769480 | tf_op jit(solution)/shard_map/ppermute | solution.py:363
  98.2 15.0 %collective-permute-start.28 = (bf16[2,1,128,1024]{3,2,1,0:T(8,128)(2,1)S(1)}, bf16[2,1,128,1024]{3,2,1,0:T(8,128)(2,1)S(1)}, u32[]{:S(2)}, u32[]{:S(2)}) collective-permute-start(bf16[2,1,128,1024]{3,2,1,0:T(8,128)(2,1)S(1)} %pass_on.5), channel_id=1, source_target_pairs={{0,2},{1,5},{2,0},{3,7},{4,6},{5,1},{6,4},{7,3},{8,10},{9,13},{10,... | collective-permute-start | bytes 1572872 | tf_op jit(solution)/shard_map/ppermute | solution.py:363
  105.9 6.4 %collective-permute-start.23 = (bf16[1,1,128,1024]{3,2,1,0:T(8,128)(2,1)S(1)}, bf16[1,1,128,1024]{3,2,1,0:T(8,128)(2,1)S(1)}, u32[]{:S(2)}, u32[]{:S(2)}) collective-permute-start(bf16[1,1,128,1024]{3,2,1,0:T(8,128)(2,1)S(1)} %get-tuple-element.82), channel_id=1, source_target_pairs={{0,4},{1,3},{2,6},{3,1},{4,0},{5,7},{6,2},{7,5},{8,12},{9,11},{10,... | collective-permute-start | bytes 786440 | tf_op jit(solution)/shard_map/ppermute | solution.py:363
  106.5 6.5 %collective-permute-start.26 = (bf16[1,1,144,1024]{3,2,1,0:T(8,128)(2,1)S(1)}, bf16[1,1,144,1024]{3,2,1,0:T(8,128)(2,1)S(1)}, u32[]{:S(2)}, u32[]{:S(2)}) collective-permute-start(bf16[1,1,144,1024]{3,2,1,0:T(8,128)(2,1)S(1)} %get-tuple-element.98), channel_id=1, source_target_pairs={{0,1},{1,0},{2,3},{3,2},{4,5},{5,4},{6,7},{7,6},{8,9},{9,8},{10,11... | collective-permute-start | bytes 884744 | tf_op jit(solution)/shard_map/ppermute | solution.py:363
  112.4 12.1 %collective-permute-start.32 = (bf16[2,1,128,1024]{3,2,1,0:T(8,128)(2,1)S(1)}, bf16[2,1,128,1024]{3,2,1,0:T(8,128)(2,1)S(1)}, u32[]{:S(2)}, u32[]{:S(2)}) collective-permute-start(bf16[2,1,128,1024]{3,2,1,0:T(8,128)(2,1)S(1)} %pass_on.6), channel_id=1, source_target_pairs={{0,2},{1,5},{2,0},{3,7},{4,6},{5,1},{6,4},{7,3},{8,10},{9,13},{10,... | collective-permute-start | bytes 1572872 | tf_op jit(solution)/shard_map/ppermute | solution.py:363
  113.3 9.3 %collective-permute-start.31 = (bf16[1,1,128,1024]{3,2,1,0:T(8,128)(2,1)S(1)}, bf16[1,1,128,1024]{3,2,1,0:T(8,128)(2,1)S(1)}, u32[]{:S(2)}, u32[]{:S(2)}) collective-permute-start(bf16[1,1,128,1024]{3,2,1,0:T(8,128)(2,1)S(1)} %get-tuple-element.92), channel_id=1, source_target_pairs={{0,4},{1,3},{2,6},{3,1},{4,0},{5,7},{6,2},{7,5},{8,12},{9,11},{10,... | collective-permute-start | bytes 786440 | tf_op jit(solution)/shard_map/ppermute | solution.py:363
  114.7 11.9 %collective-permute-start.27 = (bf16[144,1024]{1,0:T(8,128)(2,1)S(1)}, bf16[144,1024]{1,0:T(8,128)(2,1)S(1)}, u32[]{:S(2)}, u32[]{:S(2)}) collective-permute-start(bf16[144,1024]{1,0:T(8,128)(2,1)S(1)} %bitcast.32), channel_id=1, source_target_pairs={{0,24},{8,16},{16,8},{24,0},{1,25},{9,17},{17,9},{25,1},{2,26},{10... | collective-permute-start | bytes 884744 | tf_op jit(solution)/shard_map/ppermute | solution.py:366
  122.7 9.2 %collective-permute-start.35 = (bf16[2,1,128,1024]{3,2,1,0:T(8,128)(2,1)S(1)}, bf16[2,1,128,1024]{3,2,1,0:T(8,128)(2,1)S(1)}, u32[]{:S(2)}, u32[]{:S(2)}) collective-permute-start(bf16[2,1,128,1024]{3,2,1,0:T(8,128)(2,1)S(1)} %pass_on.7), channel_id=1, source_target_pairs={{0,2},{1,5},{2,0},{3,7},{4,6},{5,1},{6,4},{7,3},{8,10},{9,13},{10,... | collective-permute-start | bytes 1572872 | tf_op jit(solution)/shard_map/ppermute | solution.py:363
  124.6 7.4 %collective-permute-start.37 = (bf16[16,1024]{1,0:T(8,128)(2,1)S(1)}, bf16[16,1024]{1,0:T(8,128)(2,1)S(1)}, u32[]{:S(2)}, u32[]{:S(2)}) collective-permute-start(bf16[16,1024]{1,0:T(8,128)(2,1)S(1)} %slice_bitcast_fusion), channel_id=1, source_target_pairs={{0,8},{8,0},{16,24},{24,16},{1,9},{9,1},{17,25},{25,17},{2,10},{10... | collective-permute-start | bytes 98312 | tf_op jit(solution)/shard_map/ppermute | solution.py:366
  124.7 7.3 %collective-permute-start.38 = (bf16[16,1024]{1,0:T(8,128)(2,1)S(1)}, bf16[16,1024]{1,0:T(8,128)(2,1)S(1)}, u32[]{:S(2)}, u32[]{:S(2)}) collective-permute-start(bf16[16,1024]{1,0:T(8,128)(2,1)S(1)} %slice_bitcast_fusion), channel_id=1, source_target_pairs={{0,16},{8,24},{16,0},{24,8},{1,17},{9,25},{17,1},{25,9},{2,18},{10... | collective-permute-start | bytes 98312 | tf_op jit(solution)/shard_map/ppermute | solution.py:366
  126.6 15.1 %collective-permute-start.30 = (bf16[128,1024]{1,0:T(8,128)(2,1)S(1)}, bf16[128,1024]{1,0:T(8,128)(2,1)S(1)}, u32[]{:S(2)}, u32[]{:S(2)}) collective-permute-start(bf16[128,1024]{1,0:T(8,128)(2,1)S(1)} %bitcast.62), channel_id=1, source_target_pairs={{0,16},{8,24},{16,0},{24,8},{1,17},{9,25},{17,1},{25,9},{2,18},{10... | collective-permute-start | bytes 786440 | tf_op jit(solution)/shard_map/ppermute | solution.py:366
  130.1 11.6 %collective-permute-start.34 = (bf16[128,1024]{1,0:T(8,128)(2,1)S(1)}, bf16[128,1024]{1,0:T(8,128)(2,1)S(1)}, u32[]{:S(2)}, u32[]{:S(2)}) collective-permute-start(bf16[128,1024]{1,0:T(8,128)(2,1)S(1)} %bitcast.63), channel_id=1, source_target_pairs={{0,8},{8,0},{16,24},{24,16},{1,9},{9,1},{17,25},{25,17},{2,10},{10... | collective-permute-start | bytes 786440 | tf_op jit(solution)/shard_map/ppermute | solution.py:366
  (25 other events, 140.0 us)

commit v6 on v5

--- a/solution.py
+++ b/solution.py
@@ -377,6 +377,9 @@
         received.append(across(after(piece, *received[1:3]), i))
     info = jnp.concatenate([expert_ids.T.astype(F32), probs.T], axis=0)[None]
     if square:
+        sib0 = swap(piece, 1, 1)
+        near0 = [swap(piece, 2, 4), swap(sib0, 2, 4)]
+        info = after(info, near0[0])
         for bit in (2, 4, 1):
             info = jnp.concatenate([info, swap(info, bit, bit)], axis=0)
         place = owners ^ me
@@ -387,21 +390,24 @@
     at = jnp.concatenate([jnp.stack([z, me * experts]), owners, place]).astype(jnp.int32)
     gated = lambda at: coefficients(at, info, topk, saved_gate, saved_up, slots // groups)
     if square:
-        sibs = [swap(x, 1, 1) for x in received[:3]]
-        pair1 = join([after(piece, info), *received[1:3]], sibs)
+        got = [after(x, info) for x in received[1:3]]
+        near0 = [after(x, *got) for x in near0]
+        pair1 = join(got, [swap(x, 1, 1) for x in got])
         first1 = swap(pair1, 2, 4)
-        coefs = gated(after(at, pair1))
+        second0 = swap(near0[0], 4, 2)
+        coefs = gated(after(at, pair1, *near0))
         got = [after(x, coefs[0]) for x in received[3:]]
         pair2 = join(got, [swap(x, 1, 1) for x in got])
-        first1 = after(first1, pair2)
+        first1, second0 = after(first1, pair2), after(second0, pair2)
         second1 = swap(first1[:1], 4, 2)
         first2 = swap(after(pair2, first1), 2, 4)
+        lot0 = [piece, sib0, *near0, *[swap(x, 1, 1) for x in near0]], [second0, swap(second0, 1, 1)]
         lot1 = [pair1, first1, swap(first1, 1, 1)]
-        (most,) = hidden(at, [(None, [(0, lot1)])], tokens, after(w_down, coefs[0]))
+        (most,) = hidden(at, [(None, [(0, lot0[0]), (1, lot1)])], tokens, after(w_down, coefs[0]))
         second1, first2, _ = lax.optimization_barrier((second1, first2, most))
         second2 = swap(first2[:1], 4, 2)
         lot1 = [second1, swap(second1, 1, 1)]
-        (few,) = hidden(at, [(None, [(0, lot1)])], tokens, w_down)
+        (few,) = hidden(at, [(None, [(0, lot0[1]), (1, lot1)])], tokens, w_down)
         second2 = after(second2, few)
         lot2 = [pair2, first2, swap(first2, 1, 1)], [second2, swap(second2, 1, 1)]
         parts = [(most, [(3, lot2[0])]), (few, [(3, lot2[1])])]

time: 143 us -> 138 us (0.965)
  waiting for transfers between devices: 55.3 us -> 49.9 us
  starting transfers between devices: 35.8 us -> 39.4 us
  local copies, waits for them, and re-layouts: 4.06 us -> 0.46 us
    unnamed x20 -> x27, local copies, waits for them, and re-layouts: 3.65 us -> 0.06 us
    ppermute x31 -> x37, waiting for transfers between devices: 44 us -> 40.8 us  [swap(): lax.ppermute(x, 'expert', [(i, i ^ (even, odd)[i % 2]) for i in range(gro...]
    ppermute x31 -> x37, starting transfers between devices: 20.7 us -> 23.9 us  [swap(): lax.ppermute(x, 'expert', [(i, i ^ (even, odd)[i % 2]) for i in range(gro...]
    ppermute x8, waiting for transfers between devices: 11.3 us -> 9.04 us  [across(): return lax.ppermute(x, 'section', [(i, i ^ by) for i in range(sections)])]
  transfers between devices with their start and end apart: 39 -> 45, of which waited for: 19 -> 21; matrix products, arithmetic and copies ran while one was open for 2% -> 2% of each run, Pallas kernels for 24% -> 26%
where the time goes in v6:
time: 138 us
  waiting for transfers between devices  49.9 us (36%)
  Pallas kernels  44.4 us (32%)
  starting transfers between devices  39.4 us (29%)
  other arithmetic  2.89 us (2%)
    pallas_call x12, Pallas kernels, call(): pl.pallas_call(kernel, grid_spec=pltpu.PrefetchScalarGridSpec(num_scalar_...  43.6 us
    ppermute x37, waiting for transfers between devices, swap(): lax.ppermute(x, 'expert', [(i, i ^ (even, odd)[i % 2]) for i in range(gro...  40.8 us
    ppermute x37, starting transfers between devices, swap(): lax.ppermute(x, 'expert', [(i, i ^ (even, odd)[i % 2]) for i in range(gro...  23.9 us
    ppermute x8, starting transfers between devices, across(): return lax.ppermute(x, 'section', [(i, i ^ by) for i in range(sections)])  15.5 us
    ppermute x8, waiting for transfers between devices, across(): return lax.ppermute(x, 'section', [(i, i ^ by) for i in range(sections)])  9.04 us
  transfers between devices with their start and end apart: 45, of which 21 were waited for; matrix products, arithmetic and copies ran while one was open for 2% of the time, Pallas kernels for 26%

profile of v6, /device:TPU:0, one launch (start us, length us, event | category | flops | bytes accessed | tf_op | source)
XLA Modules:
  0.0 138.2 jit_solution(4218196178330715411)
XLA Ops:
  0.6 3.0 %collective-permute-start.1 = (bf16[1,1,128,1024]{3,2,1,0:T(8,128)(2,1)}, bf16[1,1,128,1024]{3,2,1,0:T(8,128)(2,1)S(1)}, u32[]{:S(2)}, u32[]{:S(2)}) collective-permute-start(bf16[1,1,128,1024]{3,2,1,0:T(8,128)(2,1)} %bitcast.57), channel_id=1, source_target_pairs={{0,2},{1,5},{2,0},{3,7},{4,6},{5,1},{6,4},{7,3},{8,10},{9,13},{10,... | collective-permute-start | bytes 786440 | tf_op jit(solution)/shard_map/ppermute | solution.py:363
  3.7 2.6 %collective-permute-start.6 = (bf16[1,1,128,1024]{3,2,1,0:T(8,128)(2,1)}, bf16[1,1,128,1024]{3,2,1,0:T(8,128)(2,1)S(1)}, u32[]{:S(2)}, u32[]{:S(2)}) collective-permute-start(bf16[1,1,128,1024]{3,2,1,0:T(8,128)(2,1)} %bitcast.58), channel_id=1, source_target_pairs={{0,16},{8,24},{16,0},{24,8},{1,17},{9,25},{17,1},{25,9},{2,18},{10... | collective-permute-start | bytes 786440 | tf_op jit(solution)/shard_map/ppermute | solution.py:366
  14.4 2.2 %collective-permute-done.4 = f32[2,16,128]{2,1,0:T(8,128)S(1)} collective-permute-done((f32[2,16,128]{2,1,0:T(8,128)S(1)}, f32[2,16,128]{2,1,0:T(8,128)S(1)}, u32[]{:S(2)}, u32[]{:S(2)}) %collective-permute-start.4) | collective-permute-done | bytes 16416 | tf_op jit(solution)/shard_map/ppermute | solution.py:363
  19.0 3.4 %collective-permute-start.13 = (bf16[1,1,128,1024]{3,2,1,0:T(8,128)(2,1)}, bf16[1,1,128,1024]{3,2,1,0:T(8,128)(2,1)S(1)}, u32[]{:S(2)}, u32[]{:S(2)}) collective-permute-start(bf16[1,1,128,1024]{3,2,1,0:T(8,128)(2,1)} %bitcast.61), channel_id=1, source_target_pairs={{0,24},{8,16},{16,8},{24,0},{1,25},{9,17},{17,9},{25,1},{2,26},{10... | collective-permute-start | bytes 786440 | tf_op jit(solution)/shard_map/ppermute | solution.py:366
  24.2 5.1 %coefficients.1 = (bf16[1024,768]{1,0:T(8,128)(2,1)S(1)}, bf16[1024,768]{1,0:T(8,128)(2,1)S(1)}, bf16[1024,768]{1,0:T(8,128)(2,1)S(1)}) custom-call(s32[18]{0:T(128)S(1)} %concatenate.18.at_ref, f32[8,16,128]{2,1,0:T(8,128)S(1)} %constant_dynamic-update-slice_fusion.info_ref, bf16[2,384,768]{2,1,0:T(8,128)(2,1)S(1)} %copy-done, ...), custom_call_target="tpu_custom_call" | custom-call | flops 38654705664 | bytes 7143496 | tf_op jit(solution)/shard_map/coefficients/pallas_call | solution.py:19
  31.2 6.3 %collective-permute-done.12.refs_8_ = bf16[2,2,128,1024]{3,2,1,0:T(8,128)(2,1)S(1)} collective-permute-done((bf16[2,2,128,1024]{3,2,1,0:T(8,128)(2,1)S(1)}, bf16[2,2,128,1024]{3,2,1,0:T(8,128)(2,1)S(1)}, u32[]{:S(2)}, u32[]{:S(2)}) %collective-permute-start.12) | collective-permute-done | bytes 1048608 | tf_op jit(solution)/shard_map/ppermute | solution.py:363
  41.8 6.3 %hidden_early.2.refs_0_ = f32[768,768]{1,0:T(8,128)S(1)} custom-call(s32[18]{0:T(128)S(1)} %concatenate.18.at_ref, bf16[1,1,128,1024]{3,2,1,0:T(8,128)(2,1)S(1)} %bitcast.62, bf16[1,1,128,1024]{3,2,1,0:T(8,128)(2,1)} %collective-permute-done.refs_1_, bf16[1,1,128,1024]{3,2,1,0:T(8,128)(2,1)S(1)} %copy-done.4, ...), custom_call_target="tpu_custom_call" | custom-call | flops 28991029248 | bytes 25952328 | tf_op jit(solution)/shard_map/hidden_early/pallas_call | solution.py:19
  48.1 5.7 %collective-permute-done.17.refs_2_ = bf16[2,1,128,1024]{3,2,1,0:T(8,128)(2,1)S(1)} collective-permute-done((bf16[2,1,128,1024]{3,2,1,0:T(8,128)(2,1)S(1)}, bf16[2,1,128,1024]{3,2,1,0:T(8,128)(2,1)S(1)}, u32[]{:S(2)}, u32[]{:S(2)}) %collective-permute-start.17) | collective-permute-done | bytes 524320 | tf_op jit(solution)/shard_map/ppermute | solution.py:363
  53.8 1.8 %collective-permute-done.16.refs_3_ = bf16[1,2,128,1024]{3,2,1,0:T(8,128)(2,1)S(1)} collective-permute-done((bf16[1,2,128,1024]{3,2,1,0:T(8,128)(2,1)S(1)}, bf16[1,2,128,1024]{3,2,1,0:T(8,128)(2,1)S(1)}, u32[]{:S(2)}, u32[]{:S(2)}) %collective-permute-start.16) | collective-permute-done | bytes 524320 | tf_op jit(solution)/shard_map/ppermute | solution.py:363
  57.9 2.8 %hidden_early.3.refs_5_ = f32[256,768]{1,0:T(8,128)S(1)} custom-call(s32[18]{0:T(128)S(1)} %concatenate.18.at_ref, bf16[1,1,128,1024]{3,2,1,0:T(8,128)(2,1)S(1)} %collective-permute-done.19.refs_0_, bf16[1,1,128,1024]{3,2,1,0:T(8,128)(2,1)S(1)} %collective-permute-done.20.refs_1_, bf16[768,4096]{1,0:T(8,128)(2,1)S(1)} %bitcast.33, ...), custom_call_target="tpu_custom_call" | custom-call | flops 9663676416 | bytes 21233736 | tf_op jit(solution)/shard_map/hidden_early/pallas_call | solution.py:19
  60.7 1.9 %collective-permute-done.22.refs_6_ = bf16[1,1,128,1024]{3,2,1,0:T(8,128)(2,1)S(1)} collective-permute-done((bf16[1,1,128,1024]{3,2,1,0:T(8,128)(2,1)S(1)}, bf16[1,1,128,1024]{3,2,1,0:T(8,128)(2,1)S(1)}, u32[]{:S(2)}, u32[]{:S(2)}) %collective-permute-start.22) | collective-permute-done | bytes 262176 | tf_op jit(solution)/shard_map/ppermute | solution.py:363
  64.2 5.7 %hidden_late.1 = (bf16[1024,768]{1,0:T(8,128)(2,1)S(1)}, bf16[1024,768]{1,0:T(8,128)(2,1)S(1)}, bf16[8,16,1024]{2,1,0:T(8,128)(2,1)S(1)}) custom-call(s32[18]{0:T(128)S(1)} %concatenate.18.at_ref, f32[768,768]{1,0:T(8,128)S(1)} %hidden_early.2.refs_0_, bf16[2,1,128,1024]{3,2,1,0:T(8,128)(2,1)S(1)} %join.3.refs_1_, ...), custom_call_target="tpu_custom_call" | custom-call | flops 12884901888 | bytes 19660872 | tf_op jit(solution)/shard_map/hidden_late/pallas_call | solution.py:19
  70.0 2.9 %expand.8 = bf16[4,1,144,1024]{3,2,1,0:T(8,128)(2,1)S(1)} custom-call(s32[18]{0:T(128)S(1)} %concatenate.18.at_ref, bf16[1024,768]{1,0:T(8,128)(2,1)S(1)} %get-tuple-element.94.ag_ref, bf16[1024,768]{1,0:T(8,128)(2,1)S(1)} %get-tuple-element.76.au_ref, bf16[768,4096]{1,0:T(8,128)(2,1)S(1)} %bitcast.39, bf16[768,4096]{1,0:T(8,128)(2,1)S(1)} %bitcast.49, ...), custom_call_target="tpu_custom_call" | custom-call | flops 12884901888 | bytes 17170504 | tf_op jit(solution)/shard_map/expand/pallas_call | solution.py:19
  73.0 2.9 %expand.9 = bf16[4,1,128,1024]{3,2,1,0:T(8,128)(2,1)S(1)} custom-call(s32[18]{0:T(128)S(1)} %concatenate.18.at_ref, bf16[1024,768]{1,0:T(8,128)(2,1)S(1)} %get-tuple-element.94.ag_ref, bf16[1024,768]{1,0:T(8,128)(2,1)S(1)} %get-tuple-element.76.au_ref, bf16[768,4096]{1,0:T(8,128)(2,1)S(1)} %bitcast.40, bf16[768,4096]{1,0:T(8,128)(2,1)S(1)} %bitcast.50), custom_call_target="tpu_custom_call" | custom-call | flops 12884901888 | bytes 16777288 | tf_op jit(solution)/shard_map/expand/pallas_call | solution.py:19
  76.4 3.0 %expand.10 = (bf16[1,1,144,1024]{3,2,1,0:T(8,128)(2,1)S(1)}, bf16[2,1,144,1024]{3,2,1,0:T(8,128)(2,1)S(1)}, bf16[1,1,144,1024]{3,2,1,0:T(8,128)(2,1)S(1)}) custom-call(s32[18]{0:T(128)S(1)} %concatenate.18.at_ref, bf16[1024,768]{1,0:T(8,128)(2,1)S(1)} %get-tuple-element.94.ag_ref, bf16[1024,768]{1,0:T(8,128)(2,1)S(1)} %get-tuple-element.76.au_ref, ...), custom_call_target="tpu_custom_call" | custom-call | flops 12884901888 | bytes 18350152 | tf_op jit(solution)/shard_map/expand/pallas_call | solution.py:19
  80.4 3.0 %expand.11 = (bf16[1,1,128,1024]{3,2,1,0:T(8,128)(2,1)S(1)}, bf16[2,1,128,1024]{3,2,1,0:T(8,128)(2,1)S(1)}, bf16[1,1,128,1024]{3,2,1,0:T(8,128)(2,1)S(1)}) custom-call(s32[18]{0:T(128)S(1)} %concatenate.18.at_ref, bf16[1024,768]{1,0:T(8,128)(2,1)S(1)} %get-tuple-element.94.ag_ref, bf16[1024,768]{1,0:T(8,128)(2,1)S(1)} %get-tuple-element.76.au_ref, ...), custom_call_target="tpu_custom_call" | custom-call | flops 12884901888 | bytes 17825864 | tf_op jit(solution)/shard_map/expand/pallas_call | solution.py:19
  86.3 2.9 %expand.12 = bf16[4,1,128,1024]{3,2,1,0:T(8,128)(2,1)S(1)} custom-call(s32[18]{0:T(128)S(1)} %concatenate.18.at_ref, bf16[1024,768]{1,0:T(8,128)(2,1)S(1)} %get-tuple-element.94.ag_ref, bf16[1024,768]{1,0:T(8,128)(2,1)S(1)} %get-tuple-element.76.au_ref, bf16[768,4096]{1,0:T(8,128)(2,1)S(1)} %bitcast.43, bf16[768,4096]{1,0:T(8,128)(2,1)S(1)} %bitcast.53), custom_call_target="tpu_custom_call" | custom-call | flops 12884901888 | bytes 16777288 | tf_op jit(solution)/shard_map/expand/pallas_call | solution.py:19
  90.7 2.9 %expand.13 = bf16[4,1,128,1024]{3,2,1,0:T(8,128)(2,1)S(1)} custom-call(s32[18]{0:T(128)S(1)} %concatenate.18.at_ref, bf16[1024,768]{1,0:T(8,128)(2,1)S(1)} %get-tuple-element.94.ag_ref, bf16[1024,768]{1,0:T(8,128)(2,1)S(1)} %get-tuple-element.76.au_ref, bf16[768,4096]{1,0:T(8,128)(2,1)S(1)} %bitcast.44, bf16[768,4096]{1,0:T(8,128)(2,1)S(1)} %bitcast.54), custom_call_target="tpu_custom_call" | custom-call | flops 12884901888 | bytes 16777288 | tf_op jit(solution)/shard_map/expand/pallas_call | solution.py:19
  94.8 3.2 %expand.14 = (bf16[1,1,128,1024]{3,2,1,0:T(8,128)(2,1)S(1)}, bf16[2,1,128,1024]{3,2,1,0:T(8,128)(2,1)S(1)}, bf16[1,1,128,1024]{3,2,1,0:T(8,128)(2,1)S(1)}) custom-call(s32[18]{0:T(128)S(1)} %concatenate.18.at_ref, bf16[1024,768]{1,0:T(8,128)(2,1)S(1)} %get-tuple-element.94.ag_ref, bf16[1024,768]{1,0:T(8,128)(2,1)S(1)} %get-tuple-element.76.au_ref, ...), custom_call_target="tpu_custom_call" | custom-call | flops 12884901888 | bytes 17825864 | tf_op jit(solution)/shard_map/expand/pallas_call | solution.py:19
  98.0 3.0 %expand.15 = (bf16[1,1,128,1024]{3,2,1,0:T(8,128)(2,1)S(1)}, bf16[2,1,128,1024]{3,2,1,0:T(8,128)(2,1)S(1)}, bf16[1,1,128,1024]{3,2,1,0:T(8,128)(2,1)S(1)}) custom-call(s32[18]{0:T(128)S(1)} %concatenate.18.at_ref, bf16[1024,768]{1,0:T(8,128)(2,1)S(1)} %get-tuple-element.94.ag_ref, bf16[1024,768]{1,0:T(8,128)(2,1)S(1)} %get-tuple-element.76.au_ref, ...), custom_call_target="tpu_custom_call" | custom-call | flops 12884901888 | bytes 17825864 | tf_op jit(solution)/shard_map/expand/pallas_call | solution.py:19
  102.3 5.1 %collective-permute-done.29.one_ref = bf16[1,1,128,1024]{3,2,1,0:T(8,128)(2,1)S(1)} collective-permute-done((bf16[1,1,128,1024]{3,2,1,0:T(8,128)(2,1)S(1)}, bf16[1,1,128,1024]{3,2,1,0:T(8,128)(2,1)S(1)}, u32[]{:S(2)}, u32[]{:S(2)}) %collective-permute-start.29) | collective-permute-done | bytes 262176 | tf_op jit(solution)/shard_map/ppermute | solution.py:363
  111.0 7.1 %collective-permute-done.37.one_ref = bf16[1,1,128,1024]{3,2,1,0:T(8,128)(2,1)S(1)} collective-permute-done((bf16[1,1,128,1024]{3,2,1,0:T(8,128)(2,1)S(1)}, bf16[1,1,128,1024]{3,2,1,0:T(8,128)(2,1)S(1)}, u32[]{:S(2)}, u32[]{:S(2)}) %collective-permute-start.37) | collective-permute-done | bytes 262176 | tf_op jit(solution)/shard_map/ppermute | solution.py:363
  121.4 5.0 %collective-permute-start.36 = (bf16[128,1024]{1,0:T(8,128)(2,1)S(1)}, bf16[128,1024]{1,0:T(8,128)(2,1)S(1)}, u32[]{:S(2)}, u32[]{:S(2)}) collective-permute-start(bf16[128,1024]{1,0:T(8,128)(2,1)S(1)} %bitcast.63), channel_id=1, source_target_pairs={{0,16},{8,24},{16,0},{24,8},{1,17},{9,25},{17,1},{25,9},{2,18},{10... | collective-permute-start | bytes 786440 | tf_op jit(solution)/shard_map/ppermute | solution.py:366
  129.2 8.1 %collective-permute-done.36 = bf16[128,1024]{1,0:T(8,128)(2,1)S(1)} collective-permute-done((bf16[128,1024]{1,0:T(8,128)(2,1)S(1)}, bf16[128,1024]{1,0:T(8,128)(2,1)S(1)}, u32[]{:S(2)}, u32[]{:S(2)}) %collective-permute-start.36) | collective-permute-done | bytes 262176 | tf_op jit(solution)/shard_map/ppermute | solution.py:366
  (139 shorter events, 41.2 us)
Async XLA Ops:
  0.6 8.6 %collective-permute-start.1 = (bf16[1,1,128,1024]{3,2,1,0:T(8,128)(2,1)}, bf16[1,1,128,1024]{3,2,1,0:T(8,128)(2,1)S(1)}, u32[]{:S(2)}, u32[]{:S(2)}) collective-permute-start(bf16[1,1,128,1024]{3,2,1,0:T(8,128)(2,1)} %bitcast.57), channel_id=1, source_target_pairs={{0,2},{1,5},{2,0},{3,7},{4,6},{5,1},{6,4},{7,3},{8,10},{9,13},{10,... | collective-permute-start | bytes 786440 | tf_op jit(solution)/shard_map/ppermute | solution.py:363
  3.7 14.6 %collective-permute-start.6 = (bf16[1,1,128,1024]{3,2,1,0:T(8,128)(2,1)}, bf16[1,1,128,1024]{3,2,1,0:T(8,128)(2,1)S(1)}, u32[]{:S(2)}, u32[]{:S(2)}) collective-permute-start(bf16[1,1,128,1024]{3,2,1,0:T(8,128)(2,1)} %bitcast.58), channel_id=1, source_target_pairs={{0,16},{8,24},{16,0},{24,8},{1,17},{9,25},{17,1},{25,9},{2,18},{10... | collective-permute-start | bytes 786440 | tf_op jit(solution)/shard_map/ppermute | solution.py:366
  6.2 12.2 %collective-permute-start.2 = (bf16[1,1,128,1024]{3,2,1,0:T(8,128)(2,1)}, bf16[1,1,128,1024]{3,2,1,0:T(8,128)(2,1)S(1)}, u32[]{:S(2)}, u32[]{:S(2)}) collective-permute-start(bf16[1,1,128,1024]{3,2,1,0:T(8,128)(2,1)} %bitcast.59), channel_id=1, source_target_pairs={{0,8},{8,0},{16,24},{24,16},{1,9},{9,1},{17,25},{25,17},{2,10},{10... | collective-permute-start | bytes 786440 | tf_op jit(solution)/shard_map/ppermute | solution.py:366
  10.2 12.2 %collective-permute-start.7 = (bf16[1,1,128,1024]{3,2,1,0:T(8,128)(2,1)}, bf16[1,1,128,1024]{3,2,1,0:T(8,128)(2,1)}, u32[]{:S(2)}, u32[]{:S(2)}) collective-permute-start(bf16[1,1,128,1024]{3,2,1,0:T(8,128)(2,1)} %collective-permute-done.refs_1_), channel_id=1, source_target_pairs={{0,2},{1,5},{2,0},{3,7},{4,6},{5,1},{6,4},{7,3},{8,10},{9,13},{10,... | collective-permute-start | bytes 786440 | tf_op jit(solution)/shard_map/ppermute | solution.py:363
  19.0 10.5 %collective-permute-start.13 = (bf16[1,1,128,1024]{3,2,1,0:T(8,128)(2,1)}, bf16[1,1,128,1024]{3,2,1,0:T(8,128)(2,1)S(1)}, u32[]{:S(2)}, u32[]{:S(2)}) collective-permute-start(bf16[1,1,128,1024]{3,2,1,0:T(8,128)(2,1)} %bitcast.61), channel_id=1, source_target_pairs={{0,24},{8,16},{16,8},{24,0},{1,25},{9,17},{17,9},{25,1},{2,26},{10... | collective-permute-start | bytes 786440 | tf_op jit(solution)/shard_map/ppermute | solution.py:366
  22.6 14.9 %collective-permute-start.12 = (bf16[2,2,128,1024]{3,2,1,0:T(8,128)(2,1)S(1)}, bf16[2,2,128,1024]{3,2,1,0:T(8,128)(2,1)S(1)}, u32[]{:S(2)}, u32[]{:S(2)}) collective-permute-start(bf16[2,2,128,1024]{3,2,1,0:T(8,128)(2,1)S(1)} %join.2.refs_7_), channel_id=1, source_target_pairs={{0,2},{1,5},{2,0},{3,7},{4,6},{5,1},{6,4},{7,3},{8,10},{9,13},{10,... | collective-permute-start | bytes 3145736 | tf_op jit(solution)/shard_map/ppermute | solution.py:363
  38.0 17.6 %collective-permute-start.19 = (bf16[1,1,128,1024]{3,2,1,0:T(8,128)(2,1)S(1)}, bf16[1,1,128,1024]{3,2,1,0:T(8,128)(2,1)S(1)}, u32[]{:S(2)}, u32[]{:S(2)}) collective-permute-start(bf16[1,1,128,1024]{3,2,1,0:T(8,128)(2,1)S(1)} %copy-done.4), channel_id=1, source_target_pairs={{0,4},{1,3},{2,6},{3,1},{4,0},{5,7},{6,2},{7,5},{8,12},{9,11},{10,... | collective-permute-start | bytes 786440 | tf_op jit(solution)/shard_map/ppermute | solution.py:363
  38.9 14.9 %collective-permute-start.17 = (bf16[2,1,128,1024]{3,2,1,0:T(8,128)(2,1)S(1)}, bf16[2,1,128,1024]{3,2,1,0:T(8,128)(2,1)S(1)}, u32[]{:S(2)}, u32[]{:S(2)}) collective-permute-start(bf16[2,1,128,1024]{3,2,1,0:T(8,128)(2,1)S(1)} %join.3.refs_1_), channel_id=1, source_target_pairs={{0,2},{1,5},{2,0},{3,7},{4,6},{5,1},{6,4},{7,3},{8,10},{9,13},{10,... | collective-permute-start | bytes 1572872 | tf_op jit(solution)/shard_map/ppermute | solution.py:363
  40.9 14.7 %collective-permute-start.16 = (bf16[1,2,128,1024]{3,2,1,0:T(8,128)(2,1)S(1)}, bf16[1,2,128,1024]{3,2,1,0:T(8,128)(2,1)S(1)}, u32[]{:S(2)}, u32[]{:S(2)}) collective-permute-start(bf16[1,2,128,1024]{3,2,1,0:T(8,128)(2,1)S(1)} %slice.46), channel_id=1, source_target_pairs={{0,4},{1,3},{2,6},{3,1},{4,0},{5,7},{6,2},{7,5},{8,12},{9,11},{10,... | collective-permute-start | bytes 1572872 | tf_op jit(solution)/shard_map/ppermute | solution.py:363
  56.1 6.5 %collective-permute-start.18 = (bf16[2,1,128,1024]{3,2,1,0:T(8,128)(2,1)S(1)}, bf16[2,1,128,1024]{3,2,1,0:T(8,128)(2,1)S(1)}, u32[]{:S(2)}, u32[]{:S(2)}) collective-permute-start(bf16[2,1,128,1024]{3,2,1,0:T(8,128)(2,1)S(1)} %collective-permute-done.17.refs_2_), channel_id=1, source_target_pairs={{0,1},{1,0},{2,3},{3,2},{4,5},{5,4},{6,7},{7,6},{8,9},{9,8},{10,11... | collective-permute-start | bytes 1572872 | tf_op jit(solution)/shard_map/ppermute | solution.py:363
  56.2 6.4 %collective-permute-start.22 = (bf16[1,1,128,1024]{3,2,1,0:T(8,128)(2,1)S(1)}, bf16[1,1,128,1024]{3,2,1,0:T(8,128)(2,1)S(1)}, u32[]{:S(2)}, u32[]{:S(2)}) collective-permute-start(bf16[1,1,128,1024]{3,2,1,0:T(8,128)(2,1)S(1)} %slice.47), channel_id=1, source_target_pairs={{0,4},{1,3},{2,6},{3,1},{4,0},{5,7},{6,2},{7,5},{8,12},{9,11},{10,... | collective-permute-start | bytes 786440 | tf_op jit(solution)/shard_map/ppermute | solution.py:363
  79.4 6.8 %collective-permute-start.27 = (bf16[1,1,144,1024]{3,2,1,0:T(8,128)(2,1)S(1)}, bf16[1,1,144,1024]{3,2,1,0:T(8,128)(2,1)S(1)}, u32[]{:S(2)}, u32[]{:S(2)}) collective-permute-start(bf16[1,1,144,1024]{3,2,1,0:T(8,128)(2,1)S(1)} %get-tuple-element.84), channel_id=1, source_target_pairs={{0,4},{1,3},{2,6},{3,1},{4,0},{5,7},{6,2},{7,5},{8,12},{9,11},{10,... | collective-permute-start | bytes 884744 | tf_op jit(solution)/shard_map/ppermute | solution.py:363
  83.3 10.3 %collective-permute-start.26 = (bf16[1,1,128,1024]{3,2,1,0:T(8,128)(2,1)S(1)}, bf16[1,1,128,1024]{3,2,1,0:T(8,128)(2,1)S(1)}, u32[]{:S(2)}, u32[]{:S(2)}) collective-permute-start(bf16[1,1,128,1024]{3,2,1,0:T(8,128)(2,1)S(1)} %get-tuple-element.82), channel_id=1, source_target_pairs={{0,4},{1,3},{2,6},{3,1},{4,0},{5,7},{6,2},{7,5},{8,12},{9,11},{10,... | collective-permute-start | bytes 786440 | tf_op jit(solution)/shard_map/ppermute | solution.py:363
  89.2 11.7 %collective-permute-start.31 = (bf16[2,1,144,1024]{3,2,1,0:T(8,128)(2,1)S(1)}, bf16[2,1,144,1024]{3,2,1,0:T(8,128)(2,1)S(1)}, u32[]{:S(2)}, u32[]{:S(2)}) collective-permute-start(bf16[2,1,144,1024]{3,2,1,0:T(8,128)(2,1)S(1)} %pass_on.4), channel_id=1, source_target_pairs={{0,2},{1,5},{2,0},{3,7},{4,6},{5,1},{6,4},{7,3},{8,10},{9,13},{10,... | collective-permute-start | bytes 1769480 | tf_op jit(solution)/shard_map/ppermute | solution.py:363
  93.7 15.0 %collective-permute-start.34 = (bf16[2,1,128,1024]{3,2,1,0:T(8,128)(2,1)S(1)}, bf16[2,1,128,1024]{3,2,1,0:T(8,128)(2,1)S(1)}, u32[]{:S(2)}, u32[]{:S(2)}) collective-permute-start(bf16[2,1,128,1024]{3,2,1,0:T(8,128)(2,1)S(1)} %pass_on.5), channel_id=1, source_target_pairs={{0,2},{1,5},{2,0},{3,7},{4,6},{5,1},{6,4},{7,3},{8,10},{9,13},{10,... | collective-permute-start | bytes 1572872 | tf_op jit(solution)/shard_map/ppermute | solution.py:363
  107.5 12.1 %collective-permute-start.38 = (bf16[2,1,128,1024]{3,2,1,0:T(8,128)(2,1)S(1)}, bf16[2,1,128,1024]{3,2,1,0:T(8,128)(2,1)S(1)}, u32[]{:S(2)}, u32[]{:S(2)}) collective-permute-start(bf16[2,1,128,1024]{3,2,1,0:T(8,128)(2,1)S(1)} %pass_on.6), channel_id=1, source_target_pairs={{0,2},{1,5},{2,0},{3,7},{4,6},{5,1},{6,4},{7,3},{8,10},{9,13},{10,... | collective-permute-start | bytes 1572872 | tf_op jit(solution)/shard_map/ppermute | solution.py:363
  108.8 9.3 %collective-permute-start.37 = (bf16[1,1,128,1024]{3,2,1,0:T(8,128)(2,1)S(1)}, bf16[1,1,128,1024]{3,2,1,0:T(8,128)(2,1)S(1)}, u32[]{:S(2)}, u32[]{:S(2)}) collective-permute-start(bf16[1,1,128,1024]{3,2,1,0:T(8,128)(2,1)S(1)} %get-tuple-element.102), channel_id=1, source_target_pairs={{0,4},{1,3},{2,6},{3,1},{4,0},{5,7},{6,2},{7,5},{8,12},{9,11},{10,... | collective-permute-start | bytes 786440 | tf_op jit(solution)/shard_map/ppermute | solution.py:363
  109.8 11.6 %collective-permute-start.33 = (bf16[144,1024]{1,0:T(8,128)(2,1)S(1)}, bf16[144,1024]{1,0:T(8,128)(2,1)S(1)}, u32[]{:S(2)}, u32[]{:S(2)}) collective-permute-start(bf16[144,1024]{1,0:T(8,128)(2,1)S(1)} %bitcast.27), channel_id=1, source_target_pairs={{0,24},{8,16},{16,8},{24,0},{1,25},{9,17},{17,9},{25,1},{2,26},{10... | collective-permute-start | bytes 884744 | tf_op jit(solution)/shard_map/ppermute | solution.py:366
  118.2 9.2 %collective-permute-start.41 = (bf16[2,1,128,1024]{3,2,1,0:T(8,128)(2,1)S(1)}, bf16[2,1,128,1024]{3,2,1,0:T(8,128)(2,1)S(1)}, u32[]{:S(2)}, u32[]{:S(2)}) collective-permute-start(bf16[2,1,128,1024]{3,2,1,0:T(8,128)(2,1)S(1)} %pass_on.7), channel_id=1, source_target_pairs={{0,2},{1,5},{2,0},{3,7},{4,6},{5,1},{6,4},{7,3},{8,10},{9,13},{10,... | collective-permute-start | bytes 1572872 | tf_op jit(solution)/shard_map/ppermute | solution.py:363
  119.6 6.9 %collective-permute-start.39 = (bf16[1,1,128,1024]{3,2,1,0:T(8,128)(2,1)S(1)}, bf16[1,1,128,1024]{3,2,1,0:T(8,128)(2,1)S(1)}, u32[]{:S(2)}, u32[]{:S(2)}) collective-permute-start(bf16[1,1,128,1024]{3,2,1,0:T(8,128)(2,1)S(1)} %get-tuple-element.112), channel_id=1, source_target_pairs={{0,1},{1,0},{2,3},{3,2},{4,5},{5,4},{6,7},{7,6},{8,9},{9,8},{10,11... | collective-permute-start | bytes 786440 | tf_op jit(solution)/shard_map/ppermute | solution.py:363
  119.7 7.9 %collective-permute-start.43 = (bf16[16,1024]{1,0:T(8,128)(2,1)S(1)}, bf16[16,1024]{1,0:T(8,128)(2,1)S(1)}, u32[]{:S(2)}, u32[]{:S(2)}) collective-permute-start(bf16[16,1024]{1,0:T(8,128)(2,1)S(1)} %slice_bitcast_fusion), channel_id=1, source_target_pairs={{0,8},{8,0},{16,24},{24,16},{1,9},{9,1},{17,25},{25,17},{2,10},{10... | collective-permute-start | bytes 98312 | tf_op jit(solution)/shard_map/ppermute | solution.py:366
  119.7 7.9 %collective-permute-start.44 = (bf16[16,1024]{1,0:T(8,128)(2,1)S(1)}, bf16[16,1024]{1,0:T(8,128)(2,1)S(1)}, u32[]{:S(2)}, u32[]{:S(2)}) collective-permute-start(bf16[16,1024]{1,0:T(8,128)(2,1)S(1)} %slice_bitcast_fusion), channel_id=1, source_target_pairs={{0,16},{8,24},{16,0},{24,8},{1,17},{9,25},{17,1},{25,9},{2,18},{10... | collective-permute-start | bytes 98312 | tf_op jit(solution)/shard_map/ppermute | solution.py:366
  121.4 15.9 %collective-permute-start.36 = (bf16[128,1024]{1,0:T(8,128)(2,1)S(1)}, bf16[128,1024]{1,0:T(8,128)(2,1)S(1)}, u32[]{:S(2)}, u32[]{:S(2)}) collective-permute-start(bf16[128,1024]{1,0:T(8,128)(2,1)S(1)} %bitcast.63), channel_id=1, source_target_pairs={{0,16},{8,24},{16,0},{24,8},{1,17},{9,25},{17,1},{25,9},{2,18},{10... | collective-permute-start | bytes 786440 | tf_op jit(solution)/shard_map/ppermute | solution.py:366
  126.5 10.8 %collective-permute-start.40 = (bf16[128,1024]{1,0:T(8,128)(2,1)S(1)}, bf16[128,1024]{1,0:T(8,128)(2,1)S(1)}, u32[]{:S(2)}, u32[]{:S(2)}) collective-permute-start(bf16[128,1024]{1,0:T(8,128)(2,1)S(1)} %bitcast.64), channel_id=1, source_target_pairs={{0,8},{8,0},{16,24},{24,16},{1,9},{9,1},{17,25},{25,17},{2,10},{10... | collective-permute-start | bytes 786440 | tf_op jit(solution)/shard_map/ppermute | solution.py:366
  (33 other events, 231.8 us)

commit v7 on v6

--- a/solution.py
+++ b/solution.py
@@ -318,23 +318,25 @@
 
 
 def pass_on(two, one):
-    return small(pass_on_kernel, "pass_on", jax.ShapeDtypeStruct(two.shape, BF16), (two, one))
-
-
-def finish_kernel(a_ref, b_ref, c_ref, *refs):
+    return small(pass_on_kernel, "pass_on", jax.ShapeDtypeStruct(two.shape, BF16), (two, one), flops=1 << 32)
+
+
+def finish_kernel(rows, a_ref, b_ref, c_ref, *refs):
     extra, out_ref = refs[:-1], refs[-1]
-    rows = a_ref.shape[2]
-    for k in range(out_ref.shape[0]):
-        y = a_ref[0, k].astype(F32) + b_ref[0, k].astype(F32) + c_ref[0, k].astype(F32)
-        out_ref[k, :rows] = y.astype(BF16)
-        if extra:
-            out_ref[k, rows:] = extra[0][...]
-
-
-def finish(a, b, c, *extra):
-    more = extra[0].shape[0] if extra else 0
-    shape = (a.shape[1], a.shape[2] + more, a.shape[3])
-    return small(finish_kernel, "finish", jax.ShapeDtypeStruct(shape, BF16), (a, b, c, *extra))
+    y = a_ref[0, 0].astype(F32) + b_ref[0, 0].astype(F32) + c_ref[0, 0].astype(F32)
+    if extra:
+        got_ref, own_ref = extra
+        out_ref[:rows] = (y + got_ref[:rows].astype(F32)).astype(BF16)
+        more = got_ref[rows:].astype(F32) + own_ref[rows:].astype(F32)
+        out_ref[rows:] = more.astype(BF16)
+    else:
+        out_ref[...] = y.astype(BF16)
+
+
+def finish(rows, a, b, c, *extra):
+    shape = extra[0].shape if extra else a.shape[2:]
+    kernel = functools.partial(finish_kernel, rows)
+    return small(kernel, "finish", jax.ShapeDtypeStruct(shape, BF16), (a, b, c, *extra), flops=1 << 30)
 
 
 def add(*terms):
@@ -352,7 +354,7 @@
     slots = saved_gate.shape[2]
     tokens, topk = expert_ids.shape
     span = grad_out.shape[1]
-    square = groups == 8
+    square = groups == 8 and sections == 4
     flat = lambda w: w.reshape(experts * units, features)
     w_gate, w_up, w_down = flat(w_gate), flat(w_up), flat(w_down)
     core = me % 2
@@ -422,7 +424,7 @@
     lots = ((3, sections), (2, 3), (1, 2), (0, 1))
     half = groups // 2
     last = [info]
-    theirs, kept, sent, parts, routers = {}, {}, {}, {}, {}
+    theirs, kept, sent, parts, firsts = {}, {}, {}, {}, {}
 
     def run_expand(n, part, counts, other=None):
         a, b = lots[n]
@@ -445,28 +447,15 @@
         last[0] = pass_on(two, after(one, *last))
         sent[n] = swap(last[0], 2, 4)
 
-    def hand_out(n, sums):
-        a = lots[n][0]
-        for k, x in enumerate(sums):
-            if a + k == 0:
-                parts[0] = x
-                continue
-            if n == 0 and k == 0:
-                routers[0] = x[tokens:]
-            x = across(x, a + k)
-            parts[a + k] = x[:tokens]
-            if n == 0:
-                routers[a + k] = x[tokens:]
-        if n == 0:
-            routers.update({i: across(routers[0], i) for i in range(1, 3) if i < sections})
-
     def receive_step(n):
         got = after(sent[n], *last)
         sent[n] = got[:1], swap(got[1:], 1, 1)
 
     def final_step(n):
-        last[0] = finish(after(kept[n][0], *last), *sent[n])
-        hand_out(n, list(last[0]))
+        extra = (parts[0], firsts[0]) if n == 1 else ()
+        x = finish(tokens, after(kept[n][0], *last), *sent[n], *extra)
+        last[0] = firsts[n] = x
+        parts[n] = across(x, (1, 2, 1)[n]) if n < 3 else x
 
     if square:
         for step, n in (
@@ -478,28 +467,32 @@
             (theirs_step, 2),
             (theirs_step, 3),
             (sent_step, 1),
+            (receive_step, 0),
             (mine_step, 2),
             (mine_step, 3),
-            (receive_step, 0),
             (sent_step, 2),
             (final_step, 0),
             (receive_step, 1),
+            (sent_step, 3),
             (final_step, 1),
             (receive_step, 2),
-            (sent_step, 3),
+            (final_step, 2),
             (receive_step, 3),
-            (final_step, 2),
             (final_step, 3),
         ):
             step(n)
+        parts[1] = after(parts[1], firsts[2])
+        grad_in = add(parts[1][:tokens], parts[2], parts[3])
+        router = firsts[1][tokens:].astype(F32) + parts[1][tokens:].astype(F32)
     else:
+        terms = []
         for n, (a, b) in enumerate(lots):
-            outs = run_expand(n, 0, (groups,))
-            sums = lax.psum_scatter(outs[0], "expert", scatter_dimension=0, tiled=True)[0]
-            hand_out(n, list(sums))
-    grad_in = add(*parts.values())
-
-    router = functools.reduce(lambda a, b: a + b, [r.astype(F32) for r in routers.values()])
+            sums = lax.psum_scatter(run_expand(n, 0, (groups,))[0], "expert", scatter_dimension=0, tiled=True)[0]
+            if n == 0:
+                router = lax.psum(sums[0, tokens:].astype(F32), "section")
+            terms += [across(sums[i - a, :tokens], i) if i else sums[0] for i in range(a, b)]
+        grad_in = add(*terms)
+
     count = groups * experts
     router = jnp.sum(router.reshape(-1)[: 2 * count * tokens].reshape(2, count, tokens), axis=0)
     match = expert_ids[None] == jnp.arange(count)[:, None, None]

time: 138 us -> 135 us (0.978)
  starting transfers between devices: 39.4 us -> 33.3 us
  waiting for transfers between devices: 49.9 us -> 53.1 us
    ppermute x8 -> x6, waiting for transfers between devices: 9.04 us -> 18.2 us  [across(): return lax.ppermute(x, 'section', [(i, i ^ by) for i in range(sections)])]
    ppermute x8 -> x6, starting transfers between devices: 15.5 us -> 8.07 us  [across(): return lax.ppermute(x, 'section', [(i, i ^ by) for i in range(sections)])]
    ppermute x37, waiting for transfers between devices: 40.8 us -> 34.8 us  [swap(): lax.ppermute(x, 'expert', [(i, i ^ (even, odd)[i % 2]) for i in range(gro...]
    ppermute x37, starting transfers between devices: 23.9 us -> 25.3 us  [swap(): lax.ppermute(x, 'expert', [(i, i ^ (even, odd)[i % 2]) for i in range(gro...]
  transfers between devices with their start and end apart: 45 -> 43, of which waited for: 21 -> 22; matrix products, arithmetic and copies ran while one was open for 2% -> 2% of each run, Pallas kernels for 26% -> 27%
where the time goes in v7:
time: 135 us
  waiting for transfers between devices  53.1 us (39%)
  Pallas kernels  44.5 us (33%)
  starting transfers between devices  33.3 us (25%)
  other arithmetic  2.84 us (2%)
    pallas_call x12, Pallas kernels, call(): pl.pallas_call(kernel, grid_spec=pltpu.PrefetchScalarGridSpec(num_scalar_...  43.6 us
    ppermute x37, waiting for transfers between devices, swap(): lax.ppermute(x, 'expert', [(i, i ^ (even, odd)[i % 2]) for i in range(gro...  34.8 us
    ppermute x37, starting transfers between devices, swap(): lax.ppermute(x, 'expert', [(i, i ^ (even, odd)[i % 2]) for i in range(gro...  25.3 us
    ppermute x6, waiting for transfers between devices, across(): return lax.ppermute(x, 'section', [(i, i ^ by) for i in range(sections)])  18.2 us
    ppermute x6, starting transfers between devices, across(): return lax.ppermute(x, 'section', [(i, i ^ by) for i in range(sections)])  8.07 us
  transfers between devices with their start and end apart: 43, of which 22 were waited for; matrix products, arithmetic and copies ran while one was open for 2% of the time, Pallas kernels for 27%

profile of v7, /device:TPU:0, one launch (start us, length us, event | category | flops | bytes accessed | tf_op | source)
XLA Modules:
  0.0 135.2 jit_solution(4409076823801948856)
XLA Ops:
  0.6 3.0 %collective-permute-start.1 = (bf16[1,1,128,1024]{3,2,1,0:T(8,128)(2,1)}, bf16[1,1,128,1024]{3,2,1,0:T(8,128)(2,1)S(1)}, u32[]{:S(2)}, u32[]{:S(2)}) collective-permute-start(bf16[1,1,128,1024]{3,2,1,0:T(8,128)(2,1)} %bitcast.48), channel_id=1, source_target_pairs={{0,2},{1,5},{2,0},{3,7},{4,6},{5,1},{6,4},{7,3},{8,10},{9,13},{10,... | collective-permute-start | bytes 786440 | tf_op jit(solution)/shard_map/ppermute | solution.py:365
  3.7 2.6 %collective-permute-start.6 = (bf16[1,1,128,1024]{3,2,1,0:T(8,128)(2,1)}, bf16[1,1,128,1024]{3,2,1,0:T(8,128)(2,1)S(1)}, u32[]{:S(2)}, u32[]{:S(2)}) collective-permute-start(bf16[1,1,128,1024]{3,2,1,0:T(8,128)(2,1)} %bitcast.49), channel_id=1, source_target_pairs={{0,16},{8,24},{16,0},{24,8},{1,17},{9,25},{17,1},{25,9},{2,18},{10... | collective-permute-start | bytes 786440 | tf_op jit(solution)/shard_map/ppermute | solution.py:368
  14.4 2.2 %collective-permute-done.4 = f32[2,16,128]{2,1,0:T(8,128)S(1)} collective-permute-done((f32[2,16,128]{2,1,0:T(8,128)S(1)}, f32[2,16,128]{2,1,0:T(8,128)S(1)}, u32[]{:S(2)}, u32[]{:S(2)}) %collective-permute-start.4) | collective-permute-done | bytes 16416 | tf_op jit(solution)/shard_map/ppermute | solution.py:365
  19.0 3.4 %collective-permute-start.13 = (bf16[1,1,128,1024]{3,2,1,0:T(8,128)(2,1)}, bf16[1,1,128,1024]{3,2,1,0:T(8,128)(2,1)S(1)}, u32[]{:S(2)}, u32[]{:S(2)}) collective-permute-start(bf16[1,1,128,1024]{3,2,1,0:T(8,128)(2,1)} %bitcast.52), channel_id=1, source_target_pairs={{0,24},{8,16},{16,8},{24,0},{1,25},{9,17},{17,9},{25,1},{2,26},{10... | collective-permute-start | bytes 786440 | tf_op jit(solution)/shard_map/ppermute | solution.py:368
  24.2 5.1 %coefficients.1 = (bf16[1024,768]{1,0:T(8,128)(2,1)S(1)}, bf16[1024,768]{1,0:T(8,128)(2,1)S(1)}, bf16[1024,768]{1,0:T(8,128)(2,1)S(1)}) custom-call(s32[18]{0:T(128)S(1)} %concatenate.18.at_ref, f32[8,16,128]{2,1,0:T(8,128)S(1)} %constant_dynamic-update-slice_fusion.info_ref, bf16[2,384,768]{2,1,0:T(8,128)(2,1)S(1)} %copy-done, ...), custom_call_target="tpu_custom_call" | custom-call | flops 38654705664 | bytes 7143496 | tf_op jit(solution)/shard_map/coefficients/pallas_call | solution.py:19
  31.2 6.3 %collective-permute-done.12.refs_8_ = bf16[2,2,128,1024]{3,2,1,0:T(8,128)(2,1)S(1)} collective-permute-done((bf16[2,2,128,1024]{3,2,1,0:T(8,128)(2,1)S(1)}, bf16[2,2,128,1024]{3,2,1,0:T(8,128)(2,1)S(1)}, u32[]{:S(2)}, u32[]{:S(2)}) %collective-permute-start.12) | collective-permute-done | bytes 1048608 | tf_op jit(solution)/shard_map/ppermute | solution.py:365
  41.8 6.3 %hidden_early.2.refs_0_ = f32[768,768]{1,0:T(8,128)S(1)} custom-call(s32[18]{0:T(128)S(1)} %concatenate.18.at_ref, bf16[1,1,128,1024]{3,2,1,0:T(8,128)(2,1)S(1)} %bitcast.53, bf16[1,1,128,1024]{3,2,1,0:T(8,128)(2,1)} %collective-permute-done.refs_1_, bf16[1,1,128,1024]{3,2,1,0:T(8,128)(2,1)S(1)} %copy-done.4, ...), custom_call_target="tpu_custom_call" | custom-call | flops 28991029248 | bytes 25952328 | tf_op jit(solution)/shard_map/hidden_early/pallas_call | solution.py:19
  48.1 5.7 %collective-permute-done.17.refs_2_ = bf16[2,1,128,1024]{3,2,1,0:T(8,128)(2,1)S(1)} collective-permute-done((bf16[2,1,128,1024]{3,2,1,0:T(8,128)(2,1)S(1)}, bf16[2,1,128,1024]{3,2,1,0:T(8,128)(2,1)S(1)}, u32[]{:S(2)}, u32[]{:S(2)}) %collective-permute-start.17) | collective-permute-done | bytes 524320 | tf_op jit(solution)/shard_map/ppermute | solution.py:365
  53.8 1.8 %collective-permute-done.16.refs_3_ = bf16[1,2,128,1024]{3,2,1,0:T(8,128)(2,1)S(1)} collective-permute-done((bf16[1,2,128,1024]{3,2,1,0:T(8,128)(2,1)S(1)}, bf16[1,2,128,1024]{3,2,1,0:T(8,128)(2,1)S(1)}, u32[]{:S(2)}, u32[]{:S(2)}) %collective-permute-start.16) | collective-permute-done | bytes 524320 | tf_op jit(solution)/shard_map/ppermute | solution.py:365
  57.9 2.8 %hidden_early.3.refs_5_ = f32[256,768]{1,0:T(8,128)S(1)} custom-call(s32[18]{0:T(128)S(1)} %concatenate.18.at_ref, bf16[1,1,128,1024]{3,2,1,0:T(8,128)(2,1)S(1)} %collective-permute-done.19.refs_0_, bf16[1,1,128,1024]{3,2,1,0:T(8,128)(2,1)S(1)} %collective-permute-done.20.refs_1_, bf16[768,4096]{1,0:T(8,128)(2,1)S(1)} %bitcast.24, ...), custom_call_target="tpu_custom_call" | custom-call | flops 9663676416 | bytes 21233736 | tf_op jit(solution)/shard_map/hidden_early/pallas_call | solution.py:19
  60.7 1.9 %collective-permute-done.22.refs_6_ = bf16[1,1,128,1024]{3,2,1,0:T(8,128)(2,1)S(1)} collective-permute-done((bf16[1,1,128,1024]{3,2,1,0:T(8,128)(2,1)S(1)}, bf16[1,1,128,1024]{3,2,1,0:T(8,128)(2,1)S(1)}, u32[]{:S(2)}, u32[]{:S(2)}) %collective-permute-start.22) | collective-permute-done | bytes 262176 | tf_op jit(solution)/shard_map/ppermute | solution.py:365
  64.2 5.7 %hidden_late.1 = (bf16[1024,768]{1,0:T(8,128)(2,1)S(1)}, bf16[1024,768]{1,0:T(8,128)(2,1)S(1)}, bf16[8,16,1024]{2,1,0:T(8,128)(2,1)S(1)}) custom-call(s32[18]{0:T(128)S(1)} %concatenate.18.at_ref, f32[768,768]{1,0:T(8,128)S(1)} %hidden_early.2.refs_0_, bf16[2,1,128,1024]{3,2,1,0:T(8,128)(2,1)S(1)} %join.3.refs_1_, ...), custom_call_target="tpu_custom_call" | custom-call | flops 12884901888 | bytes 19660872 | tf_op jit(solution)/shard_map/hidden_late/pallas_call | solution.py:19
  70.0 2.9 %expand.8 = bf16[4,1,144,1024]{3,2,1,0:T(8,128)(2,1)S(1)} custom-call(s32[18]{0:T(128)S(1)} %concatenate.18.at_ref, bf16[1024,768]{1,0:T(8,128)(2,1)S(1)} %get-tuple-element.93.ag_ref, bf16[1024,768]{1,0:T(8,128)(2,1)S(1)} %get-tuple-element.77.au_ref, bf16[768,4096]{1,0:T(8,128)(2,1)S(1)} %bitcast.30, bf16[768,4096]{1,0:T(8,128)(2,1)S(1)} %bitcast.40, ...), custom_call_target="tpu_custom_call" | custom-call | flops 12884901888 | bytes 17170504 | tf_op jit(solution)/shard_map/expand/pallas_call | solution.py:19
  73.0 2.9 %expand.9 = bf16[4,1,128,1024]{3,2,1,0:T(8,128)(2,1)S(1)} custom-call(s32[18]{0:T(128)S(1)} %concatenate.18.at_ref, bf16[1024,768]{1,0:T(8,128)(2,1)S(1)} %get-tuple-element.93.ag_ref, bf16[1024,768]{1,0:T(8,128)(2,1)S(1)} %get-tuple-element.77.au_ref, bf16[768,4096]{1,0:T(8,128)(2,1)S(1)} %bitcast.31, bf16[768,4096]{1,0:T(8,128)(2,1)S(1)} %bitcast.41), custom_call_target="tpu_custom_call" | custom-call | flops 12884901888 | bytes 16777288 | tf_op jit(solution)/shard_map/expand/pallas_call | solution.py:19
  76.4 3.0 %expand.10 = (bf16[1,1,144,1024]{3,2,1,0:T(8,128)(2,1)S(1)}, bf16[2,1,144,1024]{3,2,1,0:T(8,128)(2,1)S(1)}, bf16[1,1,144,1024]{3,2,1,0:T(8,128)(2,1)S(1)}) custom-call(s32[18]{0:T(128)S(1)} %concatenate.18.at_ref, bf16[1024,768]{1,0:T(8,128)(2,1)S(1)} %get-tuple-element.93.ag_ref, bf16[1024,768]{1,0:T(8,128)(2,1)S(1)} %get-tuple-element.77.au_ref, ...), custom_call_target="tpu_custom_call" | custom-call | flops 12884901888 | bytes 18350152 | tf_op jit(solution)/shard_map/expand/pallas_call | solution.py:19
  80.4 3.0 %expand.11 = (bf16[1,1,128,1024]{3,2,1,0:T(8,128)(2,1)S(1)}, bf16[2,1,128,1024]{3,2,1,0:T(8,128)(2,1)S(1)}, bf16[1,1,128,1024]{3,2,1,0:T(8,128)(2,1)S(1)}) custom-call(s32[18]{0:T(128)S(1)} %concatenate.18.at_ref, bf16[1024,768]{1,0:T(8,128)(2,1)S(1)} %get-tuple-element.93.ag_ref, bf16[1024,768]{1,0:T(8,128)(2,1)S(1)} %get-tuple-element.77.au_ref, ...), custom_call_target="tpu_custom_call" | custom-call | flops 12884901888 | bytes 17825864 | tf_op jit(solution)/shard_map/expand/pallas_call | solution.py:19
  87.7 2.9 %expand.12 = bf16[4,1,128,1024]{3,2,1,0:T(8,128)(2,1)S(1)} custom-call(s32[18]{0:T(128)S(1)} %concatenate.18.at_ref, bf16[1024,768]{1,0:T(8,128)(2,1)S(1)} %get-tuple-element.93.ag_ref, bf16[1024,768]{1,0:T(8,128)(2,1)S(1)} %get-tuple-element.77.au_ref, bf16[768,4096]{1,0:T(8,128)(2,1)S(1)} %bitcast.34, bf16[768,4096]{1,0:T(8,128)(2,1)S(1)} %bitcast.44), custom_call_target="tpu_custom_call" | custom-call | flops 12884901888 | bytes 16777288 | tf_op jit(solution)/shard_map/expand/pallas_call | solution.py:19
  90.7 2.9 %expand.13 = bf16[4,1,128,1024]{3,2,1,0:T(8,128)(2,1)S(1)} custom-call(s32[18]{0:T(128)S(1)} %concatenate.18.at_ref, bf16[1024,768]{1,0:T(8,128)(2,1)S(1)} %get-tuple-element.93.ag_ref, bf16[1024,768]{1,0:T(8,128)(2,1)S(1)} %get-tuple-element.77.au_ref, bf16[768,4096]{1,0:T(8,128)(2,1)S(1)} %bitcast.35, bf16[768,4096]{1,0:T(8,128)(2,1)S(1)} %bitcast.45), custom_call_target="tpu_custom_call" | custom-call | flops 12884901888 | bytes 16777288 | tf_op jit(solution)/shard_map/expand/pallas_call | solution.py:19
  96.4 3.2 %expand.14 = (bf16[1,1,128,1024]{3,2,1,0:T(8,128)(2,1)S(1)}, bf16[2,1,128,1024]{3,2,1,0:T(8,128)(2,1)S(1)}, bf16[1,1,128,1024]{3,2,1,0:T(8,128)(2,1)S(1)}) custom-call(s32[18]{0:T(128)S(1)} %concatenate.18.at_ref, bf16[1024,768]{1,0:T(8,128)(2,1)S(1)} %get-tuple-element.93.ag_ref, bf16[1024,768]{1,0:T(8,128)(2,1)S(1)} %get-tuple-element.77.au_ref, ...), custom_call_target="tpu_custom_call" | custom-call | flops 12884901888 | bytes 17825864 | tf_op jit(solution)/shard_map/expand/pallas_call | solution.py:19
  100.6 3.0 %expand.15 = (bf16[1,1,128,1024]{3,2,1,0:T(8,128)(2,1)S(1)}, bf16[2,1,128,1024]{3,2,1,0:T(8,128)(2,1)S(1)}, bf16[1,1,128,1024]{3,2,1,0:T(8,128)(2,1)S(1)}) custom-call(s32[18]{0:T(128)S(1)} %concatenate.18.at_ref, bf16[1024,768]{1,0:T(8,128)(2,1)S(1)} %get-tuple-element.93.ag_ref, bf16[1024,768]{1,0:T(8,128)(2,1)S(1)} %get-tuple-element.77.au_ref, ...), custom_call_target="tpu_custom_call" | custom-call | flops 12884901888 | bytes 17825864 | tf_op jit(solution)/shard_map/expand/pallas_call | solution.py:19
  107.8 3.3 %collective-permute-done.30.one_ref = bf16[1,1,128,1024]{3,2,1,0:T(8,128)(2,1)S(1)} collective-permute-done((bf16[1,1,128,1024]{3,2,1,0:T(8,128)(2,1)S(1)}, bf16[1,1,128,1024]{3,2,1,0:T(8,128)(2,1)S(1)}, u32[]{:S(2)}, u32[]{:S(2)}) %collective-permute-start.30) | collective-permute-done | bytes 262176 | tf_op jit(solution)/shard_map/ppermute | solution.py:365
  111.2 1.9 %collective-permute-start.41 = (bf16[2,1,128,1024]{3,2,1,0:T(8,128)(2,1)S(1)}, bf16[2,1,128,1024]{3,2,1,0:T(8,128)(2,1)S(1)}, u32[]{:S(2)}, u32[]{:S(2)}) collective-permute-start(bf16[2,1,128,1024]{3,2,1,0:T(8,128)(2,1)S(1)} %pass_on.7), channel_id=1, source_target_pairs={{0,2},{1,5},{2,0},{3,7},{4,6},{5,1},{6,4},{7,3},{8,10},{9,13},{10,... | collective-permute-start | bytes 1572872 | tf_op jit(solution)/shard_map/ppermute | solution.py:365
  113.1 2.9 %collective-permute-done.36.refs_0_ = bf16[144,1024]{1,0:T(8,128)(2,1)S(1)} collective-permute-done((bf16[144,1024]{1,0:T(8,128)(2,1)S(1)}, bf16[144,1024]{1,0:T(8,128)(2,1)S(1)}, u32[]{:S(2)}, u32[]{:S(2)}) %collective-permute-start.36) | collective-permute-done | bytes 294944 | tf_op jit(solution)/shard_map/ppermute | solution.py:368
  118.3 14.4 %collective-permute-done.37 = bf16[144,1024]{1,0:T(8,128)(2,1)S(1)} collective-permute-done((bf16[144,1024]{1,0:T(8,128)(2,1)S(1)}, bf16[144,1024]{1,0:T(8,128)(2,1)S(1)}, u32[]{:S(2)}, u32[]{:S(2)}) %collective-permute-start.37) | collective-permute-done | bytes 294944 | tf_op jit(solution)/shard_map/ppermute | solution.py:368
  (135 shorter events, 41.1 us)
Async XLA Ops:
  0.6 8.6 %collective-permute-start.1 = (bf16[1,1,128,1024]{3,2,1,0:T(8,128)(2,1)}, bf16[1,1,128,1024]{3,2,1,0:T(8,128)(2,1)S(1)}, u32[]{:S(2)}, u32[]{:S(2)}) collective-permute-start(bf16[1,1,128,1024]{3,2,1,0:T(8,128)(2,1)} %bitcast.48), channel_id=1, source_target_pairs={{0,2},{1,5},{2,0},{3,7},{4,6},{5,1},{6,4},{7,3},{8,10},{9,13},{10,... | collective-permute-start | bytes 786440 | tf_op jit(solution)/shard_map/ppermute | solution.py:365
  3.7 14.6 %collective-permute-start.6 = (bf16[1,1,128,1024]{3,2,1,0:T(8,128)(2,1)}, bf16[1,1,128,1024]{3,2,1,0:T(8,128)(2,1)S(1)}, u32[]{:S(2)}, u32[]{:S(2)}) collective-permute-start(bf16[1,1,128,1024]{3,2,1,0:T(8,128)(2,1)} %bitcast.49), channel_id=1, source_target_pairs={{0,16},{8,24},{16,0},{24,8},{1,17},{9,25},{17,1},{25,9},{2,18},{10... | collective-permute-start | bytes 786440 | tf_op jit(solution)/shard_map/ppermute | solution.py:368
  6.2 12.2 %collective-permute-start.2 = (bf16[1,1,128,1024]{3,2,1,0:T(8,128)(2,1)}, bf16[1,1,128,1024]{3,2,1,0:T(8,128)(2,1)S(1)}, u32[]{:S(2)}, u32[]{:S(2)}) collective-permute-start(bf16[1,1,128,1024]{3,2,1,0:T(8,128)(2,1)} %bitcast.50), channel_id=1, source_target_pairs={{0,8},{8,0},{16,24},{24,16},{1,9},{9,1},{17,25},{25,17},{2,10},{10... | collective-permute-start | bytes 786440 | tf_op jit(solution)/shard_map/ppermute | solution.py:368
  10.2 12.2 %collective-permute-start.7 = (bf16[1,1,128,1024]{3,2,1,0:T(8,128)(2,1)}, bf16[1,1,128,1024]{3,2,1,0:T(8,128)(2,1)}, u32[]{:S(2)}, u32[]{:S(2)}) collective-permute-start(bf16[1,1,128,1024]{3,2,1,0:T(8,128)(2,1)} %collective-permute-done.refs_1_), channel_id=1, source_target_pairs={{0,2},{1,5},{2,0},{3,7},{4,6},{5,1},{6,4},{7,3},{8,10},{9,13},{10,... | collective-permute-start | bytes 786440 | tf_op jit(solution)/shard_map/ppermute | solution.py:365
  19.0 10.5 %collective-permute-start.13 = (bf16[1,1,128,1024]{3,2,1,0:T(8,128)(2,1)}, bf16[1,1,128,1024]{3,2,1,0:T(8,128)(2,1)S(1)}, u32[]{:S(2)}, u32[]{:S(2)}) collective-permute-start(bf16[1,1,128,1024]{3,2,1,0:T(8,128)(2,1)} %bitcast.52), channel_id=1, source_target_pairs={{0,24},{8,16},{16,8},{24,0},{1,25},{9,17},{17,9},{25,1},{2,26},{10... | collective-permute-start | bytes 786440 | tf_op jit(solution)/shard_map/ppermute | solution.py:368
  22.6 14.9 %collective-permute-start.12 = (bf16[2,2,128,1024]{3,2,1,0:T(8,128)(2,1)S(1)}, bf16[2,2,128,1024]{3,2,1,0:T(8,128)(2,1)S(1)}, u32[]{:S(2)}, u32[]{:S(2)}) collective-permute-start(bf16[2,2,128,1024]{3,2,1,0:T(8,128)(2,1)S(1)} %join.2.refs_7_), channel_id=1, source_target_pairs={{0,2},{1,5},{2,0},{3,7},{4,6},{5,1},{6,4},{7,3},{8,10},{9,13},{10,... | collective-permute-start | bytes 3145736 | tf_op jit(solution)/shard_map/ppermute | solution.py:365
  38.0 17.6 %collective-permute-start.19 = (bf16[1,1,128,1024]{3,2,1,0:T(8,128)(2,1)S(1)}, bf16[1,1,128,1024]{3,2,1,0:T(8,128)(2,1)S(1)}, u32[]{:S(2)}, u32[]{:S(2)}) collective-permute-start(bf16[1,1,128,1024]{3,2,1,0:T(8,128)(2,1)S(1)} %copy-done.4), channel_id=1, source_target_pairs={{0,4},{1,3},{2,6},{3,1},{4,0},{5,7},{6,2},{7,5},{8,12},{9,11},{10,... | collective-permute-start | bytes 786440 | tf_op jit(solution)/shard_map/ppermute | solution.py:365
  38.9 14.9 %collective-permute-start.17 = (bf16[2,1,128,1024]{3,2,1,0:T(8,128)(2,1)S(1)}, bf16[2,1,128,1024]{3,2,1,0:T(8,128)(2,1)S(1)}, u32[]{:S(2)}, u32[]{:S(2)}) collective-permute-start(bf16[2,1,128,1024]{3,2,1,0:T(8,128)(2,1)S(1)} %join.3.refs_1_), channel_id=1, source_target_pairs={{0,2},{1,5},{2,0},{3,7},{4,6},{5,1},{6,4},{7,3},{8,10},{9,13},{10,... | collective-permute-start | bytes 1572872 | tf_op jit(solution)/shard_map/ppermute | solution.py:365
  40.9 14.7 %collective-permute-start.16 = (bf16[1,2,128,1024]{3,2,1,0:T(8,128)(2,1)S(1)}, bf16[1,2,128,1024]{3,2,1,0:T(8,128)(2,1)S(1)}, u32[]{:S(2)}, u32[]{:S(2)}) collective-permute-start(bf16[1,2,128,1024]{3,2,1,0:T(8,128)(2,1)S(1)} %slice.43), channel_id=1, source_target_pairs={{0,4},{1,3},{2,6},{3,1},{4,0},{5,7},{6,2},{7,5},{8,12},{9,11},{10,... | collective-permute-start | bytes 1572872 | tf_op jit(solution)/shard_map/ppermute | solution.py:365
  56.1 6.5 %collective-permute-start.18 = (bf16[2,1,128,1024]{3,2,1,0:T(8,128)(2,1)S(1)}, bf16[2,1,128,1024]{3,2,1,0:T(8,128)(2,1)S(1)}, u32[]{:S(2)}, u32[]{:S(2)}) collective-permute-start(bf16[2,1,128,1024]{3,2,1,0:T(8,128)(2,1)S(1)} %collective-permute-done.17.refs_2_), channel_id=1, source_target_pairs={{0,1},{1,0},{2,3},{3,2},{4,5},{5,4},{6,7},{7,6},{8,9},{9,8},{10,11... | collective-permute-start | bytes 1572872 | tf_op jit(solution)/shard_map/ppermute | solution.py:365
  56.2 6.4 %collective-permute-start.22 = (bf16[1,1,128,1024]{3,2,1,0:T(8,128)(2,1)S(1)}, bf16[1,1,128,1024]{3,2,1,0:T(8,128)(2,1)S(1)}, u32[]{:S(2)}, u32[]{:S(2)}) collective-permute-start(bf16[1,1,128,1024]{3,2,1,0:T(8,128)(2,1)S(1)} %slice.44), channel_id=1, source_target_pairs={{0,4},{1,3},{2,6},{3,1},{4,0},{5,7},{6,2},{7,5},{8,12},{9,11},{10,... | collective-permute-start | bytes 786440 | tf_op jit(solution)/shard_map/ppermute | solution.py:365
  79.4 6.8 %collective-permute-start.27 = (bf16[1,1,144,1024]{3,2,1,0:T(8,128)(2,1)S(1)}, bf16[1,1,144,1024]{3,2,1,0:T(8,128)(2,1)S(1)}, u32[]{:S(2)}, u32[]{:S(2)}) collective-permute-start(bf16[1,1,144,1024]{3,2,1,0:T(8,128)(2,1)S(1)} %get-tuple-element.86), channel_id=1, source_target_pairs={{0,4},{1,3},{2,6},{3,1},{4,0},{5,7},{6,2},{7,5},{8,12},{9,11},{10,... | collective-permute-start | bytes 884744 | tf_op jit(solution)/shard_map/ppermute | solution.py:365
  83.3 10.8 %collective-permute-start.26 = (bf16[1,1,128,1024]{3,2,1,0:T(8,128)(2,1)S(1)}, bf16[1,1,128,1024]{3,2,1,0:T(8,128)(2,1)S(1)}, u32[]{:S(2)}, u32[]{:S(2)}) collective-permute-start(bf16[1,1,128,1024]{3,2,1,0:T(8,128)(2,1)S(1)} %get-tuple-element.84), channel_id=1, source_target_pairs={{0,4},{1,3},{2,6},{3,1},{4,0},{5,7},{6,2},{7,5},{8,12},{9,11},{10,... | collective-permute-start | bytes 786440 | tf_op jit(solution)/shard_map/ppermute | solution.py:365
  86.3 9.9 %collective-permute-start.32 = (bf16[2,1,144,1024]{3,2,1,0:T(8,128)(2,1)S(1)}, bf16[2,1,144,1024]{3,2,1,0:T(8,128)(2,1)S(1)}, u32[]{:S(2)}, u32[]{:S(2)}) collective-permute-start(bf16[2,1,144,1024]{3,2,1,0:T(8,128)(2,1)S(1)} %pass_on.4), channel_id=1, source_target_pairs={{0,2},{1,5},{2,0},{3,7},{4,6},{5,1},{6,4},{7,3},{8,10},{9,13},{10,... | collective-permute-start | bytes 1769480 | tf_op jit(solution)/shard_map/ppermute | solution.py:365
  93.5 7.0 %collective-permute-start.29 = (bf16[4,1,128,1024]{3,2,1,0:T(8,128)(2,1)S(1)}, bf16[4,1,128,1024]{3,2,1,0:T(8,128)(2,1)S(1)}, u32[]{:S(2)}, u32[]{:S(2)}) collective-permute-start(bf16[4,1,128,1024]{3,2,1,0:T(8,128)(2,1)S(1)} %expand.13), channel_id=1, source_target_pairs={{0,1},{1,0},{2,3},{3,2},{4,5},{5,4},{6,7},{7,6},{8,9},{9,8},{10,11... | collective-permute-start | bytes 3145736 | tf_op jit(solution)/shard_map/ppermute | solution.py:365
  94.2 13.5 %collective-permute-start.34 = (bf16[2,1,128,1024]{3,2,1,0:T(8,128)(2,1)S(1)}, bf16[2,1,128,1024]{3,2,1,0:T(8,128)(2,1)S(1)}, u32[]{:S(2)}, u32[]{:S(2)}) collective-permute-start(bf16[2,1,128,1024]{3,2,1,0:T(8,128)(2,1)S(1)} %pass_on.5), channel_id=1, source_target_pairs={{0,2},{1,5},{2,0},{3,7},{4,6},{5,1},{6,4},{7,3},{8,10},{9,13},{10,... | collective-permute-start | bytes 1572872 | tf_op jit(solution)/shard_map/ppermute | solution.py:365
  96.3 11.2 %collective-permute-start.33 = (bf16[1,1,144,1024]{3,2,1,0:T(8,128)(2,1)S(1)}, bf16[1,1,144,1024]{3,2,1,0:T(8,128)(2,1)S(1)}, u32[]{:S(2)}, u32[]{:S(2)}) collective-permute-start(bf16[1,1,144,1024]{3,2,1,0:T(8,128)(2,1)S(1)} %get-tuple-element.110), channel_id=1, source_target_pairs={{0,1},{1,0},{2,3},{3,2},{4,5},{5,4},{6,7},{7,6},{8,9},{9,8},{10,11... | collective-permute-start | bytes 884744 | tf_op jit(solution)/shard_map/ppermute | solution.py:365
  99.5 6.4 %collective-permute-start.31 = (bf16[1,1,128,1024]{3,2,1,0:T(8,128)(2,1)S(1)}, bf16[1,1,128,1024]{3,2,1,0:T(8,128)(2,1)S(1)}, u32[]{:S(2)}, u32[]{:S(2)}) collective-permute-start(bf16[1,1,128,1024]{3,2,1,0:T(8,128)(2,1)S(1)} %get-tuple-element.97), channel_id=1, source_target_pairs={{0,4},{1,3},{2,6},{3,1},{4,0},{5,7},{6,2},{7,5},{8,12},{9,11},{10,... | collective-permute-start | bytes 786440 | tf_op jit(solution)/shard_map/ppermute | solution.py:365
  103.5 7.5 %collective-permute-start.30 = (bf16[1,1,128,1024]{3,2,1,0:T(8,128)(2,1)S(1)}, bf16[1,1,128,1024]{3,2,1,0:T(8,128)(2,1)S(1)}, u32[]{:S(2)}, u32[]{:S(2)}) collective-permute-start(bf16[1,1,128,1024]{3,2,1,0:T(8,128)(2,1)S(1)} %get-tuple-element.95), channel_id=1, source_target_pairs={{0,4},{1,3},{2,6},{3,1},{4,0},{5,7},{6,2},{7,5},{8,12},{9,11},{10,... | collective-permute-start | bytes 786440 | tf_op jit(solution)/shard_map/ppermute | solution.py:365
  106.0 10.1 %collective-permute-start.38 = (bf16[2,1,128,1024]{3,2,1,0:T(8,128)(2,1)S(1)}, bf16[2,1,128,1024]{3,2,1,0:T(8,128)(2,1)S(1)}, u32[]{:S(2)}, u32[]{:S(2)}) collective-permute-start(bf16[2,1,128,1024]{3,2,1,0:T(8,128)(2,1)S(1)} %pass_on.6), channel_id=1, source_target_pairs={{0,2},{1,5},{2,0},{3,7},{4,6},{5,1},{6,4},{7,3},{8,10},{9,13},{10,... | collective-permute-start | bytes 1572872 | tf_op jit(solution)/shard_map/ppermute | solution.py:365
  107.6 8.4 %collective-permute-start.36 = (bf16[144,1024]{1,0:T(8,128)(2,1)S(1)}, bf16[144,1024]{1,0:T(8,128)(2,1)S(1)}, u32[]{:S(2)}, u32[]{:S(2)}) collective-permute-start(bf16[144,1024]{1,0:T(8,128)(2,1)S(1)} %finish.4.refs_1_), channel_id=1, source_target_pairs={{0,8},{8,0},{16,24},{24,16},{1,9},{9,1},{17,25},{25,17},{2,10},{10... | collective-permute-start | bytes 884744 | tf_op jit(solution)/shard_map/ppermute | solution.py:368
  111.2 21.5 %collective-permute-start.41 = (bf16[2,1,128,1024]{3,2,1,0:T(8,128)(2,1)S(1)}, bf16[2,1,128,1024]{3,2,1,0:T(8,128)(2,1)S(1)}, u32[]{:S(2)}, u32[]{:S(2)}) collective-permute-start(bf16[2,1,128,1024]{3,2,1,0:T(8,128)(2,1)S(1)} %pass_on.7), channel_id=1, source_target_pairs={{0,2},{1,5},{2,0},{3,7},{4,6},{5,1},{6,4},{7,3},{8,10},{9,13},{10,... | collective-permute-start | bytes 1572872 | tf_op jit(solution)/shard_map/ppermute | solution.py:365
  116.3 16.4 %collective-permute-start.37 = (bf16[144,1024]{1,0:T(8,128)(2,1)S(1)}, bf16[144,1024]{1,0:T(8,128)(2,1)S(1)}, u32[]{:S(2)}, u32[]{:S(2)}) collective-permute-start(bf16[144,1024]{1,0:T(8,128)(2,1)S(1)} %finish.5), channel_id=1, source_target_pairs={{0,16},{8,24},{16,0},{24,8},{1,17},{9,25},{17,1},{25,9},{2,18},{10... | collective-permute-start | bytes 884744 | tf_op jit(solution)/shard_map/ppermute | solution.py:368
  117.9 16.5 %collective-permute-start.40 = (bf16[128,1024]{1,0:T(8,128)(2,1)S(1)}, bf16[128,1024]{1,0:T(8,128)(2,1)S(1)}, u32[]{:S(2)}, u32[]{:S(2)}) collective-permute-start(bf16[128,1024]{1,0:T(8,128)(2,1)S(1)} %finish.6), channel_id=1, source_target_pairs={{0,8},{8,0},{16,24},{24,16},{1,9},{9,1},{17,25},{25,17},{2,10},{10... | collective-permute-start | bytes 786440 | tf_op jit(solution)/shard_map/ppermute | solution.py:368
  (31 other events, 233.4 us)

commit v8 on v7

--- a/solution.py
+++ b/solution.py
@@ -375,8 +375,6 @@
 
     piece = grad_out[None, None]
     received = [piece] + [across(piece, i) for i in (1, 2) if i < sections]
-    for i in range(3, sections):
-        received.append(across(after(piece, *received[1:3]), i))
     info = jnp.concatenate([expert_ids.T.astype(F32), probs.T], axis=0)[None]
     if square:
         sib0 = swap(piece, 1, 1)
@@ -397,6 +395,7 @@
         pair1 = join(got, [swap(x, 1, 1) for x in got])
         first1 = swap(pair1, 2, 4)
         second0 = swap(near0[0], 4, 2)
+        received.append(across(after(piece, pair1), 3))
         coefs = gated(after(at, pair1, *near0))
         got = [after(x, coefs[0]) for x in received[3:]]
         pair2 = join(got, [swap(x, 1, 1) for x in got])
@@ -414,6 +413,7 @@
         lot2 = [pair2, first2, swap(first2, 1, 1)], [second2, swap(second2, 1, 1)]
         parts = [(most, [(3, lot2[0])]), (few, [(3, lot2[1])])]
     else:
+        received += [across(piece, i) for i in range(3, sections)]
         coefs = gated(at)
         gather = lambda xs: [lax.all_gather(jnp.concatenate(xs, axis=1), "expert", axis=0, tiled=True)]
         (h,) = hidden(at, [(None, [(0, gather(received[:3]))])], tokens, w_down)
@@ -481,7 +481,7 @@
             (final_step, 3),
         ):
             step(n)
-        parts[1] = after(parts[1], firsts[2])
+        parts[1] = after(parts[1], firsts[2], sent[3][1])
         grad_in = add(parts[1][:tokens], parts[2], parts[3])
         router = firsts[1][tokens:].astype(F32) + parts[1][tokens:].astype(F32)
     else:

time: 135 us -> 135 us (level)
  waiting for transfers between devices: 53.1 us -> 43.8 us
  starting transfers between devices: 33.3 us -> 41.7 us
    ppermute x6, starting transfers between devices: 8.07 us -> 16.5 us  [across(): return lax.ppermute(x, 'section', [(i, i ^ by) for i in range(sections)])]
    ppermute x37, waiting for transfers between devices: 34.8 us -> 26.9 us  [swap(): lax.ppermute(x, 'expert', [(i, i ^ (even, odd)[i % 2]) for i in range(gro...]
  transfers between devices with their start and end apart: 43 -> 43, of which waited for: 22 -> 24; matrix products, arithmetic and copies ran while one was open for 2% -> 2% of each run, Pallas kernels for 27% -> 26%
where the time goes in v8:
time: 135 us
  Pallas kernels  44.5 us (33%)
  waiting for transfers between devices  43.8 us (32%)
  starting transfers between devices  41.7 us (31%)
  other arithmetic  2.84 us (2%)
    pallas_call x12, Pallas kernels, call(): pl.pallas_call(kernel, grid_spec=pltpu.PrefetchScalarGridSpec(num_scalar_...  43.6 us
    ppermute x37, waiting for transfers between devices, swap(): lax.ppermute(x, 'expert', [(i, i ^ (even, odd)[i % 2]) for i in range(gro...  26.9 us
    ppermute x37, starting transfers between devices, swap(): lax.ppermute(x, 'expert', [(i, i ^ (even, odd)[i % 2]) for i in range(gro...  25.2 us
    ppermute x6, waiting for transfers between devices, across(): return lax.ppermute(x, 'section', [(i, i ^ by) for i in range(sections)])  16.9 us
    ppermute x6, starting transfers between devices, across(): return lax.ppermute(x, 'section', [(i, i ^ by) for i in range(sections)])  16.5 us
  transfers between devices with their start and end apart: 43, of which 24 were waited for; matrix products, arithmetic and copies ran while one was open for 2% of the time, Pallas kernels for 26%

profile of v8, /device:TPU:0, one launch (start us, length us, event | category | flops | bytes accessed | tf_op | source)
XLA Modules:
  0.0 134.9 jit_solution(5502063730301206801)
XLA Ops:
  0.6 3.0 %collective-permute-start.1 = (bf16[1,1,128,1024]{3,2,1,0:T(8,128)(2,1)}, bf16[1,1,128,1024]{3,2,1,0:T(8,128)(2,1)S(1)}, u32[]{:S(2)}, u32[]{:S(2)}) collective-permute-start(bf16[1,1,128,1024]{3,2,1,0:T(8,128)(2,1)} %bitcast.48), channel_id=1, source_target_pairs={{0,2},{1,5},{2,0},{3,7},{4,6},{5,1},{6,4},{7,3},{8,10},{9,13},{10,... | collective-permute-start | bytes 786440 | tf_op jit(solution)/shard_map/ppermute | solution.py:365
  3.7 2.6 %collective-permute-start.6 = (bf16[1,1,128,1024]{3,2,1,0:T(8,128)(2,1)}, bf16[1,1,128,1024]{3,2,1,0:T(8,128)(2,1)S(1)}, u32[]{:S(2)}, u32[]{:S(2)}) collective-permute-start(bf16[1,1,128,1024]{3,2,1,0:T(8,128)(2,1)} %bitcast.49), channel_id=1, source_target_pairs={{0,16},{8,24},{16,0},{24,8},{1,17},{9,25},{17,1},{25,9},{2,18},{10... | collective-permute-start | bytes 786440 | tf_op jit(solution)/shard_map/ppermute | solution.py:368
  14.4 2.2 %collective-permute-done.4 = f32[2,16,128]{2,1,0:T(8,128)S(1)} collective-permute-done((f32[2,16,128]{2,1,0:T(8,128)S(1)}, f32[2,16,128]{2,1,0:T(8,128)S(1)}, u32[]{:S(2)}, u32[]{:S(2)}) %collective-permute-start.4) | collective-permute-done | bytes 16416 | tf_op jit(solution)/shard_map/ppermute | solution.py:365
  21.9 3.4 %collective-permute-start.13 = (bf16[1,1,128,1024]{3,2,1,0:T(8,128)(2,1)}, bf16[1,1,128,1024]{3,2,1,0:T(8,128)(2,1)S(1)}, u32[]{:S(2)}, u32[]{:S(2)}) collective-permute-start(bf16[1,1,128,1024]{3,2,1,0:T(8,128)(2,1)} %bitcast.52), channel_id=1, source_target_pairs={{0,24},{8,16},{16,8},{24,0},{1,25},{9,17},{17,9},{25,1},{2,26},{10... | collective-permute-start | bytes 786440 | tf_op jit(solution)/shard_map/ppermute | solution.py:368
  25.3 5.1 %coefficients.1 = (bf16[1024,768]{1,0:T(8,128)(2,1)S(1)}, bf16[1024,768]{1,0:T(8,128)(2,1)S(1)}, bf16[1024,768]{1,0:T(8,128)(2,1)S(1)}) custom-call(s32[18]{0:T(128)S(1)} %concatenate.18.at_ref, f32[8,16,128]{2,1,0:T(8,128)S(1)} %constant_dynamic-update-slice_fusion.info_ref, bf16[2,384,768]{2,1,0:T(8,128)(2,1)S(1)} %copy-done, ...), custom_call_target="tpu_custom_call" | custom-call | flops 38654705664 | bytes 7143496 | tf_op jit(solution)/shard_map/coefficients/pallas_call | solution.py:19
  33.3 1.9 %collective-permute-done.12.refs_8_ = bf16[2,2,128,1024]{3,2,1,0:T(8,128)(2,1)S(1)} collective-permute-done((bf16[2,2,128,1024]{3,2,1,0:T(8,128)(2,1)S(1)}, bf16[2,2,128,1024]{3,2,1,0:T(8,128)(2,1)S(1)}, u32[]{:S(2)}, u32[]{:S(2)}) %collective-permute-start.12) | collective-permute-done | bytes 1048608 | tf_op jit(solution)/shard_map/ppermute | solution.py:365
  39.8 6.3 %hidden_early.2.refs_0_ = f32[768,768]{1,0:T(8,128)S(1)} custom-call(s32[18]{0:T(128)S(1)} %concatenate.18.at_ref, bf16[1,1,128,1024]{3,2,1,0:T(8,128)(2,1)S(1)} %bitcast.53, bf16[1,1,128,1024]{3,2,1,0:T(8,128)(2,1)} %collective-permute-done.refs_1_, bf16[1,1,128,1024]{3,2,1,0:T(8,128)(2,1)S(1)} %copy-done.4, ...), custom_call_target="tpu_custom_call" | custom-call | flops 28991029248 | bytes 25952328 | tf_op jit(solution)/shard_map/hidden_early/pallas_call | solution.py:19
  46.1 5.8 %collective-permute-done.17.refs_2_ = bf16[2,1,128,1024]{3,2,1,0:T(8,128)(2,1)S(1)} collective-permute-done((bf16[2,1,128,1024]{3,2,1,0:T(8,128)(2,1)S(1)}, bf16[2,1,128,1024]{3,2,1,0:T(8,128)(2,1)S(1)}, u32[]{:S(2)}, u32[]{:S(2)}) %collective-permute-start.17) | collective-permute-done | bytes 524320 | tf_op jit(solution)/shard_map/ppermute | solution.py:365
  55.6 2.9 %hidden_early.3.refs_5_ = f32[256,768]{1,0:T(8,128)S(1)} custom-call(s32[18]{0:T(128)S(1)} %concatenate.18.at_ref, bf16[1,1,128,1024]{3,2,1,0:T(8,128)(2,1)S(1)} %collective-permute-done.19.refs_0_, bf16[1,1,128,1024]{3,2,1,0:T(8,128)(2,1)S(1)} %collective-permute-done.20.refs_1_, bf16[768,4096]{1,0:T(8,128)(2,1)S(1)} %bitcast.24, ...), custom_call_target="tpu_custom_call" | custom-call | flops 9663676416 | bytes 21233736 | tf_op jit(solution)/shard_map/hidden_early/pallas_call | solution.py:19
  58.5 1.9 %collective-permute-done.22.refs_6_ = bf16[1,1,128,1024]{3,2,1,0:T(8,128)(2,1)S(1)} collective-permute-done((bf16[1,1,128,1024]{3,2,1,0:T(8,128)(2,1)S(1)}, bf16[1,1,128,1024]{3,2,1,0:T(8,128)(2,1)S(1)}, u32[]{:S(2)}, u32[]{:S(2)}) %collective-permute-start.22) | collective-permute-done | bytes 262176 | tf_op jit(solution)/shard_map/ppermute | solution.py:365
  61.9 5.7 %hidden_late.1 = (bf16[1024,768]{1,0:T(8,128)(2,1)S(1)}, bf16[1024,768]{1,0:T(8,128)(2,1)S(1)}, bf16[8,16,1024]{2,1,0:T(8,128)(2,1)S(1)}) custom-call(s32[18]{0:T(128)S(1)} %concatenate.18.at_ref, f32[768,768]{1,0:T(8,128)S(1)} %hidden_early.2.refs_0_, bf16[2,1,128,1024]{3,2,1,0:T(8,128)(2,1)S(1)} %join.3.refs_1_, ...), custom_call_target="tpu_custom_call" | custom-call | flops 12884901888 | bytes 19660872 | tf_op jit(solution)/shard_map/hidden_late/pallas_call | solution.py:19
  67.7 2.9 %expand.8 = bf16[4,1,144,1024]{3,2,1,0:T(8,128)(2,1)S(1)} custom-call(s32[18]{0:T(128)S(1)} %concatenate.18.at_ref, bf16[1024,768]{1,0:T(8,128)(2,1)S(1)} %get-tuple-element.93.ag_ref, bf16[1024,768]{1,0:T(8,128)(2,1)S(1)} %get-tuple-element.77.au_ref, bf16[768,4096]{1,0:T(8,128)(2,1)S(1)} %bitcast.30, bf16[768,4096]{1,0:T(8,128)(2,1)S(1)} %bitcast.40, ...), custom_call_target="tpu_custom_call" | custom-call | flops 12884901888 | bytes 17170504 | tf_op jit(solution)/shard_map/expand/pallas_call | solution.py:19
  70.8 2.9 %expand.9 = bf16[4,1,128,1024]{3,2,1,0:T(8,128)(2,1)S(1)} custom-call(s32[18]{0:T(128)S(1)} %concatenate.18.at_ref, bf16[1024,768]{1,0:T(8,128)(2,1)S(1)} %get-tuple-element.93.ag_ref, bf16[1024,768]{1,0:T(8,128)(2,1)S(1)} %get-tuple-element.77.au_ref, bf16[768,4096]{1,0:T(8,128)(2,1)S(1)} %bitcast.31, bf16[768,4096]{1,0:T(8,128)(2,1)S(1)} %bitcast.41), custom_call_target="tpu_custom_call" | custom-call | flops 12884901888 | bytes 16777288 | tf_op jit(solution)/shard_map/expand/pallas_call | solution.py:19
  74.2 3.0 %expand.10 = (bf16[1,1,144,1024]{3,2,1,0:T(8,128)(2,1)S(1)}, bf16[2,1,144,1024]{3,2,1,0:T(8,128)(2,1)S(1)}, bf16[1,1,144,1024]{3,2,1,0:T(8,128)(2,1)S(1)}) custom-call(s32[18]{0:T(128)S(1)} %concatenate.18.at_ref, bf16[1024,768]{1,0:T(8,128)(2,1)S(1)} %get-tuple-element.93.ag_ref, bf16[1024,768]{1,0:T(8,128)(2,1)S(1)} %get-tuple-element.77.au_ref, ...), custom_call_target="tpu_custom_call" | custom-call | flops 12884901888 | bytes 18350152 | tf_op jit(solution)/shard_map/expand/pallas_call | solution.py:19
  78.4 3.0 %expand.11 = (bf16[1,1,128,1024]{3,2,1,0:T(8,128)(2,1)S(1)}, bf16[2,1,128,1024]{3,2,1,0:T(8,128)(2,1)S(1)}, bf16[1,1,128,1024]{3,2,1,0:T(8,128)(2,1)S(1)}) custom-call(s32[18]{0:T(128)S(1)} %concatenate.18.at_ref, bf16[1024,768]{1,0:T(8,128)(2,1)S(1)} %get-tuple-element.93.ag_ref, bf16[1024,768]{1,0:T(8,128)(2,1)S(1)} %get-tuple-element.77.au_ref, ...), custom_call_target="tpu_custom_call" | custom-call | flops 12884901888 | bytes 17825864 | tf_op jit(solution)/shard_map/expand/pallas_call | solution.py:19
  85.5 2.9 %expand.12 = bf16[4,1,128,1024]{3,2,1,0:T(8,128)(2,1)S(1)} custom-call(s32[18]{0:T(128)S(1)} %concatenate.18.at_ref, bf16[1024,768]{1,0:T(8,128)(2,1)S(1)} %get-tuple-element.93.ag_ref, bf16[1024,768]{1,0:T(8,128)(2,1)S(1)} %get-tuple-element.77.au_ref, bf16[768,4096]{1,0:T(8,128)(2,1)S(1)} %bitcast.34, bf16[768,4096]{1,0:T(8,128)(2,1)S(1)} %bitcast.44), custom_call_target="tpu_custom_call" | custom-call | flops 12884901888 | bytes 16777288 | tf_op jit(solution)/shard_map/expand/pallas_call | solution.py:19
  88.5 2.9 %expand.13 = bf16[4,1,128,1024]{3,2,1,0:T(8,128)(2,1)S(1)} custom-call(s32[18]{0:T(128)S(1)} %concatenate.18.at_ref, bf16[1024,768]{1,0:T(8,128)(2,1)S(1)} %get-tuple-element.93.ag_ref, bf16[1024,768]{1,0:T(8,128)(2,1)S(1)} %get-tuple-element.77.au_ref, bf16[768,4096]{1,0:T(8,128)(2,1)S(1)} %bitcast.35, bf16[768,4096]{1,0:T(8,128)(2,1)S(1)} %bitcast.45), custom_call_target="tpu_custom_call" | custom-call | flops 12884901888 | bytes 16777288 | tf_op jit(solution)/shard_map/expand/pallas_call | solution.py:19
  94.2 3.2 %expand.14 = (bf16[1,1,128,1024]{3,2,1,0:T(8,128)(2,1)S(1)}, bf16[2,1,128,1024]{3,2,1,0:T(8,128)(2,1)S(1)}, bf16[1,1,128,1024]{3,2,1,0:T(8,128)(2,1)S(1)}) custom-call(s32[18]{0:T(128)S(1)} %concatenate.18.at_ref, bf16[1024,768]{1,0:T(8,128)(2,1)S(1)} %get-tuple-element.93.ag_ref, bf16[1024,768]{1,0:T(8,128)(2,1)S(1)} %get-tuple-element.77.au_ref, ...), custom_call_target="tpu_custom_call" | custom-call | flops 12884901888 | bytes 17825864 | tf_op jit(solution)/shard_map/expand/pallas_call | solution.py:19
  98.5 3.0 %expand.15 = (bf16[1,1,128,1024]{3,2,1,0:T(8,128)(2,1)S(1)}, bf16[2,1,128,1024]{3,2,1,0:T(8,128)(2,1)S(1)}, bf16[1,1,128,1024]{3,2,1,0:T(8,128)(2,1)S(1)}) custom-call(s32[18]{0:T(128)S(1)} %concatenate.18.at_ref, bf16[1024,768]{1,0:T(8,128)(2,1)S(1)} %get-tuple-element.93.ag_ref, bf16[1024,768]{1,0:T(8,128)(2,1)S(1)} %get-tuple-element.77.au_ref, ...), custom_call_target="tpu_custom_call" | custom-call | flops 12884901888 | bytes 17825864 | tf_op jit(solution)/shard_map/expand/pallas_call | solution.py:19
  105.4 3.2 %collective-permute-start.36 = (bf16[144,1024]{1,0:T(8,128)(2,1)S(1)}, bf16[144,1024]{1,0:T(8,128)(2,1)S(1)}, u32[]{:S(2)}, u32[]{:S(2)}) collective-permute-start(bf16[144,1024]{1,0:T(8,128)(2,1)S(1)} %finish.4.refs_1_), channel_id=1, source_target_pairs={{0,8},{8,0},{16,24},{24,16},{1,9},{9,1},{17,25},{25,17},{2,10},{10... | collective-permute-start | bytes 884744 | tf_op jit(solution)/shard_map/ppermute | solution.py:368
  110.6 4.7 %collective-permute-done.36.refs_0_ = bf16[144,1024]{1,0:T(8,128)(2,1)S(1)} collective-permute-done((bf16[144,1024]{1,0:T(8,128)(2,1)S(1)}, bf16[144,1024]{1,0:T(8,128)(2,1)S(1)}, u32[]{:S(2)}, u32[]{:S(2)}) %collective-permute-start.36) | collective-permute-done | bytes 294944 | tf_op jit(solution)/shard_map/ppermute | solution.py:368
  115.6 2.4 %collective-permute-start.37 = (bf16[144,1024]{1,0:T(8,128)(2,1)S(1)}, bf16[144,1024]{1,0:T(8,128)(2,1)S(1)}, u32[]{:S(2)}, u32[]{:S(2)}) collective-permute-start(bf16[144,1024]{1,0:T(8,128)(2,1)S(1)} %finish.5), channel_id=1, source_target_pairs={{0,16},{8,24},{16,0},{24,8},{1,17},{9,25},{17,1},{25,9},{2,18},{10... | collective-permute-start | bytes 884744 | tf_op jit(solution)/shard_map/ppermute | solution.py:368
  119.1 3.4 %collective-permute-start.42 = (bf16[128,1024]{1,0:T(8,128)(2,1)S(1)}, bf16[128,1024]{1,0:T(8,128)(2,1)S(1)}, u32[]{:S(2)}, u32[]{:S(2)}) collective-permute-start(bf16[128,1024]{1,0:T(8,128)(2,1)S(1)} %finish.6), channel_id=1, source_target_pairs={{0,8},{8,0},{16,24},{24,16},{1,9},{9,1},{17,25},{25,17},{2,10},{10... | collective-permute-start | bytes 786440 | tf_op jit(solution)/shard_map/ppermute | solution.py:368
  122.5 9.8 %collective-permute-done.37 = bf16[144,1024]{1,0:T(8,128)(2,1)S(1)} collective-permute-done((bf16[144,1024]{1,0:T(8,128)(2,1)S(1)}, bf16[144,1024]{1,0:T(8,128)(2,1)S(1)}, u32[]{:S(2)}, u32[]{:S(2)}) %collective-permute-start.37) | collective-permute-done | bytes 294944 | tf_op jit(solution)/shard_map/ppermute | solution.py:368
  (135 shorter events, 46.1 us)
Async XLA Ops:
  0.6 8.6 %collective-permute-start.1 = (bf16[1,1,128,1024]{3,2,1,0:T(8,128)(2,1)}, bf16[1,1,128,1024]{3,2,1,0:T(8,128)(2,1)S(1)}, u32[]{:S(2)}, u32[]{:S(2)}) collective-permute-start(bf16[1,1,128,1024]{3,2,1,0:T(8,128)(2,1)} %bitcast.48), channel_id=1, source_target_pairs={{0,2},{1,5},{2,0},{3,7},{4,6},{5,1},{6,4},{7,3},{8,10},{9,13},{10,... | collective-permute-start | bytes 786440 | tf_op jit(solution)/shard_map/ppermute | solution.py:365
  3.7 14.6 %collective-permute-start.6 = (bf16[1,1,128,1024]{3,2,1,0:T(8,128)(2,1)}, bf16[1,1,128,1024]{3,2,1,0:T(8,128)(2,1)S(1)}, u32[]{:S(2)}, u32[]{:S(2)}) collective-permute-start(bf16[1,1,128,1024]{3,2,1,0:T(8,128)(2,1)} %bitcast.49), channel_id=1, source_target_pairs={{0,16},{8,24},{16,0},{24,8},{1,17},{9,25},{17,1},{25,9},{2,18},{10... | collective-permute-start | bytes 786440 | tf_op jit(solution)/shard_map/ppermute | solution.py:368
  6.2 12.2 %collective-permute-start.2 = (bf16[1,1,128,1024]{3,2,1,0:T(8,128)(2,1)}, bf16[1,1,128,1024]{3,2,1,0:T(8,128)(2,1)S(1)}, u32[]{:S(2)}, u32[]{:S(2)}) collective-permute-start(bf16[1,1,128,1024]{3,2,1,0:T(8,128)(2,1)} %bitcast.50), channel_id=1, source_target_pairs={{0,8},{8,0},{16,24},{24,16},{1,9},{9,1},{17,25},{25,17},{2,10},{10... | collective-permute-start | bytes 786440 | tf_op jit(solution)/shard_map/ppermute | solution.py:368
  10.2 8.8 %collective-permute-start.7 = (bf16[1,1,128,1024]{3,2,1,0:T(8,128)(2,1)}, bf16[1,1,128,1024]{3,2,1,0:T(8,128)(2,1)}, u32[]{:S(2)}, u32[]{:S(2)}) collective-permute-start(bf16[1,1,128,1024]{3,2,1,0:T(8,128)(2,1)} %collective-permute-done.refs_1_), channel_id=1, source_target_pairs={{0,2},{1,5},{2,0},{3,7},{4,6},{5,1},{6,4},{7,3},{8,10},{9,13},{10,... | collective-permute-start | bytes 786440 | tf_op jit(solution)/shard_map/ppermute | solution.py:365
  20.4 14.9 %collective-permute-start.12 = (bf16[2,2,128,1024]{3,2,1,0:T(8,128)(2,1)S(1)}, bf16[2,2,128,1024]{3,2,1,0:T(8,128)(2,1)S(1)}, u32[]{:S(2)}, u32[]{:S(2)}) collective-permute-start(bf16[2,2,128,1024]{3,2,1,0:T(8,128)(2,1)S(1)} %join.2.refs_7_), channel_id=1, source_target_pairs={{0,2},{1,5},{2,0},{3,7},{4,6},{5,1},{6,4},{7,3},{8,10},{9,13},{10,... | collective-permute-start | bytes 3145736 | tf_op jit(solution)/shard_map/ppermute | solution.py:365
  21.9 9.8 %collective-permute-start.13 = (bf16[1,1,128,1024]{3,2,1,0:T(8,128)(2,1)}, bf16[1,1,128,1024]{3,2,1,0:T(8,128)(2,1)S(1)}, u32[]{:S(2)}, u32[]{:S(2)}) collective-permute-start(bf16[1,1,128,1024]{3,2,1,0:T(8,128)(2,1)} %bitcast.52), channel_id=1, source_target_pairs={{0,24},{8,16},{16,8},{24,0},{1,25},{9,17},{17,9},{25,1},{2,26},{10... | collective-permute-start | bytes 786440 | tf_op jit(solution)/shard_map/ppermute | solution.py:368
  35.7 17.6 %collective-permute-start.19 = (bf16[1,1,128,1024]{3,2,1,0:T(8,128)(2,1)S(1)}, bf16[1,1,128,1024]{3,2,1,0:T(8,128)(2,1)S(1)}, u32[]{:S(2)}, u32[]{:S(2)}) collective-permute-start(bf16[1,1,128,1024]{3,2,1,0:T(8,128)(2,1)S(1)} %copy-done.4), channel_id=1, source_target_pairs={{0,4},{1,3},{2,6},{3,1},{4,0},{5,7},{6,2},{7,5},{8,12},{9,11},{10,... | collective-permute-start | bytes 786440 | tf_op jit(solution)/shard_map/ppermute | solution.py:365
  36.9 14.9 %collective-permute-start.17 = (bf16[2,1,128,1024]{3,2,1,0:T(8,128)(2,1)S(1)}, bf16[2,1,128,1024]{3,2,1,0:T(8,128)(2,1)S(1)}, u32[]{:S(2)}, u32[]{:S(2)}) collective-permute-start(bf16[2,1,128,1024]{3,2,1,0:T(8,128)(2,1)S(1)} %join.3.refs_1_), channel_id=1, source_target_pairs={{0,2},{1,5},{2,0},{3,7},{4,6},{5,1},{6,4},{7,3},{8,10},{9,13},{10,... | collective-permute-start | bytes 1572872 | tf_op jit(solution)/shard_map/ppermute | solution.py:365
  38.6 14.7 %collective-permute-start.16 = (bf16[1,2,128,1024]{3,2,1,0:T(8,128)(2,1)S(1)}, bf16[1,2,128,1024]{3,2,1,0:T(8,128)(2,1)S(1)}, u32[]{:S(2)}, u32[]{:S(2)}) collective-permute-start(bf16[1,2,128,1024]{3,2,1,0:T(8,128)(2,1)S(1)} %slice.43), channel_id=1, source_target_pairs={{0,4},{1,3},{2,6},{3,1},{4,0},{5,7},{6,2},{7,5},{8,12},{9,11},{10,... | collective-permute-start | bytes 1572872 | tf_op jit(solution)/shard_map/ppermute | solution.py:365
  53.9 6.5 %collective-permute-start.18 = (bf16[2,1,128,1024]{3,2,1,0:T(8,128)(2,1)S(1)}, bf16[2,1,128,1024]{3,2,1,0:T(8,128)(2,1)S(1)}, u32[]{:S(2)}, u32[]{:S(2)}) collective-permute-start(bf16[2,1,128,1024]{3,2,1,0:T(8,128)(2,1)S(1)} %collective-permute-done.17.refs_2_), channel_id=1, source_target_pairs={{0,1},{1,0},{2,3},{3,2},{4,5},{5,4},{6,7},{7,6},{8,9},{9,8},{10,11... | collective-permute-start | bytes 1572872 | tf_op jit(solution)/shard_map/ppermute | solution.py:365
  54.0 6.4 %collective-permute-start.22 = (bf16[1,1,128,1024]{3,2,1,0:T(8,128)(2,1)S(1)}, bf16[1,1,128,1024]{3,2,1,0:T(8,128)(2,1)S(1)}, u32[]{:S(2)}, u32[]{:S(2)}) collective-permute-start(bf16[1,1,128,1024]{3,2,1,0:T(8,128)(2,1)S(1)} %slice.44), channel_id=1, source_target_pairs={{0,4},{1,3},{2,6},{3,1},{4,0},{5,7},{6,2},{7,5},{8,12},{9,11},{10,... | collective-permute-start | bytes 786440 | tf_op jit(solution)/shard_map/ppermute | solution.py:365
  77.2 6.8 %collective-permute-start.27 = (bf16[1,1,144,1024]{3,2,1,0:T(8,128)(2,1)S(1)}, bf16[1,1,144,1024]{3,2,1,0:T(8,128)(2,1)S(1)}, u32[]{:S(2)}, u32[]{:S(2)}) collective-permute-start(bf16[1,1,144,1024]{3,2,1,0:T(8,128)(2,1)S(1)} %get-tuple-element.86), channel_id=1, source_target_pairs={{0,4},{1,3},{2,6},{3,1},{4,0},{5,7},{6,2},{7,5},{8,12},{9,11},{10,... | collective-permute-start | bytes 884744 | tf_op jit(solution)/shard_map/ppermute | solution.py:365
  81.3 10.6 %collective-permute-start.26 = (bf16[1,1,128,1024]{3,2,1,0:T(8,128)(2,1)S(1)}, bf16[1,1,128,1024]{3,2,1,0:T(8,128)(2,1)S(1)}, u32[]{:S(2)}, u32[]{:S(2)}) collective-permute-start(bf16[1,1,128,1024]{3,2,1,0:T(8,128)(2,1)S(1)} %get-tuple-element.84), channel_id=1, source_target_pairs={{0,4},{1,3},{2,6},{3,1},{4,0},{5,7},{6,2},{7,5},{8,12},{9,11},{10,... | collective-permute-start | bytes 786440 | tf_op jit(solution)/shard_map/ppermute | solution.py:365
  84.0 9.9 %collective-permute-start.32 = (bf16[2,1,144,1024]{3,2,1,0:T(8,128)(2,1)S(1)}, bf16[2,1,144,1024]{3,2,1,0:T(8,128)(2,1)S(1)}, u32[]{:S(2)}, u32[]{:S(2)}) collective-permute-start(bf16[2,1,144,1024]{3,2,1,0:T(8,128)(2,1)S(1)} %pass_on.4), channel_id=1, source_target_pairs={{0,2},{1,5},{2,0},{3,7},{4,6},{5,1},{6,4},{7,3},{8,10},{9,13},{10,... | collective-permute-start | bytes 1769480 | tf_op jit(solution)/shard_map/ppermute | solution.py:365
  91.3 7.1 %collective-permute-start.29 = (bf16[4,1,128,1024]{3,2,1,0:T(8,128)(2,1)S(1)}, bf16[4,1,128,1024]{3,2,1,0:T(8,128)(2,1)S(1)}, u32[]{:S(2)}, u32[]{:S(2)}) collective-permute-start(bf16[4,1,128,1024]{3,2,1,0:T(8,128)(2,1)S(1)} %expand.13), channel_id=1, source_target_pairs={{0,1},{1,0},{2,3},{3,2},{4,5},{5,4},{6,7},{7,6},{8,9},{9,8},{10,11... | collective-permute-start | bytes 3145736 | tf_op jit(solution)/shard_map/ppermute | solution.py:365
  92.0 16.6 %collective-permute-start.34 = (bf16[2,1,128,1024]{3,2,1,0:T(8,128)(2,1)S(1)}, bf16[2,1,128,1024]{3,2,1,0:T(8,128)(2,1)S(1)}, u32[]{:S(2)}, u32[]{:S(2)}) collective-permute-start(bf16[2,1,128,1024]{3,2,1,0:T(8,128)(2,1)S(1)} %pass_on.5), channel_id=1, source_target_pairs={{0,2},{1,5},{2,0},{3,7},{4,6},{5,1},{6,4},{7,3},{8,10},{9,13},{10,... | collective-permute-start | bytes 1572872 | tf_op jit(solution)/shard_map/ppermute | solution.py:365
  94.0 11.2 %collective-permute-start.33 = (bf16[1,1,144,1024]{3,2,1,0:T(8,128)(2,1)S(1)}, bf16[1,1,144,1024]{3,2,1,0:T(8,128)(2,1)S(1)}, u32[]{:S(2)}, u32[]{:S(2)}) collective-permute-start(bf16[1,1,144,1024]{3,2,1,0:T(8,128)(2,1)S(1)} %get-tuple-element.110), channel_id=1, source_target_pairs={{0,1},{1,0},{2,3},{3,2},{4,5},{5,4},{6,7},{7,6},{8,9},{9,8},{10,11... | collective-permute-start | bytes 884744 | tf_op jit(solution)/shard_map/ppermute | solution.py:365
  101.5 7.6 %collective-permute-start.30 = (bf16[1,1,128,1024]{3,2,1,0:T(8,128)(2,1)S(1)}, bf16[1,1,128,1024]{3,2,1,0:T(8,128)(2,1)S(1)}, u32[]{:S(2)}, u32[]{:S(2)}) collective-permute-start(bf16[1,1,128,1024]{3,2,1,0:T(8,128)(2,1)S(1)} %get-tuple-element.95), channel_id=1, source_target_pairs={{0,4},{1,3},{2,6},{3,1},{4,0},{5,7},{6,2},{7,5},{8,12},{9,11},{10,... | collective-permute-start | bytes 786440 | tf_op jit(solution)/shard_map/ppermute | solution.py:365
  103.9 11.6 %collective-permute-start.38 = (bf16[2,1,128,1024]{3,2,1,0:T(8,128)(2,1)S(1)}, bf16[2,1,128,1024]{3,2,1,0:T(8,128)(2,1)S(1)}, u32[]{:S(2)}, u32[]{:S(2)}) collective-permute-start(bf16[2,1,128,1024]{3,2,1,0:T(8,128)(2,1)S(1)} %pass_on.6), channel_id=1, source_target_pairs={{0,2},{1,5},{2,0},{3,7},{4,6},{5,1},{6,4},{7,3},{8,10},{9,13},{10,... | collective-permute-start | bytes 1572872 | tf_op jit(solution)/shard_map/ppermute | solution.py:365
  105.4 9.9 %collective-permute-start.36 = (bf16[144,1024]{1,0:T(8,128)(2,1)S(1)}, bf16[144,1024]{1,0:T(8,128)(2,1)S(1)}, u32[]{:S(2)}, u32[]{:S(2)}) collective-permute-start(bf16[144,1024]{1,0:T(8,128)(2,1)S(1)} %finish.4.refs_1_), channel_id=1, source_target_pairs={{0,8},{8,0},{16,24},{24,16},{1,9},{9,1},{17,25},{25,17},{2,10},{10... | collective-permute-start | bytes 884744 | tf_op jit(solution)/shard_map/ppermute | solution.py:368
  109.1 9.6 %collective-permute-start.40 = (bf16[2,1,128,1024]{3,2,1,0:T(8,128)(2,1)S(1)}, bf16[2,1,128,1024]{3,2,1,0:T(8,128)(2,1)S(1)}, u32[]{:S(2)}, u32[]{:S(2)}) collective-permute-start(bf16[2,1,128,1024]{3,2,1,0:T(8,128)(2,1)S(1)} %pass_on.7), channel_id=1, source_target_pairs={{0,2},{1,5},{2,0},{3,7},{4,6},{5,1},{6,4},{7,3},{8,10},{9,13},{10,... | collective-permute-start | bytes 1572872 | tf_op jit(solution)/shard_map/ppermute | solution.py:365
  115.6 16.8 %collective-permute-start.37 = (bf16[144,1024]{1,0:T(8,128)(2,1)S(1)}, bf16[144,1024]{1,0:T(8,128)(2,1)S(1)}, u32[]{:S(2)}, u32[]{:S(2)}) collective-permute-start(bf16[144,1024]{1,0:T(8,128)(2,1)S(1)} %finish.5), channel_id=1, source_target_pairs={{0,16},{8,24},{16,0},{24,8},{1,17},{9,25},{17,1},{25,9},{2,18},{10... | collective-permute-start | bytes 884744 | tf_op jit(solution)/shard_map/ppermute | solution.py:368
  118.8 13.5 %collective-permute-start.41 = (bf16[1,1,128,1024]{3,2,1,0:T(8,128)(2,1)S(1)}, bf16[1,1,128,1024]{3,2,1,0:T(8,128)(2,1)S(1)}, u32[]{:S(2)}, u32[]{:S(2)}) collective-permute-start(bf16[1,1,128,1024]{3,2,1,0:T(8,128)(2,1)S(1)} %get-tuple-element.112), channel_id=1, source_target_pairs={{0,1},{1,0},{2,3},{3,2},{4,5},{5,4},{6,7},{7,6},{8,9},{9,8},{10,11... | collective-permute-start | bytes 786440 | tf_op jit(solution)/shard_map/ppermute | solution.py:365
  119.1 15.0 %collective-permute-start.42 = (bf16[128,1024]{1,0:T(8,128)(2,1)S(1)}, bf16[128,1024]{1,0:T(8,128)(2,1)S(1)}, u32[]{:S(2)}, u32[]{:S(2)}) collective-permute-start(bf16[128,1024]{1,0:T(8,128)(2,1)S(1)} %finish.6), channel_id=1, source_target_pairs={{0,8},{8,0},{16,24},{24,16},{1,9},{9,1},{17,25},{25,17},{2,10},{10... | collective-permute-start | bytes 786440 | tf_op jit(solution)/shard_map/ppermute | solution.py:368
  (31 other events, 216.3 us)
